TPU v7x, 512 devices: a whole 4x4x16 slice. The times are simulated.
512 devices in a mesh: rep: 4 (over z_hi, core), expert: 128 (over y, z_lo, x).
Axes of the slice: x: 4, y: 4, z: 16 (z_hi: 2, z_lo: 8; z = z_hi * 8 + z_lo), core: 2. Of those that a mesh axis runs over, the one named last changes fastest.
Arguments:
- tokens: bfloat16 [256, 256, 1280], P('expert', 'rep'), may hold values from -128 to 128, as said below
- router: bfloat16 [1280, 64], replicated, may hold values from -1 to 1
- up_proj: bfloat16 [128, 1280, 1280], P('expert', 'rep'), may hold values from -0.15625 to 0.15625
- down_proj: bfloat16 [128, 1280, 1280], P('expert', 'rep'), may hold values from -0.125 to 0.125
- out_grad: bfloat16 [256, 256, 1280], P('expert', 'rep'), may hold values from -6 to 6
Outputs:
- tokens_grad: bfloat16 [256, 256, 1280], P('expert', 'rep')
- router_grad: float32 [1280, 64], replicated
- up_grad: bfloat16 [128, 1280, 1280], P('expert', 'rep')
- down_grad: bfloat16 [128, 1280, 1280], P('expert', 'rep')
Inputs may be any that keep to these rules, and one draw needn't show every extreme that they name: `tokens`: token features.
All inputs are finite; a program needn't handle non-finite values.
Results may differ from a plain program's by a relative error of at most 0.017.
Values may be sent and summed in bfloat16 or wider, within the bound.
No kernel may reach another device: no remote copies, remote signals or barrier semaphores. Data moves between devices by JAX's collectives and lax.ppermute only.
A program may use at most 64 MiB of HBM per device.

v0:
```python
import jax
import jax.numpy as jnp
from jax import lax
from jax.sharding import PartitionSpec as P


def gelu_exact(values):
    return jax.nn.gelu(values, approximate=False)


def on_device(tokens, router, up_proj, down_proj, out_grad):
    images_here = tokens.shape[0]
    feat_width = tokens.shape[2]
    groups = lax.axis_size("expert")
    logits = jnp.einsum("btd,ds->bts", tokens, router, preferred_element_type=jnp.float32)
    top_logit = lax.pmax(jnp.max(logits, axis=1), "rep")
    raised = jnp.exp(logits - top_logit[:, None, :])
    exp_total = lax.psum(jnp.sum(raised, axis=1), "rep")
    dispatch = raised / exp_total[:, None, :]
    combine = jax.nn.softmax(logits, axis=2)
    dispatch_w = dispatch.astype(jnp.bfloat16)
    combine_w = combine.astype(jnp.bfloat16)
    in_partial = jnp.einsum("bts,btd->bsd", dispatch_w, tokens, preferred_element_type=jnp.float32)
    grad_partial = jnp.einsum(
        "bts,btd->bsd", combine_w, out_grad, preferred_element_type=jnp.float32
    )
    in_summed, grad_summed = lax.psum((in_partial, grad_partial), "rep")
    in_rows = jnp.repeat(in_summed.astype(jnp.bfloat16), 2, axis=1)
    grad_rows = jnp.repeat(grad_summed.astype(jnp.bfloat16), 2, axis=1)
    in_rows, grad_rows = (
        lax.all_to_all(in_rows, "expert", split_axis=1, concat_axis=0, tiled=True),
        lax.all_to_all(grad_rows, "expert", split_axis=1, concat_axis=0, tiled=True),
    )
    slot_in = in_rows.reshape(-1, feat_width)
    slot_grad = grad_rows.reshape(-1, feat_width)
    w_up = up_proj[0]
    w_down = down_proj[0]
    contract_rows = (((1,), (1,)), ((), ()))
    contract_cols = (((0,), (0,)), ((), ()))
    pre_act = lax.dot_general(slot_in, w_up, contract_rows, preferred_element_type=jnp.float32)
    hidden = gelu_exact(pre_act).astype(jnp.bfloat16)
    out_partial = jnp.dot(hidden, w_down, preferred_element_type=jnp.float32)
    hid_grad = lax.dot_general(slot_grad, w_down, contract_rows, preferred_element_type=jnp.float32)
    unused, gelu_pull = jax.vjp(gelu_exact, pre_act)
    pre_grad = gelu_pull(hid_grad)[0].astype(jnp.bfloat16)
    up_grad = lax.dot_general(pre_grad, slot_in, contract_cols, preferred_element_type=jnp.float32)
    down_grad = lax.dot_general(
        hidden, slot_grad, contract_cols, preferred_element_type=jnp.float32
    )
    back_partial = jnp.dot(pre_grad, w_up, preferred_element_type=jnp.float32)
    out_blocks = out_partial.reshape(groups, images_here, feat_width)
    back_blocks = back_partial.reshape(groups, images_here, feat_width)
    out_blocks, back_blocks = (
        lax.all_to_all(out_blocks, "expert", split_axis=0, concat_axis=0, tiled=True),
        lax.all_to_all(back_blocks, "expert", split_axis=0, concat_axis=0, tiled=True),
    )
    out_pairs = (
        out_blocks.reshape(groups // 2, 2, images_here, feat_width).sum(axis=1).transpose(1, 0, 2)
    )
    back_pairs = (
        back_blocks.reshape(groups // 2, 2, images_here, feat_width).sum(axis=1).transpose(1, 0, 2)
    )
    out_total, back_total = lax.psum((out_pairs, back_pairs), "rep")
    slot_out = out_total.astype(jnp.bfloat16)
    slot_in_grad = back_total.astype(jnp.bfloat16)
    cgrad = jnp.einsum("btd,bsd->bts", out_grad, slot_out, preferred_element_type=jnp.float32)
    dgrad = jnp.einsum("btd,bsd->bts", tokens, slot_in_grad, preferred_element_type=jnp.float32)
    comb_part = combine * (cgrad - jnp.sum(combine * cgrad, axis=2, keepdims=True))
    disp_total = lax.psum(jnp.sum(dispatch * dgrad, axis=1), "rep")
    disp_part = dispatch * (dgrad - disp_total[:, None, :])
    logit_grad = (comb_part + disp_part).astype(jnp.bfloat16)
    tokens_grad = jnp.einsum(
        "bts,bsd->btd", dispatch_w, slot_in_grad, preferred_element_type=jnp.float32
    ) + jnp.einsum("bts,ds->btd", logit_grad, router, preferred_element_type=jnp.float32)
    router_local = jnp.einsum("btd,bts->ds", tokens, logit_grad, preferred_element_type=jnp.float32)
    router_grad = lax.psum(router_local, ("rep", "expert"))
    return (
        tokens_grad.astype(jnp.bfloat16),
        router_grad,
        up_grad.astype(jnp.bfloat16)[None],
        down_grad.astype(jnp.bfloat16)[None],
    )


def solution(mesh):
    return jax.shard_map(
        on_device,
        mesh=mesh,
        in_specs=(
            P("expert", "rep", None),
            P(),
            P("expert", "rep", None),
            P("expert", "rep", None),
            P("expert", "rep", None),
        ),
        out_specs=(
            P("expert", "rep", None),
            P(),
            P("expert", "rep", None),
            P("expert", "rep", None),
        ),
        check_vma=False,
    )
```

profile of v0, /device:TPU:1, one launch (start us, length us, event | category | flops | bytes accessed | tf_op | source)
XLA Modules:
  0.0 976.0 jit_solution(13192432915350298541)
XLA Ops:
  7.2 0.0 copy-start
  7.2 1.3 fusion.54
  8.5 20.6 %pmax.7 = f32[2,64]{1,0:T(2,128)S(1)} all-reduce(f32[2,64]{1,0:T(2,128)S(1)} %get-tuple-element.10), channel_id=1, replica_groups=mesh['rep'=4,'expert'=128] {'rep'}, use_global_device_ids=true, to_apply=%region_1.0 | all-reduce | flops 128 | bytes 1024 | tf_op jit(solution)/shard_map/pmax | solution.py:16
  29.1 0.7 fusion.53
  29.9 22.6 %psum.49 = f32[2,64]{1,0:T(2,128)S(1)} all-reduce(f32[2,64]{1,0:T(2,128)S(1)} %fusion.41), channel_id=1, replica_groups=mesh['rep'=4,'expert'=128] {'rep'}, use_global_device_ids=true, to_apply=%region_3.0 | all-reduce | flops 128 | bytes 1024 | tf_op jit(solution)/shard_map/psum | solution.py:18
  52.5 1.4 fusion.42
  53.9 0.3 fusion.45
  54.2 95.1 %all-reduce.8 = (bf16[2,64,1280]{2,1,0:T(8,128)(2,1)S(1)}, bf16[2,64,1280]{2,1,0:T(8,128)(2,1)S(1)}) all-reduce(f32[2,64,1280]{2,1,0:T(8,128)S(1)} %fusion.42, f32[2,64,1280]{2,1,0:T(8,128)S(1)} %fusion.45), channel_id=1, replica_groups=mesh['rep'=4,'expert'=128] {'rep'}, use_global_device_ids=true, to_apply=%region_7.0 | all-reduce | flops 327680 | bytes 1966080 | tf_op jit(solution)/shard_map/psum | solution.py:27
  149.2 0.3 copy.40
  149.6 1.2 broadcast_in_dim.9
  150.8 22.6 %all-to-all-start.1 = ((bf16[2,128,1280]{2,0,1:T(2,128)(2,1)}), bf16[2,128,1280]{2,0,1:T(2,128)(2,1)S(1)}, u32[]{:S(2)}, u32[]{:S(2)}) async-start(bf16[2,128,1280]{2,0,1:T(2,128)(2,1)} %bitcast.5), calls=%async_computation.1 | async-start | bytes 1310720 | tf_op jit(solution)/shard_map/all_to_all | solution.py:32
  173.4 0.3 copy.38
  173.7 35.8 %all-to-all-done.1 = bf16[2,128,1280]{2,0,1:T(2,128)(2,1)S(1)} async-done(((bf16[2,128,1280]{2,0,1:T(2,128)(2,1)}), bf16[2,128,1280]{2,0,1:T(2,128)(2,1)S(1)}, u32[]{:S(2)}, u32[]{:S(2)}) %all-to-all-start.1) | async-done | bytes 655392 | tf_op jit(solution)/shard_map/all_to_all | solution.py:32
  209.6 1.2 broadcast_in_dim.8
  210.7 8.2 all-to-all-start
  218.9 0.2 reshape.41
  219.2 35.9 %all-to-all-done = bf16[2,128,1280]{2,0,1:T(2,128)(2,1)S(1)} async-done(((bf16[2,128,1280]{2,0,1:T(2,128)(2,1)}), bf16[2,128,1280]{2,0,1:T(2,128)(2,1)S(1)}, u32[]{:S(2)}, u32[]{:S(2)}) %all-to-all-start) | async-done | bytes 655392 | tf_op jit(solution)/shard_map/all_to_all | solution.py:31
  255.1 0.2 reshape.39
  255.4 1.1 multiply_convert_fusion
  256.5 0.3 copy-done.7
  256.7 1.1 add_convert_fusion
  257.8 0.2 copy.41
  258.0 0.1 dot_general.57
  258.1 0.5 fusion.13
  258.6 2.1 copy.43
  260.7 8.1 all-to-all-start.2
  268.9 0.2 copy.45
  269.0 0.1 dot_general.60
  269.1 0.5 fusion.11
  269.6 2.1 copy.47
  271.7 59.5 %all-to-all-done.2 = f32[128,2,1280]{2,1,0:T(2,128)S(1)} async-done(((f32[128,2,1280]{2,1,0:T(2,128)}), f32[128,2,1280]{2,1,0:T(2,128)S(1)}, u32[]{:S(2)}, u32[]{:S(2)}) %all-to-all-start.2) | async-done | bytes 1310752 | tf_op jit(solution)/shard_map/all_to_all | solution.py:55
  331.3 9.6 all-to-all-start.3
  340.8 0.0 all-reduce.7.cloned.1.call-start
  340.9 2.5 fusion.3
  343.4 1.3 fusion.2
  344.7 0.6 bitcast_reduce_fusion.1
  345.4 53.7 %all-reduce.9 = bf16[2,64,1280]{2,1,0:T(8,128)(2,1)S(1)} all-reduce(f32[2,64,1280]{2,1,0:T(8,128)S(1)} %bitcast.77), channel_id=1, replica_groups=mesh['rep'=4,'expert'=128] {'rep'}, use_global_device_ids=true, to_apply=%region_9.0 | all-reduce | flops 163840 | bytes 983040 | tf_op jit(solution)/shard_map/psum | solution.py:63
  399.1 0.9 multiply_reduce_fusion.1
  399.9 0.2 fusion.34
  400.2 37.7 %all-to-all-done.3 = f32[128,2,1280]{2,1,0:T(2,128)S(1)} async-done(((f32[128,2,1280]{2,1,0:T(2,128)}), f32[128,2,1280]{2,1,0:T(2,128)S(1)}, u32[]{:S(2)}, u32[]{:S(2)}) %all-to-all-start.3) | async-done | bytes 1310752 | tf_op jit(solution)/shard_map/all_to_all | solution.py:54
  437.8 0.6 bitcast_reduce_fusion
  438.5 47.1 %all-reduce.10 = (bf16[2,64,1280]{2,1,0:T(8,128)(2,1)S(1)}, f32[2,64]{1,0:T(2,128)S(1)}) all-reduce(f32[2,64,1280]{2,1,0:T(8,128)S(1)} %bitcast.76, f32[2,64]{1,0:T(2,128)S(1)} %get-tuple-element.14), channel_id=1, replica_groups=mesh['rep'=4,'expert'=128] {'rep'}, use_global_device_ids=true, to_apply=%region_11.0 | all-reduce | flops 163968 | bytes 984064 | tf_op jit(solution)/shard_map/psum | solution.py:63
  485.7 0.2 convolution_bitcast_fusion.2
  485.9 2.1 convolution_bitcast_fusion
  488.0 0.0 all-reduce.7.cloned.1.call-update
  488.1 2.1 fusion.4
  490.1 477.3 %all-reduce.7.cloned.1.call-done = f32[1280,64]{0,1:T(8,128)} async-done(((f32[1280,64]{0,1:T(8,128)}), f32[1280,64]{0,1:T(8,128)}) %all-reduce.7.cloned.1.call-update) | async-done | bytes 327696 | tf_op jit(solution)/shard_map/psum | solution.py:76
  967.4 1.7 copy.73
  (27 shorter events, 0.2 us)
Async XLA Ops:
  7.2 248.2 %copy-start = (bf16[1,320,1280]{2,1,0:T(8,128)(2,1)S(1)}, bf16[1,320,1280]{2,1,0:T(8,128)(2,1)}, u32[]{:S(2)}) copy-start(bf16[1,320,1280]{2,1,0:T(8,128)(2,1)} %param.7) | copy-start | bytes 2457604
  7.2 46.7 %copy-start.1 = (bf16[2,64,1280]{2,1,0:T(8,128)(2,1)S(1)}, bf16[2,64,1280]{2,1,0:T(8,128)(2,1)}, u32[]{:S(2)}) copy-start(bf16[2,64,1280]{2,1,0:T(8,128)(2,1)} %param.5) | copy-start | bytes 983044
  150.8 58.8 %all-to-all-start.1 = ((bf16[2,128,1280]{2,0,1:T(2,128)(2,1)}), bf16[2,128,1280]{2,0,1:T(2,128)(2,1)S(1)}, u32[]{:S(2)}, u32[]{:S(2)}) async-start(bf16[2,128,1280]{2,0,1:T(2,128)(2,1)} %bitcast.5), calls=%async_computation.1 | async-start | bytes 1310720 | tf_op jit(solution)/shard_map/all_to_all | solution.py:32
  210.7 44.3 %all-to-all-start = ((bf16[2,128,1280]{2,0,1:T(2,128)(2,1)}), bf16[2,128,1280]{2,0,1:T(2,128)(2,1)S(1)}, u32[]{:S(2)}, u32[]{:S(2)}) async-start(bf16[2,128,1280]{2,0,1:T(2,128)(2,1)} %bitcast.1), calls=%async_computation | async-start | bytes 1310720 | tf_op jit(solution)/shard_map/all_to_all | solution.py:31
  219.2 37.3 %copy-start.3 = (bf16[256,1280]{1,0:T(8,128)(2,1)}, bf16[256,1280]{1,0:T(8,128)(2,1)S(1)}, u32[]{:S(2)}) copy-start(bf16[256,1280]{1,0:T(8,128)(2,1)S(1)} %reshape.41) | copy-start | bytes 1966084
  255.3 1.1 copy-start.4
  255.3 1.4 copy-start.7
  256.4 12.4 %copy-start.10 = (bf16[256,320]{0,1:T(8,128)(2,1)}, bf16[256,320]{0,1:T(8,128)(2,1)S(1)}, u32[]{:S(2)}) copy-start(bf16[256,320]{0,1:T(8,128)(2,1)S(1)} %get-tuple-element.12) | copy-start | bytes 491524
  257.8 0.8 copy-start.8
  260.7 70.5 %all-to-all-start.2 = ((f32[128,2,1280]{2,1,0:T(2,128)}), f32[128,2,1280]{2,1,0:T(2,128)S(1)}, u32[]{:S(2)}, u32[]{:S(2)}) async-start(f32[128,2,1280]{2,1,0:T(2,128)} %copy.43), calls=%async_computation.2 | async-start | bytes 2621440 | tf_op jit(solution)/shard_map/all_to_all | solution.py:55
  331.3 106.6 %all-to-all-start.3 = ((f32[128,2,1280]{2,1,0:T(2,128)}), f32[128,2,1280]{2,1,0:T(2,128)S(1)}, u32[]{:S(2)}, u32[]{:S(2)}) async-start(f32[128,2,1280]{2,1,0:T(2,128)} %copy.47), calls=%async_computation.3 | async-start | bytes 2621440 | tf_op jit(solution)/shard_map/all_to_all | solution.py:54
  340.8 626.6 %all-reduce.7.cloned.1.call-start = ((), (), s32[]{:S(2)}) async-start(), calls=%async_computation.4 | async-start | bytes 655360 | tf_op jit(solution)/shard_map/psum | solution.py:76
  340.9 2.5 copy-start.5
  340.9 2.5 copy-start.9
  345.3 53.8 %copy-start.2 = (bf16[2,64,1280]{2,1,0:T(8,128)(2,1)S(1)}, bf16[2,64,1280]{2,1,0:T(8,128)(2,1)}, u32[]{:S(2)}) copy-start(bf16[2,64,1280]{2,1,0:T(8,128)(2,1)} %param.5) | copy-start | bytes 983044
  438.4 47.2 %copy-start.6 = (bf16[2,64,1280]{2,1,0:T(8,128)(2,1)S(1)}, bf16[2,64,1280]{2,1,0:T(8,128)(2,1)}, u32[]{:S(2)}) copy-start(bf16[2,64,1280]{2,1,0:T(8,128)(2,1)} %param.9) | copy-start | bytes 983044
  438.5 47.4 %copy-start.12 = (f32[2,64,64]{2,1,0:T(8,128)S(1)}, f32[2,64,64]{2,1,0:T(8,128)}, u32[]{:S(2)}) copy-start(f32[2,64,64]{2,1,0:T(8,128)} %get-tuple-element.15) | copy-start | bytes 98308
  438.5 49.5 %copy-start.11 = (bf16[1280,64]{0,1:T(8,128)(2,1)S(1)}, bf16[1280,64]{0,1:T(8,128)(2,1)}, u32[]{:S(2)}) copy-start(bf16[1280,64]{0,1:T(8,128)(2,1)} %param.6) | copy-start | bytes 491524
Sparse Core Ops, SparseCore 0:
  488.2 479.1 all-reduce.6
where the time goes:
time: 977 us; the launch traced here: 976 us
  waiting for transfers between devices  646 us (66%)
  blocking collectives  239 us (24%)
  starting transfers between devices  48.5 us (5%)
  matrix products  15.4 us (2%)
  between operations  14.4 us (1%)
  local copies, waits for them, and re-layouts  10.4 us (1%)
    psum x1, waiting for transfers between devices, on_device(): router_grad = lax.psum(router_local, ('rep', 'expert'))  477 us
    psum x2, blocking collectives, on_device(): out_total, back_total = lax.psum((out_pairs, back_pairs), 'rep')  101 us
    psum x1, blocking collectives, on_device(): in_summed, grad_summed = lax.psum((in_partial, grad_partial), 'rep')  95.1 us
    all_to_all x1, waiting for transfers between devices, on_device(): lax.all_to_all(back_blocks, 'expert', split_axis=0, concat_axis=0, tiled=...  59.5 us
    all_to_all x1, waiting for transfers between devices, on_device(): lax.all_to_all(out_blocks, 'expert', split_axis=0, concat_axis=0, tiled=T...  37.7 us
    all_to_all x1, waiting for transfers between devices, on_device(): lax.all_to_all(in_rows, 'expert', split_axis=1, concat_axis=0, tiled=True)  35.9 us
    all_to_all x1, waiting for transfers between devices, on_device(): lax.all_to_all(grad_rows, 'expert', split_axis=1, concat_axis=0, tiled=True)  35.8 us
    all_to_all x1, starting transfers between devices, on_device(): lax.all_to_all(grad_rows, 'expert', split_axis=1, concat_axis=0, tiled=True)  22.6 us
  transfers between devices with their start and end apart: 5, of which 5 were waited for; matrix products, arithmetic and copies ran while one was open for 1% of the time, Pallas kernels for 0%

commit v1 on v0

v1 whole, which is shorter than its diff:
```python
import functools
import jax
import jax.numpy as jnp
from jax import lax
from jax.experimental import pallas as pl
from jax.experimental.pallas import tpu as pltpu
from jax.sharding import Mesh, PartitionSpec as P

D = 1280
LANES = 128
WIDE = D + LANES
SLOTS = 64
Y, ZL, XH = 4, 8, 2
PLANE = ("y", "xh", "xl")
COLUMN = ("zh", "zl")
EVERY_GROUP = ("y", "zl", "xh", "xl")
bf16, f32 = jnp.bfloat16, jnp.float32
NT = (((1,), (1,)), ((), ()))
TN = (((0,), (0,)), ((), ()))
SMEM = pl.BlockSpec(memory_space=pltpu.SMEM)
VMEM = pl.BlockSpec(memory_space=pltpu.VMEM)


def call(kernel, outs, *operands, flops=0):
    bytes_accessed = sum(a.size * a.dtype.itemsize for a in list(operands) + list(outs))
    return pl.pallas_call(
        kernel,
        out_shape=outs,
        in_specs=[SMEM] + [VMEM] * (len(operands) - 1),
        out_specs=[VMEM] * len(outs),
        compiler_params=pltpu.CompilerParams(vmem_limit_bytes=48 * 1024 * 1024),
        cost_estimate=pl.CostEstimate(flops=flops, bytes_accessed=bytes_accessed, transcendentals=0),
    )(*operands)


def shaped(shape, dtype):
    return jax.ShapeDtypeStruct(shape, dtype)


def pieces(value):
    first = value.astype(bf16).astype(f32)
    second = (value - first).astype(bf16).astype(f32)
    third = (value - first - second).astype(bf16).astype(f32)
    return [first, second, third]


def lanes_of(columns):
    rows = columns[0].shape[0]
    lane = lax.broadcasted_iota(jnp.int32, (rows, LANES), 1)
    packed = jnp.zeros((rows, LANES), f32)
    for k, column in enumerate(columns):
        packed = jnp.where(lane == k, column, packed)
    return packed


def three(stats, first):
    return stats[:, first : first + 1] + stats[:, first + 1 : first + 2] + stats[:, first + 2 : first + 3]


def combine_of(logits):
    raised = jnp.exp(logits - jnp.max(logits, axis=0, keepdims=True))
    return raised / jnp.sum(raised, axis=0, keepdims=True)


def slots_kernel(core, router_t, tok_a, tok_b, grad_a, grad_b, out):
    on_first = core[0] == 0
    rows = []
    for image in range(2):
        tok = jnp.concatenate([tok_a[image], tok_b[image]], axis=0)
        grad = jnp.concatenate([grad_a[image], grad_b[image]], axis=0)
        logits = lax.dot_general(router_t[...], tok, NT, preferred_element_type=f32)
        top = jnp.max(logits, axis=1, keepdims=True)
        raised = jnp.exp(logits - top)
        total = jnp.sum(raised, axis=1, keepdims=True)
        weights = jnp.where(on_first, raised / total, combine_of(logits)).astype(bf16)
        data = jnp.where(on_first, tok, grad)
        part = jnp.dot(weights, data, preferred_element_type=f32)
        rows.append((part, lanes_of(pieces(top) + pieces(total))))
    for zl in range(ZL):
        at = slice(zl * 8, zl * 8 + 8)
        for zh in range(2):
            place = zh * ZL + zl
            out[place, :, :D] = jnp.concatenate([rows[0][0][at], rows[1][0][at]], axis=0).astype(bf16)
            out[place, :, D:] = jnp.concatenate([rows[0][1][at], rows[1][1][at]], axis=0).astype(bf16)


def middle_kernel(core, got, out, kept, stats_out):
    on_first = core[0] == 0
    stats = [got[h * ZL : (h + 1) * ZL, :, D:].reshape(LANES, LANES).astype(f32) for h in range(2)]
    tops = [three(s, 0) for s in stats]
    totals = [three(s, 3) for s in stats]
    top = jnp.maximum(tops[0], tops[1])
    parts = [totals[h] * jnp.exp(tops[h] - top) for h in range(2)]
    total = parts[0] + parts[1]
    shares = [jnp.where(on_first, part / total, 1.0) for part in parts]
    halves = [got[h * ZL : (h + 1) * ZL, :, :D].reshape(LANES, D).astype(f32) for h in range(2)]
    summed = halves[0] * shares[0] + halves[1] * shares[1]
    kept[...] = summed
    stats_out[...] = lanes_of([top, total])
    row = lax.broadcasted_iota(jnp.int32, (LANES, LANES), 0)
    col = lax.broadcasted_iota(jnp.int32, (LANES, LANES), 1)
    source = ((row & 15) >> 1) * 16 + (row & 1) * 8 + (row >> 4)
    pick = jnp.where(col == source, 1.0, 0.0).astype(bf16)
    sorted_rows = jnp.dot(pick, summed.astype(bf16), preferred_element_type=f32).astype(bf16)
    for yx in range(Y * XH):
        for xl in range(2):
            out[2 * yx + xl] = sorted_rows[yx * 16 : yx * 16 + 16]


def expert_kernel(core, mine, other, w_up, w_down, up_grad, down_grad, keep, send):
    on_first = core[0] == 0
    slot_in = jnp.where(on_first, mine[...], other[...])
    slot_grad = jnp.where(on_first, other[...], mine[...])
    pre_act = lax.dot_general(slot_in, w_up[...], NT, preferred_element_type=f32)
    hid_grad = lax.dot_general(slot_grad, w_down[...], NT, preferred_element_type=f32)
    cdf = 0.5 * (1.0 + lax.erf(pre_act * 0.7071067811865476))
    density = jnp.exp(pre_act * pre_act * -0.5) * 0.3989422804014327
    hidden = (pre_act * cdf).astype(bf16)
    pre_grad = (hid_grad * (cdf + pre_act * density)).astype(bf16)
    slot_out = jnp.dot(hidden, w_down[...], preferred_element_type=f32)
    in_grad = jnp.dot(pre_grad, w_up[...], preferred_element_type=f32)
    keep[...] = jnp.where(on_first, in_grad, slot_out)
    send[...] = jnp.where(on_first, slot_out, in_grad).astype(bf16)
    up_grad[0] = lax.dot_general(pre_grad, slot_in, TN, preferred_element_type=f32).astype(bf16)
    down_grad[0] = lax.dot_general(hidden, slot_grad, TN, preferred_element_type=f32).astype(bf16)


def return_kernel(core, got, kept, stats, out):
    row = lax.broadcasted_iota(jnp.int32, (LANES, 2 * LANES), 0)
    col = lax.broadcasted_iota(jnp.int32, (LANES, 2 * LANES), 1)
    source = (row & 7) * 32 + (row >> 4) * 2 + ((row >> 3) & 1)
    pick = jnp.where((col & ~16) == source, 1.0, 0.0).astype(bf16)
    summed = jnp.dot(pick, got[...], preferred_element_type=f32).astype(bf16)
    share = jnp.sum(kept[...] * summed.astype(f32), axis=1, keepdims=True)
    top, total = stats[:, 0:1], stats[:, 1:2]
    extra = lanes_of(pieces(share) + pieces(top) + pieces(total)).astype(bf16)
    for zl in range(ZL):
        at = slice(zl * 16, zl * 16 + 16)
        for zh in range(2):
            out[zh * ZL + zl, :, :D] = summed[at]
            out[zh * ZL + zl, :, D:] = extra[at]


def tokens_kernel(core, router_t, tok_a, tok_b, grad_a, grad_b, mine, other, tokens_grad, router_grad):
    on_first = core[0] == 0
    back = [jnp.where(on_first, mine[h * ZL : (h + 1) * ZL], other[h * ZL : (h + 1) * ZL]).astype(f32) for h in range(2)]
    outs = [jnp.where(on_first, other[h * ZL : (h + 1) * ZL], mine[h * ZL : (h + 1) * ZL]).astype(f32) for h in range(2)]
    back_sum = back[0] + back[1]
    outs_sum = outs[0] + outs[1]
    router_sum = jnp.zeros((SLOTS, D), f32)
    for image in range(2):
        at = slice(image * 8, image * 8 + 8)
        slot_in_grad = back_sum[:, at, :D].reshape(SLOTS, D).astype(bf16)
        slot_out = outs_sum[:, at, :D].reshape(SLOTS, D).astype(bf16)
        weighted = three(back_sum[:, at, D:].reshape(SLOTS, LANES), 0)
        stats = back[0][:, at, D:].reshape(SLOTS, LANES)
        top, total = three(stats, 3), three(stats, 6)
        tok = jnp.concatenate([tok_a[image], tok_b[image]], axis=0)
        grad = jnp.concatenate([grad_a[image], grad_b[image]], axis=0)
        logits = lax.dot_general(router_t[...], tok, NT, preferred_element_type=f32)
        dispatch = jnp.exp(logits - top) / total
        combine = combine_of(logits)
        cgrad = lax.dot_general(slot_out, grad, NT, preferred_element_type=f32)
        dgrad = lax.dot_general(slot_in_grad, tok, NT, preferred_element_type=f32)
        comb_part = combine * (cgrad - jnp.sum(combine * cgrad, axis=0, keepdims=True))
        disp_part = dispatch * (dgrad - weighted)
        logit_grad = comb_part + disp_part
        router_sum += jnp.dot(logit_grad.astype(bf16), tok, preferred_element_type=f32)
        left = jnp.concatenate([dispatch[:, :64], logit_grad[:, :64]], axis=0).astype(bf16)
        right = jnp.concatenate([slot_in_grad, router_t[...]], axis=0)
        tokens_grad[image] = lax.dot_general(left, right, TN, preferred_element_type=f32).astype(bf16)
    router_grad[...] = router_sum.astype(bf16)


def swap(value):
    return lax.ppermute(value, "core", [(0, 1), (1, 0)])


def exchange(value, axes):
    return lax.all_to_all(value, axes, split_axis=0, concat_axis=0, tiled=True)


def on_device(tokens, router, up_proj, down_proj, out_grad):
    core = lax.axis_index("core").astype(jnp.int32).reshape(1)
    router_t = router.T.reshape(Y, ZL, XH, D).transpose(1, 0, 2, 3).reshape(SLOTS, D)
    tok_b, grad_b = swap(tokens), swap(out_grad)
    (slots,) = call(
        slots_kernel, [shaped((16, 16, WIDE), bf16)], core, router_t, tokens, tok_b, out_grad, grad_b
    )
    got = exchange(slots, COLUMN)
    by_expert, kept, stats = call(
        middle_kernel,
        [shaped((16, 16, D), bf16), shaped((LANES, D), f32), shaped((LANES, LANES), f32)],
        core, got,
    )
    mine = exchange(by_expert, PLANE).reshape(256, D)
    other = swap(mine)
    up_grad, down_grad, keep, send = call(
        expert_kernel,
        [shaped((1, 320, D), bf16), shaped((1, 320, D), bf16), shaped((256, D), f32), shaped((256, D), bf16)],
        core, mine, other, up_proj[0], down_proj[0],
    )
    summed = (keep + swap(send).astype(f32)).astype(bf16).reshape(16, 16, D)
    back = exchange(summed, PLANE).reshape(256, D)
    (by_owner,) = call(return_kernel, [shaped((16, 16, WIDE), bf16)], core, back, kept, stats)
    mine = exchange(by_owner, COLUMN)
    other = swap(mine)
    tokens_grad, router_part = call(
        tokens_kernel,
        [shaped((2, 64, D), bf16), shaped((SLOTS, D), bf16)],
        core, router_t, tokens, tok_b, out_grad, grad_b, mine, other,
    )
    part = exchange(router_part.reshape(16, 4, D), PLANE).astype(f32).sum(axis=0).astype(bf16)
    whole = exchange(jnp.broadcast_to(part, (16, 4, D)), COLUMN).astype(f32).sum(axis=0).astype(bf16)
    full = exchange(jnp.broadcast_to(whole, (16, 4, D)), PLANE).reshape(ZL, Y, XH, D)
    router_grad = full.transpose(1, 0, 2, 3).reshape(SLOTS, D).T.astype(f32)
    return tokens_grad, router_grad, up_grad, down_grad


def solution(mesh):
    fine = Mesh(mesh.devices.reshape(2, 2, Y, ZL, XH, 2), ("zh", "core", "y", "zl", "xh", "xl"))
    rows = P(EVERY_GROUP, ("zh", "core"), None)
    return jax.shard_map(
        on_device,
        mesh=fine,
        in_specs=(rows, P(), rows, rows, rows),
        out_specs=(rows, P(), rows, rows),
        check_vma=False,
    )
```

time: 977 us -> 205 us (0.21)
  the two profiles are of different devices: /device:TPU:1 before, /device:TPU:32 now
where the time goes in v1:
time: 205 us
  blocking collectives  175 us (85%)
  starting transfers between devices  10.2 us (5%)
  Pallas kernels  7.19 us (4%)
  waiting for transfers between devices  6.42 us (3%)
  local copies, waits for them, and re-layouts  4.4 us (2%)
    all_to_all x7, blocking collectives, exchange(): return lax.all_to_all(value, axes, split_axis=0, concat_axis=0, tiled=True)  175 us
    ppermute x5, starting transfers between devices, swap(): return lax.ppermute(value, 'core', [(0, 1), (1, 0)])  10.2 us
    pallas_call x5, Pallas kernels, call(): pl.pallas_call(kernel, out_shape=outs, in_specs=[SMEM] + [VMEM] * (len(op...  7.19 us
    ppermute x5, waiting for transfers between devices, swap(): return lax.ppermute(value, 'core', [(0, 1), (1, 0)])  6.42 us
  transfers between devices with their start and end apart: 5, of which 4 were waited for; matrix products, arithmetic and copies ran while one was open for 1% of the time, Pallas kernels for 0%

profile of v1, /device:TPU:32, one launch (start us, length us, event | category | flops | bytes accessed | tf_op | source)
XLA Modules:
  0.0 204.7 jit_solution(7630723745764312528)
XLA Ops:
  0.6 1.9 collective-permute-start
  2.6 2.4 %collective-permute-start.1 = (bf16[2,64,1280]{2,1,0:T(8,128)(2,1)}, bf16[2,64,1280]{2,1,0:T(8,128)(2,1)S(1)}, u32[]{:S(2)}, u32[]{:S(2)}) collective-permute-start(bf16[2,64,1280]{2,1,0:T(8,128)(2,1)} %grad_a.3), channel_id=1, source_target_pairs={{0,128},{128,0},{1,129},{129,1},{2,130},{130,2},{3,131},{131,3},{4... | collective-permute-start | bytes 983048 | tf_op jit(solution)/shard_map/ppermute | solution.py:176
  5.0 1.0 reshape.36
  6.0 0.1 copy.20
  6.1 0.1 reshape.37.router_t
  6.2 0.0 collective-permute-done.tok_b
  6.2 0.3 collective-permute-done.1.grad_b
  6.4 0.0 copy-start
  6.4 1.0 copy-done
  7.4 0.0 copy-start.2
  7.4 1.0 copy-done.2
  8.4 1.2 shard_map.84
  9.6 53.9 %all_to_all.35.got = bf16[16,16,1408]{2,1,0:T(8,128)(2,1)S(1)} all-to-all(bf16[16,16,1408]{2,1,0:T(8,128)(2,1)S(1)} %shard_map.84), channel_id=1, replica_groups=mesh['zh'=2,'core'=2,'y'=4,'zl'=8,'xh'=2,'xl'=2] {'zh','zl'}, dimensions={0} | all-to-all | bytes 1441792 | tf_op jit(solution)/shard_map/all_to_all | solution.py:180
  63.5 0.0 copy-start.4
  63.5 0.0 copy-start.5
  63.5 0.5 shard_map.85
  64.0 19.3 %all_to_all.36 = bf16[16,16,1280]{2,1,0:T(8,128)(2,1)S(1)} all-to-all(bf16[16,16,1280]{2,1,0:T(8,128)(2,1)S(1)} %get-tuple-element.13), channel_id=1, replica_groups=mesh['zh'=2,'core'=2,'y'=4,'zl'=8,'xh'=2,'xl'=2] {'y','xh','xl'}, dimensions={0} | all-to-all | bytes 1310720 | tf_op jit(solution)/shard_map/all_to_all | solution.py:180
  83.3 1.9 collective-permute-start.2
  85.2 2.1 %collective-permute-done.2.other = bf16[256,1280]{1,0:T(8,128)(2,1)S(1)} collective-permute-done((bf16[256,1280]{1,0:T(8,128)(2,1)S(1)}, bf16[256,1280]{1,0:T(8,128)(2,1)S(1)}, u32[]{:S(2)}, u32[]{:S(2)}) %collective-permute-start.2) | collective-permute-done | bytes 655392 | tf_op jit(solution)/shard_map/ppermute | solution.py:176
  87.3 0.0 copy-done.4
  87.3 0.0 copy-done.5
  87.3 2.9 %shard_map.86 = (bf16[1,320,1280]{2,1,0:T(8,128)(2,1)}, bf16[1,320,1280]{2,1,0:T(8,128)(2,1)}, f32[256,1280]{1,0:T(8,128)S(1)}, bf16[256,1280]{1,0:T(8,128)(2,1)S(1)}) custom-call(s32[1]{0:T(128)} %bitcast.core, bf16[256,1280]{1,0:T(8,128)(2,1)S(1)} %bitcast.14, bf16[256,1280]{1,0:T(8,128)(2,1)S(1)} %collective-permute-done.2.other, ...), custom_call_target="tpu_custom_call" | custom-call | bytes 6553604 | tf_op jit(solution)/shard_map/pallas_call | solution.py:26
  90.2 2.0 collective-permute-start.3
  92.2 1.9 collective-permute-done.3
  94.2 0.1 add_convert_fusion
  94.3 16.4 %all_to_all.37 = bf16[16,16,1280]{2,1,0:T(8,128)(2,1)S(1)} all-to-all(bf16[16,16,1280]{2,1,0:T(8,128)(2,1)S(1)} %bitcast.17), channel_id=1, replica_groups=mesh['zh'=2,'core'=2,'y'=4,'zl'=8,'xh'=2,'xl'=2] {'y','xh','xl'}, dimensions={0} | all-to-all | bytes 1310720 | tf_op jit(solution)/shard_map/all_to_all | solution.py:180
  110.7 0.0 copy-start.1
  110.7 0.0 copy-start.3
  110.7 0.4 shard_map.87
  111.1 43.7 %all_to_all.38.mine = bf16[16,16,1408]{2,1,0:T(8,128)(2,1)S(1)} all-to-all(bf16[16,16,1408]{2,1,0:T(8,128)(2,1)S(1)} %shard_map.87), channel_id=1, replica_groups=mesh['zh'=2,'core'=2,'y'=4,'zl'=8,'xh'=2,'xl'=2] {'zh','zl'}, dimensions={0} | all-to-all | bytes 1441792 | tf_op jit(solution)/shard_map/all_to_all | solution.py:180
  154.8 1.9 collective-permute-start.4
  156.7 2.2 %collective-permute-done.4.other = bf16[16,16,1408]{2,1,0:T(8,128)(2,1)S(1)} collective-permute-done((bf16[16,16,1408]{2,1,0:T(8,128)(2,1)S(1)}, bf16[16,16,1408]{2,1,0:T(8,128)(2,1)S(1)}, u32[]{:S(2)}, u32[]{:S(2)}) %collective-permute-start.4) | collective-permute-done | bytes 720928 | tf_op jit(solution)/shard_map/ppermute | solution.py:176
  158.9 0.0 copy-done.1
  158.9 0.0 copy-done.3
  158.9 2.2 %shard_map.88 = (bf16[2,64,1280]{2,1,0:T(8,128)(2,1)}, bf16[64,1280]{1,0:T(8,128)(2,1)S(1)}) custom-call(s32[1]{0:T(128)} %bitcast.core, bf16[64,1280]{1,0:T(8,128)(2,1)S(1)} %reshape.37.router_t, bf16[2,64,1280]{2,1,0:T(8,128)(2,1)S(1)} %copy-done.1, bf16[2,64,1280]{2,1,0:T(8,128)(2,1)S(1)} %collective-permute-done.tok_b, ...), custom_call_target="tpu_custom_call" | custom-call | bytes 3407876 | tf_op jit(solution)/shard_map/pallas_call | solution.py:26
  161.1 11.6 %all_to_all.39 = bf16[16,4,1280]{2,1,0:T(4,128)(2,1)S(1)} all-to-all(bf16[16,4,1280]{2,1,0:T(4,128)(2,1)S(1)} %reshape.41), channel_id=1, replica_groups=mesh['zh'=2,'core'=2,'y'=4,'zl'=8,'xh'=2,'xl'=2] {'y','xh','xl'}, dimensions={0} | all-to-all | bytes 327680 | tf_op jit(solution)/shard_map/all_to_all | solution.py:180
  172.7 0.1 reduce_sum.24
  172.8 19.0 %all_to_all.40 = bf16[16,4,1280]{2,1,0:T(4,128)(2,1)S(1)} all-to-all(bf16[16,4,1280]{2,1,0:T(4,128)(2,1)S(1)} %broadcast_in_dim.6), channel_id=1, replica_groups=mesh['zh'=2,'core'=2,'y'=4,'zl'=8,'xh'=2,'xl'=2] {'zh','zl'}, dimensions={0} | all-to-all | bytes 327680 | tf_op jit(solution)/shard_map/all_to_all | solution.py:180
  191.9 0.1 reduce_sum.25
  192.0 11.5 %all_to_all.41 = bf16[16,4,1280]{2,1,0:T(4,128)(2,1)S(1)} all-to-all(bf16[16,4,1280]{2,1,0:T(4,128)(2,1)S(1)} %broadcast_in_dim.7), channel_id=1, replica_groups=mesh['zh'=2,'core'=2,'y'=4,'zl'=8,'xh'=2,'xl'=2] {'y','xh','xl'}, dimensions={0} | all-to-all | bytes 327680 | tf_op jit(solution)/shard_map/all_to_all | solution.py:180
  203.6 0.2 reshape.43
  203.8 0.9 reshape.42
  (4 shorter events, 0.2 us)
Async XLA Ops:
  0.6 5.5 %collective-permute-start = (bf16[2,64,1280]{2,1,0:T(8,128)(2,1)}, bf16[2,64,1280]{2,1,0:T(8,128)(2,1)S(1)}, u32[]{:S(2)}, u32[]{:S(2)}) collective-permute-start(bf16[2,64,1280]{2,1,0:T(8,128)(2,1)} %tok_a.3), channel_id=1, source_target_pairs={{0,128},{128,0},{1,129},{129,1},{2,130},{130,2},{3,131},{131,3},{4... | collective-permute-start | bytes 983048 | tf_op jit(solution)/shard_map/ppermute | solution.py:176
  2.6 3.9 %collective-permute-start.1 = (bf16[2,64,1280]{2,1,0:T(8,128)(2,1)}, bf16[2,64,1280]{2,1,0:T(8,128)(2,1)S(1)}, u32[]{:S(2)}, u32[]{:S(2)}) collective-permute-start(bf16[2,64,1280]{2,1,0:T(8,128)(2,1)} %grad_a.3), channel_id=1, source_target_pairs={{0,128},{128,0},{1,129},{129,1},{2,130},{130,2},{3,131},{131,3},{4... | collective-permute-start | bytes 983048 | tf_op jit(solution)/shard_map/ppermute | solution.py:176
  6.4 1.0 copy-start
  7.4 1.0 copy-start.2
  63.5 23.8 %copy-start.4 = (bf16[1,320,1280]{2,1,0:T(8,128)(2,1)S(1)}, bf16[1,320,1280]{2,1,0:T(8,128)(2,1)}, u32[]{:S(2)}) copy-start(bf16[1,320,1280]{2,1,0:T(8,128)(2,1)} %param.7) | copy-start | bytes 2457604
  63.5 23.8 %copy-start.5 = (bf16[1,320,1280]{2,1,0:T(8,128)(2,1)S(1)}, bf16[1,320,1280]{2,1,0:T(8,128)(2,1)}, u32[]{:S(2)}) copy-start(bf16[1,320,1280]{2,1,0:T(8,128)(2,1)} %param.8) | copy-start | bytes 2457604
  83.3 4.0 %collective-permute-start.2 = (bf16[256,1280]{1,0:T(8,128)(2,1)S(1)}, bf16[256,1280]{1,0:T(8,128)(2,1)S(1)}, u32[]{:S(2)}, u32[]{:S(2)}) collective-permute-start(bf16[256,1280]{1,0:T(8,128)(2,1)S(1)} %bitcast.13), channel_id=1, source_target_pairs={{0,128},{128,0},{1,129},{129,1},{2,130},{130,2},{3,131},{131,3},{4... | collective-permute-start | bytes 1966088 | tf_op jit(solution)/shard_map/ppermute | solution.py:176
  90.2 4.0 %collective-permute-start.3 = (bf16[256,1280]{1,0:T(8,128)(2,1)S(1)}, bf16[256,1280]{1,0:T(8,128)(2,1)S(1)}, u32[]{:S(2)}, u32[]{:S(2)}) collective-permute-start(bf16[256,1280]{1,0:T(8,128)(2,1)S(1)} %get-tuple-element.15), channel_id=1, source_target_pairs={{0,128},{128,0},{1,129},{129,1},{2,130},{130,2},{3,131},{131,3},{4... | collective-permute-start | bytes 1966088 | tf_op jit(solution)/shard_map/ppermute | solution.py:176
  110.7 48.2 %copy-start.1 = (bf16[2,64,1280]{2,1,0:T(8,128)(2,1)S(1)}, bf16[2,64,1280]{2,1,0:T(8,128)(2,1)}, u32[]{:S(2)}) copy-start(bf16[2,64,1280]{2,1,0:T(8,128)(2,1)} %tok_a.3) | copy-start | bytes 983044
  110.7 48.2 %copy-start.3 = (bf16[2,64,1280]{2,1,0:T(8,128)(2,1)S(1)}, bf16[2,64,1280]{2,1,0:T(8,128)(2,1)}, u32[]{:S(2)}) copy-start(bf16[2,64,1280]{2,1,0:T(8,128)(2,1)} %grad_a.3) | copy-start | bytes 983044
  154.8 4.1 %collective-permute-start.4 = (bf16[16,16,1408]{2,1,0:T(8,128)(2,1)S(1)}, bf16[16,16,1408]{2,1,0:T(8,128)(2,1)S(1)}, u32[]{:S(2)}, u32[]{:S(2)}) collective-permute-start(bf16[16,16,1408]{2,1,0:T(8,128)(2,1)S(1)} %all_to_all.38.mine), channel_id=1, source_target_pairs={{0,128},{128,0},{1,129},{129,1},{2,130},{130,2},{3,131},{131,3},{4... | collective-permute-start | bytes 2162696 | tf_op jit(solution)/shard_map/ppermute | solution.py:176

commit v2 on v1

v2 whole, which is shorter than its diff:
```python
import jax
import jax.numpy as jnp
from jax import lax
from jax.experimental import pallas as pl
from jax.experimental.pallas import tpu as pltpu
from jax.sharding import Mesh, PartitionSpec as P

D = 1280
LANES = 128
WIDE = D + LANES
SLOTS = 64
Y, ZL, XH = 4, 8, 2
PLANE = ("y", "xh", "xl")
PLANE_CORES = ("core", "y", "xh", "xl")
COLUMN = ("zh", "zl")
EVERY_GROUP = ("y", "zl", "xh", "xl")
bf16, f32 = jnp.bfloat16, jnp.float32
NT = (((1,), (1,)), ((), ()))
TN = (((0,), (0,)), ((), ()))
SMEM = pl.BlockSpec(memory_space=pltpu.SMEM)
VMEM = pl.BlockSpec(memory_space=pltpu.VMEM)
ANY = pl.BlockSpec(memory_space=pl.ANY)


def call(kernel, outs, *operands, after=()):
    body = kernel
    if after:
        first, last = len(operands), len(operands) + len(after)
        body = lambda *refs: kernel(*refs[:first], *refs[last:])
    bytes_accessed = sum(a.size * a.dtype.itemsize for a in list(operands) + list(outs))
    return pl.pallas_call(
        body,
        out_shape=outs,
        in_specs=[SMEM] + [VMEM] * (len(operands) - 1) + [ANY] * len(after),
        out_specs=[VMEM] * len(outs),
        compiler_params=pltpu.CompilerParams(vmem_limit_bytes=48 * 1024 * 1024),
        cost_estimate=pl.CostEstimate(flops=0, bytes_accessed=bytes_accessed, transcendentals=0),
    )(*operands, *after)


def shaped(shape, dtype):
    return jax.ShapeDtypeStruct(shape, dtype)


def pieces(value):
    first = value.astype(bf16).astype(f32)
    second = (value - first).astype(bf16).astype(f32)
    third = (value - first - second).astype(bf16).astype(f32)
    return [first, second, third]


def lanes_of(columns):
    rows = columns[0].shape[0]
    lane = lax.broadcasted_iota(jnp.int32, (rows, LANES), 1)
    packed = jnp.zeros((rows, LANES), f32)
    for k, column in enumerate(columns):
        packed = jnp.where(lane == k, column, packed)
    return packed


def three(stats, first):
    return stats[:, first : first + 1] + stats[:, first + 1 : first + 2] + stats[:, first + 2 : first + 3]


def combine_of(logits):
    raised = jnp.exp(logits - jnp.max(logits, axis=0, keepdims=True))
    return raised / jnp.sum(raised, axis=0, keepdims=True)


def slots_kernel(where_am_i, router_t, tok_a, tok_b, grad_a, grad_b, keep, send):
    on_first, zh = where_am_i[0] == 0, where_am_i[1]
    for image, out in ((1 - zh, send), (zh, keep)):
        tok = jnp.concatenate([tok_a[image], tok_b[image]], axis=0)
        grad = jnp.concatenate([grad_a[image], grad_b[image]], axis=0)
        logits = lax.dot_general(router_t[...], tok, NT, preferred_element_type=f32)
        top = jnp.max(logits, axis=1, keepdims=True)
        raised = jnp.exp(logits - top)
        total = jnp.sum(raised, axis=1, keepdims=True)
        weights = jnp.where(on_first, raised / total, combine_of(logits)).astype(bf16)
        data = jnp.where(on_first, tok, grad)
        out[:, :D] = jnp.dot(weights, data, preferred_element_type=f32).astype(out.dtype)
        out[:, D:] = lanes_of(pieces(top) + pieces(total)).astype(out.dtype)


def join_kernel(where_am_i, keep, got, out):
    on_first = where_am_i[0] == 0
    halves = [keep[...], got[...].astype(f32)]
    tops = [three(h[:, D:], 0) for h in halves]
    totals = [three(h[:, D:], 3) for h in halves]
    top = jnp.maximum(tops[0], tops[1])
    parts = [totals[h] * jnp.exp(tops[h] - top) for h in range(2)]
    total = parts[0] + parts[1]
    shares = [jnp.where(on_first, part / total, 1.0) for part in parts]
    rows = (halves[0][:, :D] * shares[0] + halves[1][:, :D] * shares[1]).astype(bf16)
    out[0] = rows
    out[1] = rows


def middle_kernel(where_am_i, got, tok_a, grad_a, out, tok_out, grad_out):
    zh = where_am_i[1]
    row = lax.broadcasted_iota(jnp.int32, (LANES, LANES), 0)
    col = lax.broadcasted_iota(jnp.int32, (LANES, LANES), 1)
    pick = jnp.where(col == (row & 15) * 8 + (row >> 4), 1.0, 0.0).astype(bf16)
    sorted_rows = jnp.dot(pick, got[...], preferred_element_type=f32).astype(bf16)
    for yx in range(Y * XH):
        for xl in range(2):
            out[2 * yx + xl] = sorted_rows[yx * 16 : yx * 16 + 16]
    tok_out[...] = tok_a[1 - zh]
    grad_out[...] = grad_a[1 - zh]


def expert_kernel(where_am_i, mine, other, w_up, w_down, up_grad, down_grad, keep, send):
    on_first = where_am_i[0] == 0
    slot_in = jnp.where(on_first, mine[...], other[...])
    slot_grad = jnp.where(on_first, other[...], mine[...])
    pre_act = lax.dot_general(slot_in, w_up[...], NT, preferred_element_type=f32)
    hid_grad = lax.dot_general(slot_grad, w_down[...], NT, preferred_element_type=f32)
    cdf = 0.5 * (1.0 + lax.erf(pre_act * 0.7071067811865476))
    density = jnp.exp(pre_act * pre_act * -0.5) * 0.3989422804014327
    hidden = (pre_act * cdf).astype(bf16)
    pre_grad = (hid_grad * (cdf + pre_act * density)).astype(bf16)
    slot_out = jnp.dot(hidden, w_down[...], preferred_element_type=f32)
    in_grad = jnp.dot(pre_grad, w_up[...], preferred_element_type=f32)
    keep[...] = jnp.where(on_first, in_grad, slot_out)
    send[...] = jnp.where(on_first, slot_out, in_grad).astype(bf16)
    up_grad[0] = lax.dot_general(pre_grad, slot_in, TN, preferred_element_type=f32).astype(bf16)
    down_grad[0] = lax.dot_general(hidden, slot_grad, TN, preferred_element_type=f32).astype(bf16)


def return_kernel(where_am_i, got, out):
    row = lax.broadcasted_iota(jnp.int32, (LANES, 2 * LANES), 0)
    col = lax.broadcasted_iota(jnp.int32, (LANES, 2 * LANES), 1)
    pick = jnp.where((col & ~16) == (row & 7) * 32 + (row >> 3), 1.0, 0.0).astype(bf16)
    out[...] = jnp.dot(pick, got[...], preferred_element_type=f32).astype(bf16)


def halves_kernel(where_am_i, got, out):
    out[...] = (got[:SLOTS].astype(f32) + got[SLOTS:].astype(f32)).astype(bf16)


def tokens_kernel(
    where_am_i, router_t, tok_a, tok_b, tok_c, tok_d, grad_a, grad_b, grad_c, grad_d, mine, other,
    own_grad, sent_grad, router_grad,
):
    on_first, zh = where_am_i[0] == 0, where_am_i[1]

    slot_in_grad = jnp.where(on_first, mine[...], other[...])
    slot_out = jnp.where(on_first, other[...], mine[...])
    tok = jnp.concatenate([tok_a[zh], tok_c[...], tok_b[zh], tok_d[...]], axis=0)
    grad = jnp.concatenate([grad_a[zh], grad_c[...], grad_b[zh], grad_d[...]], axis=0)
    logits = lax.dot_general(router_t[...], tok, NT, preferred_element_type=f32)
    raised = jnp.exp(logits - jnp.max(logits, axis=1, keepdims=True))
    dispatch = raised / jnp.sum(raised, axis=1, keepdims=True)
    combine = combine_of(logits)
    cgrad = lax.dot_general(slot_out, grad, NT, preferred_element_type=f32)
    dgrad = lax.dot_general(slot_in_grad, tok, NT, preferred_element_type=f32)
    comb_part = combine * (cgrad - jnp.sum(combine * cgrad, axis=0, keepdims=True))
    disp_part = dispatch * (dgrad - jnp.sum(dispatch * dgrad, axis=1, keepdims=True))
    logit_grad = (comb_part + disp_part)[:, :LANES].astype(bf16)
    router_grad[...] = jnp.dot(logit_grad, tok[:LANES], preferred_element_type=f32).astype(bf16)
    left = jnp.concatenate([dispatch[:, :LANES].astype(bf16), logit_grad], axis=0)
    right = jnp.concatenate([slot_in_grad, router_t[...]], axis=0)
    both = lax.dot_general(left, right, TN, preferred_element_type=f32).astype(bf16)
    own_grad[...] = both[:64]
    sent_grad[...] = both[64:]


def fence_kernel(where_am_i, value, out):
    out[...] = value[...]


def swap(value, axis="core"):
    return lax.ppermute(value, axis, [(0, 1), (1, 0)])


def exchange(value, axes):
    return lax.all_to_all(value, axes, split_axis=0, concat_axis=0, tiled=True)


def on_device(tokens, router, up_proj, down_proj, out_grad):
    zh = lax.axis_index("zh").astype(jnp.int32)
    here = jnp.stack([lax.axis_index("core").astype(jnp.int32), zh])
    router_t = router.T.reshape(Y, ZL, XH, D).transpose(1, 0, 2, 3).reshape(SLOTS, D)
    tok_b, grad_b = swap(tokens), swap(out_grad)
    keep, send = call(
        slots_kernel,
        [shaped((SLOTS, WIDE), f32), shaped((SLOTS, WIDE), bf16)],
        here, router_t, tokens, tok_b, out_grad, grad_b,
    )
    (slots,) = call(join_kernel, [shaped((2, SLOTS, D), bf16)], here, keep, swap(send, "zh"))
    got = exchange(slots.reshape(16, 8, D), COLUMN).reshape(LANES, D)
    by_expert, tok_send, grad_send = call(
        middle_kernel,
        [shaped((16, 16, D), bf16), shaped((64, D), bf16), shaped((64, D), bf16)],
        here, got, tokens, out_grad,
    )
    tok_c, grad_c = swap(tok_send, "zh"), swap(grad_send, "zh")
    tok_d, grad_d = swap(tok_c), swap(grad_c)
    got = exchange(by_expert, PLANE).reshape(256, D)
    (mine,) = call(fence_kernel, [shaped((256, D), bf16)], here, got, after=(tok_c,))
    other = swap(mine)
    up_grad, down_grad, keep, send = call(
        expert_kernel,
        [shaped((1, 320, D), bf16), shaped((1, 320, D), bf16), shaped((256, D), f32), shaped((256, D), bf16)],
        here, mine, other, up_proj[0], down_proj[0],
    )
    summed = (keep + swap(send).astype(f32)).astype(bf16).reshape(16, 16, D)
    back = exchange(summed, PLANE).reshape(256, D)
    (by_owner,) = call(return_kernel, [shaped((LANES, D), bf16)], here, back, after=(tok_d, grad_c))
    got = exchange(by_owner.reshape(16, 8, D), COLUMN).reshape(LANES, D)
    (mine,) = call(halves_kernel, [shaped((SLOTS, D), bf16)], here, got, after=(grad_d,))
    other = swap(mine)
    own_grad, sent_grad, router_part = call(
        tokens_kernel,
        [shaped((64, D), bf16), shaped((64, D), bf16), shaped((SLOTS, D), bf16)],
        here, router_t, tokens, tok_b, tok_c, tok_d, out_grad, grad_b, grad_c, grad_d, mine, other,
    )
    got_grad = swap(sent_grad, "zh")
    tokens_grad = jnp.where(zh == 0, jnp.stack([own_grad, got_grad]), jnp.stack([got_grad, own_grad]))
    part = exchange(router_part.reshape(32, 2, D), PLANE_CORES).astype(f32).sum(axis=0).astype(bf16)
    whole = exchange(jnp.broadcast_to(part, (16, 2, D)), COLUMN).astype(f32).sum(axis=0).astype(bf16)
    full = exchange(jnp.broadcast_to(whole, (32, 2, D)), PLANE_CORES).reshape(ZL, Y, XH, D)
    router_grad = full.transpose(1, 0, 2, 3).reshape(SLOTS, D).T.astype(f32)
    return tokens_grad, router_grad, up_grad, down_grad


def solution(mesh):
    fine = Mesh(mesh.devices.reshape(2, 2, Y, ZL, XH, 2), ("zh", "core", "y", "zl", "xh", "xl"))
    rows = P(EVERY_GROUP, ("zh", "core"), None)
    return jax.shard_map(
        on_device,
        mesh=fine,
        in_specs=(rows, P(), rows, rows, rows),
        out_specs=(rows, P(), rows, rows),
        check_vma=False,
    )
```

time: 205 us -> 241 us (1.18)
  the two profiles are of different devices: /device:TPU:32 before, /device:TPU:1 now
where the time goes in v2:
time: 241 us; the launch traced here: 240 us
  starting transfers between devices  122 us (51%)
  waiting for transfers between devices  49.3 us (20%)
  blocking collectives  47.9 us (20%)
  Pallas kernels  11.3 us (5%)
  local copies, waits for them, and re-layouts  6.43 us (3%)
    ppermute x11, starting transfers between devices, swap(): return lax.ppermute(value, axis, [(0, 1), (1, 0)])  88.5 us
    all_to_all x2, blocking collectives, exchange(): return lax.all_to_all(value, axes, split_axis=0, concat_axis=0, tiled=True)  47.9 us
    ppermute x11, waiting for transfers between devices, swap(): return lax.ppermute(value, axis, [(0, 1), (1, 0)])  37.9 us
    all_to_all x5, starting transfers between devices, exchange(): return lax.all_to_all(value, axes, split_axis=0, concat_axis=0, tiled=True)  33.3 us
    all_to_all x5, waiting for transfers between devices, exchange(): return lax.all_to_all(value, axes, split_axis=0, concat_axis=0, tiled=True)  11.4 us
    pallas_call x8, Pallas kernels, call(): pl.pallas_call(body, out_shape=outs, in_specs=[SMEM] + [VMEM] * (len(oper...  11.3 us
  transfers between devices with their start and end apart: 16, of which 10 were waited for; matrix products, arithmetic and copies ran while one was open for 1% of the time, Pallas kernels for 0%

profile of v2, /device:TPU:1, one launch (start us, length us, event | category | flops | bytes accessed | tf_op | source)
XLA Modules:
  0.0 239.7 jit_solution(7078742983670415422)
XLA Ops:
  0.6 8.8 %collective-permute-start = (bf16[2,64,1280]{2,1,0:T(8,128)(2,1)}, bf16[2,64,1280]{2,1,0:T(8,128)(2,1)S(1)}, u32[]{:S(2)}, u32[]{:S(2)}) collective-permute-start(bf16[2,64,1280]{2,1,0:T(8,128)(2,1)} %tok_a.5), channel_id=1, source_target_pairs={{0,128},{128,0},{1,129},{129,1},{2,130},{130,2},{3,131},{131,3},{4... | collective-permute-start | bytes 983048 | tf_op jit(solution)/shard_map/ppermute | solution.py:173
  9.4 1.9 collective-permute-start.1
  11.4 1.0 reshape.44
  12.3 0.1 copy.20
  12.6 0.5 collective-permute-done.1.grad_b
  13.2 1.0 copy-done
  14.1 1.0 copy-done.2
  15.1 1.7 shard_map.84
  16.8 10.1 %collective-permute-start.2 = (bf16[64,1408]{1,0:T(8,128)(2,1)S(1)}, bf16[64,1408]{1,0:T(8,128)(2,1)S(1)}, u32[]{:S(2)}, u32[]{:S(2)}) collective-permute-start(bf16[64,1408]{1,0:T(8,128)(2,1)S(1)} %get-tuple-element.17), channel_id=1, source_target_pairs={{0,256},{256,0},{1,257},{257,1},{2,258},{258,2},{3,259},{259,3},{4... | collective-permute-start | bytes 540680 | tf_op jit(solution)/shard_map/ppermute | solution.py:173
  26.9 6.5 %collective-permute-done.2.got = bf16[64,1408]{1,0:T(8,128)(2,1)S(1)} collective-permute-done((bf16[64,1408]{1,0:T(8,128)(2,1)S(1)}, bf16[64,1408]{1,0:T(8,128)(2,1)S(1)}, u32[]{:S(2)}, u32[]{:S(2)}) %collective-permute-start.2) | collective-permute-done | bytes 180256 | tf_op jit(solution)/shard_map/ppermute | solution.py:173
  33.5 0.8 shard_map.85
  34.3 32.9 %all_to_all.35 = bf16[16,8,1280]{2,1,0:T(8,128)(2,1)S(1)} all-to-all(bf16[16,8,1280]{2,1,0:T(8,128)(2,1)S(1)} %bitcast.26), channel_id=1, replica_groups=mesh['zh'=2,'core'=2,'y'=4,'zl'=8,'xh'=2,'xl'=2] {'zh','zl'}, dimensions={0} | all-to-all | bytes 655360 | tf_op jit(solution)/shard_map/all_to_all | solution.py:177
  67.2 0.8 shard_map.86
  68.0 0.8 copy-done.6
  68.9 7.2 %all-to-all-start.1 = ((bf16[16,16,1280]{2,1,0:T(8,128)(2,1)}), bf16[16,16,1280]{2,1,0:T(8,128)(2,1)S(1)}, u32[]{:S(2)}, u32[]{:S(2)}) async-start(bf16[16,16,1280]{2,1,0:T(8,128)(2,1)} %copy-done.6), calls=%async_computation.1 | async-start | bytes 1310720 | tf_op jit(solution)/shard_map/all_to_all | solution.py:177
  76.0 12.3 %collective-permute-start.3 = (bf16[64,1280]{1,0:T(8,128)(2,1)S(1)}, bf16[64,1280]{1,0:T(8,128)(2,1)S(1)}, u32[]{:S(2)}, u32[]{:S(2)}) collective-permute-start(bf16[64,1280]{1,0:T(8,128)(2,1)S(1)} %get-tuple-element.18), channel_id=1, source_target_pairs={{0,256},{256,0},{1,257},{257,1},{2,258},{258,2},{3,259},{259,3},{4... | collective-permute-start | bytes 491528 | tf_op jit(solution)/shard_map/ppermute | solution.py:173
  88.3 2.7 %collective-permute-done.3.refs_2_.tok_c = bf16[64,1280]{1,0:T(8,128)(2,1)S(1)} collective-permute-done((bf16[64,1280]{1,0:T(8,128)(2,1)S(1)}, bf16[64,1280]{1,0:T(8,128)(2,1)S(1)}, u32[]{:S(2)}, u32[]{:S(2)}) %collective-permute-start.3) | collective-permute-done | bytes 163872 | tf_op jit(solution)/shard_map/ppermute | solution.py:173
  91.1 0.6 shard_map.87.mine
  91.6 18.2 %collective-permute-start.7 = (bf16[256,1280]{1,0:T(8,128)(2,1)S(1)}, bf16[256,1280]{1,0:T(8,128)(2,1)S(1)}, u32[]{:S(2)}, u32[]{:S(2)}) collective-permute-start(bf16[256,1280]{1,0:T(8,128)(2,1)S(1)} %shard_map.87.mine), channel_id=1, source_target_pairs={{0,128},{128,0},{1,129},{129,1},{2,130},{130,2},{3,131},{131,3},{4... | collective-permute-start | bytes 1966088 | tf_op jit(solution)/shard_map/ppermute | solution.py:173
  109.9 1.7 collective-permute-done.7.other
  111.6 3.5 %shard_map.88 = (bf16[1,320,1280]{2,1,0:T(8,128)(2,1)}, bf16[1,320,1280]{2,1,0:T(8,128)(2,1)}, f32[256,1280]{1,0:T(8,128)S(1)}, bf16[256,1280]{1,0:T(8,128)(2,1)S(1)}) custom-call(s32[2]{0:T(128)S(1)} %pad_add_fusion.where_am_i.refs_0_, bf16[256,1280]{1,0:T(8,128)(2,1)S(1)} %shard_map.87.mine, bf16[256,1280]{1,0:T(8,128)(2,1)S(1)} %collective-permute-done.7.other, ...), custom_call_target="tpu_custom_call" | custom-call | bytes 6553608 | tf_op jit(solution)/shard_map/pallas_call | solution.py:31
  115.1 2.3 collective-permute-start.8
  117.4 1.7 collective-permute-done.8
  119.1 1.0 add_convert_fusion
  120.0 6.6 %all-to-all-start.2 = ((bf16[16,16,1280]{2,1,0:T(8,128)(2,1)}), bf16[16,16,1280]{2,1,0:T(8,128)(2,1)S(1)}, u32[]{:S(2)}, u32[]{:S(2)}) async-start(bf16[16,16,1280]{2,1,0:T(8,128)(2,1)} %bitcast.9), calls=%async_computation.2 | async-start | bytes 1310720 | tf_op jit(solution)/shard_map/all_to_all | solution.py:177
  126.7 8.8 %collective-permute-start.5 = (bf16[64,1280]{1,0:T(8,128)(2,1)S(1)}, bf16[64,1280]{1,0:T(8,128)(2,1)S(1)}, u32[]{:S(2)}, u32[]{:S(2)}) collective-permute-start(bf16[64,1280]{1,0:T(8,128)(2,1)S(1)} %get-tuple-element.19), channel_id=1, source_target_pairs={{0,256},{256,0},{1,257},{257,1},{2,258},{258,2},{3,259},{259,3},{4... | collective-permute-start | bytes 491528 | tf_op jit(solution)/shard_map/ppermute | solution.py:173
  135.5 2.8 %collective-permute-start.4 = (bf16[64,1280]{1,0:T(8,128)(2,1)S(1)}, bf16[64,1280]{1,0:T(8,128)(2,1)S(1)}, u32[]{:S(2)}, u32[]{:S(2)}) collective-permute-start(bf16[64,1280]{1,0:T(8,128)(2,1)S(1)} %collective-permute-done.3.refs_2_.tok_c), channel_id=1, source_target_pairs={{0,128},{128,0},{1,129},{129,1},{2,130},{130,2},{3,131},{131,3},{4... | collective-permute-start | bytes 491528 | tf_op jit(solution)/shard_map/ppermute | solution.py:173
  138.3 15.4 %collective-permute-done.5.refs_3_.grad_c = bf16[64,1280]{1,0:T(8,128)(2,1)S(1)} collective-permute-done((bf16[64,1280]{1,0:T(8,128)(2,1)S(1)}, bf16[64,1280]{1,0:T(8,128)(2,1)S(1)}, u32[]{:S(2)}, u32[]{:S(2)}) %collective-permute-start.5) | collective-permute-done | bytes 163872 | tf_op jit(solution)/shard_map/ppermute | solution.py:173
  153.7 1.5 shard_map.89
  155.2 7.6 %all-to-all-start.3 = ((bf16[16,8,1280]{2,1,0:T(8,128)(2,1)}), bf16[16,8,1280]{2,1,0:T(8,128)(2,1)S(1)}, u32[]{:S(2)}, u32[]{:S(2)}) async-start(bf16[16,8,1280]{2,1,0:T(8,128)(2,1)} %bitcast.11), calls=%async_computation.3 | async-start | bytes 655360 | tf_op jit(solution)/shard_map/all_to_all | solution.py:177
  162.8 2.7 %collective-permute-start.6 = (bf16[64,1280]{1,0:T(8,128)(2,1)S(1)}, bf16[64,1280]{1,0:T(8,128)(2,1)S(1)}, u32[]{:S(2)}, u32[]{:S(2)}) collective-permute-start(bf16[64,1280]{1,0:T(8,128)(2,1)S(1)} %collective-permute-done.5.refs_3_.grad_c), channel_id=1, source_target_pairs={{0,128},{128,0},{1,129},{129,1},{2,130},{130,2},{3,131},{131,3},{4... | collective-permute-start | bytes 491528 | tf_op jit(solution)/shard_map/ppermute | solution.py:173
  165.5 1.0 collective-permute-done.6.refs_2_.grad_d
  166.5 11.4 %all-to-all-done.3 = bf16[16,8,1280]{2,1,0:T(8,128)(2,1)S(1)} async-done(((bf16[16,8,1280]{2,1,0:T(8,128)(2,1)}), bf16[16,8,1280]{2,1,0:T(8,128)(2,1)S(1)}, u32[]{:S(2)}, u32[]{:S(2)}) %all-to-all-start.3) | async-done | bytes 327712 | tf_op jit(solution)/shard_map/all_to_all | solution.py:177
  177.9 0.6 shard_map.90.mine
  178.5 8.7 %collective-permute-start.9 = (bf16[64,1280]{1,0:T(8,128)(2,1)S(1)}, bf16[64,1280]{1,0:T(8,128)(2,1)S(1)}, u32[]{:S(2)}, u32[]{:S(2)}) collective-permute-start(bf16[64,1280]{1,0:T(8,128)(2,1)S(1)} %shard_map.90.mine), channel_id=1, source_target_pairs={{0,128},{128,0},{1,129},{129,1},{2,130},{130,2},{3,131},{131,3},{4... | collective-permute-start | bytes 491528 | tf_op jit(solution)/shard_map/ppermute | solution.py:173
  187.2 1.0 collective-permute-done.9.other
  188.2 1.8 shard_map.91
  190.1 15.0 %all_to_all.36 = bf16[32,2,1280]{2,1,0:T(2,128)(2,1)S(1)} all-to-all(bf16[32,2,1280]{2,1,0:T(2,128)(2,1)S(1)} %reshape.53), channel_id=1, replica_groups=mesh['zh'=2,'core'=2,'y'=4,'zl'=8,'xh'=2,'xl'=2] {'core','y','xh','xl'}, dimensions={0} | all-to-all | bytes 327680 | tf_op jit(solution)/shard_map/all_to_all | solution.py:177
  205.0 0.2 reduce_sum.24
  205.2 0.7 broadcast_in_dim.6
  205.9 5.7 %all-to-all-start.5 = ((bf16[16,2,1280]{2,1,0:T(2,128)(2,1)}), bf16[16,2,1280]{2,1,0:T(2,128)(2,1)S(1)}, u32[]{:S(2)}, u32[]{:S(2)}) async-start(bf16[16,2,1280]{2,1,0:T(2,128)(2,1)} %broadcast_in_dim.6), calls=%async_computation.5 | async-start | bytes 163840 | tf_op jit(solution)/shard_map/all_to_all | solution.py:177
  211.6 12.0 %collective-permute-start.10 = (bf16[64,1280]{1,0:T(8,128)(2,1)S(1)}, bf16[64,1280]{1,0:T(8,128)(2,1)S(1)}, u32[]{:S(2)}, u32[]{:S(2)}) collective-permute-start(bf16[64,1280]{1,0:T(8,128)(2,1)S(1)} %get-tuple-element.24), channel_id=1, source_target_pairs={{0,256},{256,0},{1,257},{257,1},{2,258},{258,2},{3,259},{259,3},{4... | collective-permute-start | bytes 491528 | tf_op jit(solution)/shard_map/ppermute | solution.py:173
  223.7 0.8 broadcast_in_dim.7
  224.4 6.2 %all-to-all-start.6 = ((bf16[32,2,1280]{2,1,0:T(2,128)(2,1)}), bf16[32,2,1280]{2,1,0:T(2,128)(2,1)S(1)}, u32[]{:S(2)}, u32[]{:S(2)}) async-start(bf16[32,2,1280]{2,1,0:T(2,128)(2,1)} %broadcast_in_dim.7), calls=%async_computation.6 | async-start | bytes 327680 | tf_op jit(solution)/shard_map/all_to_all | solution.py:177
  230.6 7.2 %collective-permute-done.10 = bf16[64,1280]{1,0:T(8,128)(2,1)S(1)} collective-permute-done((bf16[64,1280]{1,0:T(8,128)(2,1)S(1)}, bf16[64,1280]{1,0:T(8,128)(2,1)S(1)}, u32[]{:S(2)}, u32[]{:S(2)}) %collective-permute-start.10) | collective-permute-done | bytes 163872 | tf_op jit(solution)/shard_map/ppermute | solution.py:173
  237.9 0.8 maximum_select_fusion
  238.6 0.1 convert_bitcast_fusion
  238.8 0.9 reshape.54
  (22 shorter events, 0.4 us)
Async XLA Ops:
  0.6 12.0 %collective-permute-start = (bf16[2,64,1280]{2,1,0:T(8,128)(2,1)}, bf16[2,64,1280]{2,1,0:T(8,128)(2,1)S(1)}, u32[]{:S(2)}, u32[]{:S(2)}) collective-permute-start(bf16[2,64,1280]{2,1,0:T(8,128)(2,1)} %tok_a.5), channel_id=1, source_target_pairs={{0,128},{128,0},{1,129},{129,1},{2,130},{130,2},{3,131},{131,3},{4... | collective-permute-start | bytes 983048 | tf_op jit(solution)/shard_map/ppermute | solution.py:173
  9.4 3.7 %collective-permute-start.1 = (bf16[2,64,1280]{2,1,0:T(8,128)(2,1)}, bf16[2,64,1280]{2,1,0:T(8,128)(2,1)S(1)}, u32[]{:S(2)}, u32[]{:S(2)}) collective-permute-start(bf16[2,64,1280]{2,1,0:T(8,128)(2,1)} %grad_a.5), channel_id=1, source_target_pairs={{0,128},{128,0},{1,129},{129,1},{2,130},{130,2},{3,131},{131,3},{4... | collective-permute-start | bytes 983048 | tf_op jit(solution)/shard_map/ppermute | solution.py:173
  13.2 1.0 copy-start
  14.1 1.0 copy-start.2
  15.1 52.1 %copy-start.1 = (bf16[2,64,1280]{2,1,0:T(8,128)(2,1)S(1)}, bf16[2,64,1280]{2,1,0:T(8,128)(2,1)}, u32[]{:S(2)}) copy-start(bf16[2,64,1280]{2,1,0:T(8,128)(2,1)} %tok_a.5) | copy-start | bytes 983044
  15.1 52.1 %copy-start.3 = (bf16[2,64,1280]{2,1,0:T(8,128)(2,1)S(1)}, bf16[2,64,1280]{2,1,0:T(8,128)(2,1)}, u32[]{:S(2)}) copy-start(bf16[2,64,1280]{2,1,0:T(8,128)(2,1)} %grad_a.5) | copy-start | bytes 983044
  16.8 16.6 %collective-permute-start.2 = (bf16[64,1408]{1,0:T(8,128)(2,1)S(1)}, bf16[64,1408]{1,0:T(8,128)(2,1)S(1)}, u32[]{:S(2)}, u32[]{:S(2)}) collective-permute-start(bf16[64,1408]{1,0:T(8,128)(2,1)S(1)} %get-tuple-element.17), channel_id=1, source_target_pairs={{0,256},{256,0},{1,257},{257,1},{2,258},{258,2},{3,259},{259,3},{4... | collective-permute-start | bytes 540680 | tf_op jit(solution)/shard_map/ppermute | solution.py:173
  68.0 0.8 copy-start.6
  68.9 42.7 %copy-start.4 = (bf16[1,320,1280]{2,1,0:T(8,128)(2,1)S(1)}, bf16[1,320,1280]{2,1,0:T(8,128)(2,1)}, u32[]{:S(2)}) copy-start(bf16[1,320,1280]{2,1,0:T(8,128)(2,1)} %param.7) | copy-start | bytes 2457604
  68.9 22.2 %all-to-all-start.1 = ((bf16[16,16,1280]{2,1,0:T(8,128)(2,1)}), bf16[16,16,1280]{2,1,0:T(8,128)(2,1)S(1)}, u32[]{:S(2)}, u32[]{:S(2)}) async-start(bf16[16,16,1280]{2,1,0:T(8,128)(2,1)} %copy-done.6), calls=%async_computation.1 | async-start | bytes 1310720 | tf_op jit(solution)/shard_map/all_to_all | solution.py:177
  76.0 15.0 %collective-permute-start.3 = (bf16[64,1280]{1,0:T(8,128)(2,1)S(1)}, bf16[64,1280]{1,0:T(8,128)(2,1)S(1)}, u32[]{:S(2)}, u32[]{:S(2)}) collective-permute-start(bf16[64,1280]{1,0:T(8,128)(2,1)S(1)} %get-tuple-element.18), channel_id=1, source_target_pairs={{0,256},{256,0},{1,257},{257,1},{2,258},{258,2},{3,259},{259,3},{4... | collective-permute-start | bytes 491528 | tf_op jit(solution)/shard_map/ppermute | solution.py:173
  91.1 20.6 %copy-start.5 = (bf16[1,320,1280]{2,1,0:T(8,128)(2,1)S(1)}, bf16[1,320,1280]{2,1,0:T(8,128)(2,1)}, u32[]{:S(2)}) copy-start(bf16[1,320,1280]{2,1,0:T(8,128)(2,1)} %param.8) | copy-start | bytes 2457604
  91.6 20.0 %collective-permute-start.7 = (bf16[256,1280]{1,0:T(8,128)(2,1)S(1)}, bf16[256,1280]{1,0:T(8,128)(2,1)S(1)}, u32[]{:S(2)}, u32[]{:S(2)}) collective-permute-start(bf16[256,1280]{1,0:T(8,128)(2,1)S(1)} %shard_map.87.mine), channel_id=1, source_target_pairs={{0,128},{128,0},{1,129},{129,1},{2,130},{130,2},{3,131},{131,3},{4... | collective-permute-start | bytes 1966088 | tf_op jit(solution)/shard_map/ppermute | solution.py:173
  115.1 4.0 %collective-permute-start.8 = (bf16[256,1280]{1,0:T(8,128)(2,1)S(1)}, bf16[256,1280]{1,0:T(8,128)(2,1)S(1)}, u32[]{:S(2)}, u32[]{:S(2)}) collective-permute-start(bf16[256,1280]{1,0:T(8,128)(2,1)S(1)} %get-tuple-element.22), channel_id=1, source_target_pairs={{0,128},{128,0},{1,129},{129,1},{2,130},{130,2},{3,131},{131,3},{4... | collective-permute-start | bytes 1966088 | tf_op jit(solution)/shard_map/ppermute | solution.py:173
  120.0 33.6 %all-to-all-start.2 = ((bf16[16,16,1280]{2,1,0:T(8,128)(2,1)}), bf16[16,16,1280]{2,1,0:T(8,128)(2,1)S(1)}, u32[]{:S(2)}, u32[]{:S(2)}) async-start(bf16[16,16,1280]{2,1,0:T(8,128)(2,1)} %bitcast.9), calls=%async_computation.2 | async-start | bytes 1310720 | tf_op jit(solution)/shard_map/all_to_all | solution.py:177
  126.7 27.0 %collective-permute-start.5 = (bf16[64,1280]{1,0:T(8,128)(2,1)S(1)}, bf16[64,1280]{1,0:T(8,128)(2,1)S(1)}, u32[]{:S(2)}, u32[]{:S(2)}) collective-permute-start(bf16[64,1280]{1,0:T(8,128)(2,1)S(1)} %get-tuple-element.19), channel_id=1, source_target_pairs={{0,256},{256,0},{1,257},{257,1},{2,258},{258,2},{3,259},{259,3},{4... | collective-permute-start | bytes 491528 | tf_op jit(solution)/shard_map/ppermute | solution.py:173
  135.5 18.2 %collective-permute-start.4 = (bf16[64,1280]{1,0:T(8,128)(2,1)S(1)}, bf16[64,1280]{1,0:T(8,128)(2,1)S(1)}, u32[]{:S(2)}, u32[]{:S(2)}) collective-permute-start(bf16[64,1280]{1,0:T(8,128)(2,1)S(1)} %collective-permute-done.3.refs_2_.tok_c), channel_id=1, source_target_pairs={{0,128},{128,0},{1,129},{129,1},{2,130},{130,2},{3,131},{131,3},{4... | collective-permute-start | bytes 491528 | tf_op jit(solution)/shard_map/ppermute | solution.py:173
  155.2 22.7 %all-to-all-start.3 = ((bf16[16,8,1280]{2,1,0:T(8,128)(2,1)}), bf16[16,8,1280]{2,1,0:T(8,128)(2,1)S(1)}, u32[]{:S(2)}, u32[]{:S(2)}) async-start(bf16[16,8,1280]{2,1,0:T(8,128)(2,1)} %bitcast.11), calls=%async_computation.3 | async-start | bytes 655360 | tf_op jit(solution)/shard_map/all_to_all | solution.py:177
  162.8 3.7 %collective-permute-start.6 = (bf16[64,1280]{1,0:T(8,128)(2,1)S(1)}, bf16[64,1280]{1,0:T(8,128)(2,1)S(1)}, u32[]{:S(2)}, u32[]{:S(2)}) collective-permute-start(bf16[64,1280]{1,0:T(8,128)(2,1)S(1)} %collective-permute-done.5.refs_3_.grad_c), channel_id=1, source_target_pairs={{0,128},{128,0},{1,129},{129,1},{2,130},{130,2},{3,131},{131,3},{4... | collective-permute-start | bytes 491528 | tf_op jit(solution)/shard_map/ppermute | solution.py:173
  178.5 9.7 %collective-permute-start.9 = (bf16[64,1280]{1,0:T(8,128)(2,1)S(1)}, bf16[64,1280]{1,0:T(8,128)(2,1)S(1)}, u32[]{:S(2)}, u32[]{:S(2)}) collective-permute-start(bf16[64,1280]{1,0:T(8,128)(2,1)S(1)} %shard_map.90.mine), channel_id=1, source_target_pairs={{0,128},{128,0},{1,129},{129,1},{2,130},{130,2},{3,131},{131,3},{4... | collective-permute-start | bytes 491528 | tf_op jit(solution)/shard_map/ppermute | solution.py:173
  205.9 17.7 %all-to-all-start.5 = ((bf16[16,2,1280]{2,1,0:T(2,128)(2,1)}), bf16[16,2,1280]{2,1,0:T(2,128)(2,1)S(1)}, u32[]{:S(2)}, u32[]{:S(2)}) async-start(bf16[16,2,1280]{2,1,0:T(2,128)(2,1)} %broadcast_in_dim.6), calls=%async_computation.5 | async-start | bytes 163840 | tf_op jit(solution)/shard_map/all_to_all | solution.py:177
  211.6 26.3 %collective-permute-start.10 = (bf16[64,1280]{1,0:T(8,128)(2,1)S(1)}, bf16[64,1280]{1,0:T(8,128)(2,1)S(1)}, u32[]{:S(2)}, u32[]{:S(2)}) collective-permute-start(bf16[64,1280]{1,0:T(8,128)(2,1)S(1)} %get-tuple-element.24), channel_id=1, source_target_pairs={{0,256},{256,0},{1,257},{257,1},{2,258},{258,2},{3,259},{259,3},{4... | collective-permute-start | bytes 491528 | tf_op jit(solution)/shard_map/ppermute | solution.py:173
  224.4 14.2 %all-to-all-start.6 = ((bf16[32,2,1280]{2,1,0:T(2,128)(2,1)}), bf16[32,2,1280]{2,1,0:T(2,128)(2,1)S(1)}, u32[]{:S(2)}, u32[]{:S(2)}) async-start(bf16[32,2,1280]{2,1,0:T(2,128)(2,1)} %broadcast_in_dim.7), calls=%async_computation.6 | async-start | bytes 327680 | tf_op jit(solution)/shard_map/all_to_all | solution.py:177

commit v3 on v1

v3 whole, which is shorter than its diff:
```python
import jax
import jax.numpy as jnp
from jax import lax
from jax.experimental import pallas as pl
from jax.experimental.pallas import tpu as pltpu
from jax.sharding import Mesh, PartitionSpec as P

D = 1280
LANES = 128
WIDE = D + LANES
SLOTS = 64
Y, ZL, XH = 4, 8, 2
PLANE = ("y", "xh", "xl")
PLANE_CORES = ("core", "y", "xh", "xl")
COLUMN = ("zh", "zl")
EVERY_GROUP = ("y", "zl", "xh", "xl")
bf16, f32 = jnp.bfloat16, jnp.float32
NT = (((1,), (1,)), ((), ()))
TN = (((0,), (0,)), ((), ()))
SMEM = pl.BlockSpec(memory_space=pltpu.SMEM)
VMEM = pl.BlockSpec(memory_space=pltpu.VMEM)
ANY = pl.BlockSpec(memory_space=pl.ANY)
HBM = pl.BlockSpec(memory_space=pltpu.HBM)


def call(kernel, outs, *operands, after=()):
    body = kernel
    if after:
        first, last = len(operands), len(operands) + len(after)
        body = lambda *refs: kernel(*refs[:first], *refs[last:])
    bytes_accessed = sum(a.size * a.dtype.itemsize for a in list(operands) + list(outs))
    return pl.pallas_call(
        body,
        out_shape=outs,
        in_specs=[SMEM] + [VMEM] * (len(operands) - 1) + [ANY] * len(after),
        out_specs=[VMEM] * len(outs),
        compiler_params=pltpu.CompilerParams(vmem_limit_bytes=20 * 1024 * 1024),
        cost_estimate=pl.CostEstimate(flops=0, bytes_accessed=bytes_accessed, transcendentals=0),
    )(*operands, *after)


def shaped(shape, dtype):
    return jax.ShapeDtypeStruct(shape, dtype)


def pieces(value):
    first = value.astype(bf16).astype(f32)
    second = (value - first).astype(bf16).astype(f32)
    third = (value - first - second).astype(bf16).astype(f32)
    return [first, second, third]


def lanes_of(columns):
    rows = columns[0].shape[0]
    lane = lax.broadcasted_iota(jnp.int32, (rows, LANES), 1)
    packed = jnp.zeros((rows, LANES), f32)
    for k, column in enumerate(columns):
        packed = jnp.where(lane == k, column, packed)
    return packed


def three(stats, first):
    return stats[:, first : first + 1] + stats[:, first + 1 : first + 2] + stats[:, first + 2 : first + 3]


def combine_of(logits):
    raised = jnp.exp(logits - jnp.max(logits, axis=0, keepdims=True))
    return raised / jnp.sum(raised, axis=0, keepdims=True)


def slot_order(transpose=False):
    own = lax.broadcasted_iota(jnp.int32, (SLOTS, SLOTS), 1 if transpose else 0)
    expert = lax.broadcasted_iota(jnp.int32, (SLOTS, SLOTS), 0 if transpose else 1)
    return jnp.where(expert == ((own >> 1) & 3) * 16 + (own >> 3) * 2 + (own & 1), 1.0, 0.0).astype(bf16)


def merged(on_first, halves):
    tops = [three(h[:, D:], 0) for h in halves]
    totals = [three(h[:, D:], 3) for h in halves]
    top = jnp.maximum(tops[0], tops[1])
    parts = [totals[h] * jnp.exp(tops[h] - top) for h in range(2)]
    total = parts[0] + parts[1]
    shares = [jnp.where(on_first, part / total, 1.0) for part in parts]
    return halves[0][:, :D] * shares[0] + halves[1][:, :D] * shares[1], top, total


def slots_kernel(where_am_i, router_rows, tok_a, tok_b, grad_a, grad_b, out, router_t):
    core = where_am_i[0]
    router_t[...] = jnp.dot(slot_order(), router_rows[...], preferred_element_type=f32).astype(bf16)
    tok = jnp.concatenate([tok_a[core], tok_b[core]], axis=0)
    grad = jnp.concatenate([grad_a[core], grad_b[core]], axis=0)
    logits = lax.dot_general(router_t[...], tok, NT, preferred_element_type=f32)
    top = jnp.max(logits, axis=1, keepdims=True)
    raised = jnp.exp(logits - top)
    total = jnp.sum(raised, axis=1, keepdims=True)
    stats = lanes_of(pieces(top) + pieces(total))
    part_in = jnp.dot((raised / total).astype(bf16), tok, preferred_element_type=f32)
    part_grad = jnp.dot(combine_of(logits).astype(bf16), grad, preferred_element_type=f32)
    for zl in range(ZL):
        at = slice(zl * 8, zl * 8 + 8)
        for zh in range(2):
            place = zh * ZL + zl
            out[place, :, :D] = jnp.concatenate([part_in[at], part_grad[at]], axis=0).astype(bf16)
            out[place, :, D:] = jnp.concatenate([stats[at], stats[at]], axis=0).astype(bf16)


def middle_kernel(where_am_i, got, out, kept, stats_out):
    halves = [got[h * ZL : (h + 1) * ZL].reshape(LANES, WIDE).astype(f32) for h in range(2)]
    weighed = (lax.broadcasted_iota(jnp.int32, (LANES, 1), 0) & 8) == 0
    summed, top, total = merged(weighed, halves)
    kept[...] = summed
    stats_out[...] = lanes_of([top, total])
    row = lax.broadcasted_iota(jnp.int32, (LANES, LANES), 0)
    col = lax.broadcasted_iota(jnp.int32, (LANES, LANES), 1)
    source = (row & 7) * 16 + (row & 8) + (row >> 4)
    pick = jnp.where(col == source, 1.0, 0.0).astype(bf16)
    sorted_rows = jnp.dot(pick, summed.astype(bf16), preferred_element_type=f32).astype(bf16)
    for yx in range(Y * XH):
        for xl in range(2):
            out[2 * yx + xl] = sorted_rows[yx * 16 : yx * 16 + 16]


def array_rows(ref, array):
    return ref[:, array].astype(f32).reshape(LANES, D).astype(bf16)


def expert_kernel(where_am_i, rows, up_own, up_other, down_own, down_other, out, pre_grads, hiddens):
    slot_in, slot_grad = array_rows(rows, 0), array_rows(rows, 1)
    in_grad = jnp.zeros((LANES, D), f32)
    slot_out = jnp.zeros((LANES, D), f32)
    for j, (w_up, w_down) in enumerate(((up_own, down_own), (up_other, down_other))):
        pre_act = lax.dot_general(w_up[...], slot_in, NT, preferred_element_type=f32)
        hid_grad = lax.dot_general(w_down[...], slot_grad, NT, preferred_element_type=f32)
        cdf = 0.5 * (1.0 + lax.erf(pre_act * 0.7071067811865476))
        density = jnp.exp(pre_act * pre_act * -0.5) * 0.3989422804014327
        hiddens[j] = (pre_act * cdf).astype(bf16)
        pre_grads[j] = (hid_grad * (cdf + pre_act * density)).astype(bf16)
        in_grad += lax.dot_general(pre_grads[j], w_up[...], TN, preferred_element_type=f32)
        slot_out += lax.dot_general(hiddens[j], w_down[...], TN, preferred_element_type=f32)
    out[:, 0] = in_grad.reshape(16, 8, D).astype(bf16)
    out[:, 1] = slot_out.reshape(16, 8, D).astype(bf16)


def weights_kernel(where_am_i, pre_grads, hiddens, rows, keep, send):
    slot_in, slot_grad = array_rows(rows, 0), array_rows(rows, 1)
    for j, out in enumerate((keep, send)):
        out[0] = jnp.dot(pre_grads[j], slot_in, preferred_element_type=f32).astype(bf16)
        out[1] = jnp.dot(hiddens[j], slot_grad, preferred_element_type=f32).astype(bf16)


def return_kernel(where_am_i, got, kept, stats, out):
    row = lax.broadcasted_iota(jnp.int32, (LANES, 2 * LANES), 0)
    col = lax.broadcasted_iota(jnp.int32, (LANES, 2 * LANES), 1)
    source = (row & 7) * 32 + (row & 8) + (row >> 4)
    pick = jnp.where((col & ~16) == source, 1.0, 0.0).astype(bf16)
    summed = jnp.dot(pick, got[...], preferred_element_type=f32).astype(bf16)
    share = jnp.sum(kept[...] * summed.astype(f32), axis=1, keepdims=True)
    top, total = stats[:, 0:1], stats[:, 1:2]
    extra = lanes_of(pieces(share) + pieces(top) + pieces(total)).astype(bf16)
    for zl in range(ZL):
        at = slice(zl * 16, zl * 16 + 16)
        for zh in range(2):
            out[zh * ZL + zl, :, :D] = summed[at]
            out[zh * ZL + zl, :, D:] = extra[at]


def tokens_kernel(
    where_am_i, router_hbm, tok_a, tok_b, grad_a, grad_b, got_hbm, own_grad, sent_grad, router_grad,
    router_t, tok, grad, got, arrived,
):
    core = where_am_i[0]
    own, other = pl.ds(0, 64), pl.ds(64, 64)
    moves = (
        (router_hbm, router_t),
        (tok_a.at[core], tok.at[own]),
        (tok_b.at[core], tok.at[other]),
        (got_hbm, got),
        (grad_a.at[core], grad.at[own]),
        (grad_b.at[core], grad.at[other]),
    )
    copies = [pltpu.make_async_copy(source, target, arrived.at[k]) for k, (source, target) in enumerate(moves)]
    for copy in copies:
        copy.start()
    for copy in copies:
        copy.wait()
    halves = [got[h * ZL : (h + 1) * ZL].astype(f32) for h in range(2)]
    both = halves[0] + halves[1]
    slot_in_grad = both[:, :8, :D].reshape(SLOTS, D).astype(bf16)
    slot_out = both[:, 8:, :D].reshape(SLOTS, D).astype(bf16)
    weighted = three(both[:, :8, D:].reshape(SLOTS, LANES), 0)
    stats = halves[0][:, :8, D:].reshape(SLOTS, LANES)
    top, total = three(stats, 3), three(stats, 6)
    logits = lax.dot_general(router_t[...], tok[...], NT, preferred_element_type=f32)
    dispatch = jnp.exp(logits - top) / total
    combine = combine_of(logits)
    cgrad = lax.dot_general(slot_out, grad[...], NT, preferred_element_type=f32)
    dgrad = lax.dot_general(slot_in_grad, tok[...], NT, preferred_element_type=f32)
    comb_part = combine * (cgrad - jnp.sum(combine * cgrad, axis=0, keepdims=True))
    disp_part = dispatch * (dgrad - weighted)
    logit_grad = (comb_part + disp_part).astype(bf16)
    by_expert = jnp.dot(slot_order(transpose=True), logit_grad, preferred_element_type=f32).astype(bf16)
    router_grad[...] = jnp.dot(by_expert, tok[...], preferred_element_type=f32).astype(bf16)
    left = jnp.concatenate([dispatch.astype(bf16), logit_grad], axis=0)
    right = jnp.concatenate([slot_in_grad, router_t[...]], axis=0)
    all_grad = lax.dot_general(left, right, TN, preferred_element_type=f32).astype(bf16)
    own_grad[...] = all_grad[:64]
    sent_grad[...] = all_grad[64:]


def swap(value):
    return lax.ppermute(value, "core", [(0, 1), (1, 0)])


def exchange(value, axes):
    return lax.all_to_all(value, axes, split_axis=0, concat_axis=0, tiled=True)


def on_device(tokens, router, up_proj, down_proj, out_grad):
    here = lax.axis_index("core").astype(jnp.int32).reshape(1)
    tok_b, grad_b = swap(tokens), swap(out_grad)
    slots, router_t = call(
        slots_kernel,
        [shaped((16, 16, WIDE), bf16), shaped((SLOTS, D), bf16)],
        here, router.T, tokens, tok_b, out_grad, grad_b,
    )
    got = exchange(slots, COLUMN)
    up_other, down_other = swap(up_proj[0]), swap(down_proj[0])
    by_expert, kept, stats = call(
        middle_kernel,
        [shaped((16, 16, D), bf16), shaped((LANES, D), f32), shaped((LANES, LANES), f32)],
        here, got, after=(up_other, down_other),
    )
    rows = exchange(by_expert.reshape(16, 2, 8, D), PLANE)
    done, pre_grads, hiddens = call(
        expert_kernel,
        [shaped((16, 2, 8, D), bf16), shaped((2, 320, LANES), bf16), shaped((2, 320, LANES), bf16)],
        here, rows, up_proj[0], up_other, down_proj[0], down_other,
    )
    back = exchange(done, PLANE).reshape(256, D)
    keep, send = call(
        weights_kernel, [shaped((2, 320, D), bf16), shaped((2, 320, D), bf16)], here, pre_grads, hiddens, rows
    )
    summed = (keep.astype(f32) + swap(send).astype(f32)).astype(bf16)
    (by_owner,) = call(return_kernel, [shaped((16, 16, WIDE), bf16)], here, back, kept, stats)
    got = exchange(by_owner, COLUMN)
    own_grad, sent_grad, router_part = pl.pallas_call(
        tokens_kernel,
        out_shape=[shaped((64, D), bf16), shaped((64, D), bf16), shaped((SLOTS, D), bf16)],
        in_specs=[SMEM] + [HBM] * 6,
        out_specs=[VMEM] * 3,
        scratch_shapes=[
            pltpu.VMEM((SLOTS, D), bf16),
            pltpu.VMEM((LANES, D), bf16),
            pltpu.VMEM((LANES, D), bf16),
            pltpu.VMEM((16, 16, WIDE), bf16),
            pltpu.SemaphoreType.DMA((6,)),
        ],
        compiler_params=pltpu.CompilerParams(vmem_limit_bytes=63 * 1024 * 1024),
    )(here, router_t, tokens, tok_b, out_grad, grad_b, got)
    got_grad = swap(sent_grad)
    own_first = here[0] == 0
    tokens_grad = jnp.where(own_first, jnp.stack([own_grad, got_grad]), jnp.stack([got_grad, own_grad]))
    part = exchange(router_part.reshape(32, 2, D), PLANE_CORES).astype(f32).sum(axis=0).astype(bf16)
    whole = exchange(jnp.broadcast_to(part, (16, 2, D)), COLUMN).astype(f32).sum(axis=0).astype(bf16)
    full = exchange(jnp.broadcast_to(whole, (32, 2, D)), PLANE_CORES).reshape(SLOTS, D)
    return tokens_grad, full.T.astype(f32), summed[:1], summed[1:]


def solution(mesh):
    fine = Mesh(mesh.devices.reshape(2, 2, Y, ZL, XH, 2), ("zh", "core", "y", "zl", "xh", "xl"))
    rows = P(EVERY_GROUP, ("zh", "core"), None)
    return jax.shard_map(
        on_device,
        mesh=fine,
        in_specs=(rows, P(), rows, rows, rows),
        out_specs=(rows, P(), rows, rows),
        check_vma=False,
    )
```

time: 205 us -> 201 us (0.980)
  the two profiles are of different devices: /device:TPU:32 before, /device:TPU:1 now
where the time goes in v3:
time: 201 us; the launch traced here: 200 us
  waiting for transfers between devices  72.7 us (36%)
  starting transfers between devices  72 us (36%)
  blocking collectives  28.7 us (14%)
  Pallas kernels  12 us (6%)
  local copies, waits for them, and re-layouts  10.8 us (5%)
  other arithmetic  3.34 us (2%)
    all_to_all x5, waiting for transfers between devices, exchange(): return lax.all_to_all(value, axes, split_axis=0, concat_axis=0, tiled=True)  68.5 us
    all_to_all x5, starting transfers between devices, exchange(): return lax.all_to_all(value, axes, split_axis=0, concat_axis=0, tiled=True)  50.2 us
    all_to_all x2, blocking collectives, exchange(): return lax.all_to_all(value, axes, split_axis=0, concat_axis=0, tiled=True)  28.7 us
    ppermute x6, starting transfers between devices, swap(): return lax.ppermute(value, 'core', [(0, 1), (1, 0)])  21.8 us
    pallas_call x5, Pallas kernels, call(): pl.pallas_call(body, out_shape=outs, in_specs=[SMEM] + [VMEM] * (len(oper...  8.73 us
    unnamed x22, local copies, waits for them, and re-layouts  5.69 us
    ppermute x6, waiting for transfers between devices, swap(): return lax.ppermute(value, 'core', [(0, 1), (1, 0)])  4.23 us
  transfers between devices with their start and end apart: 11, of which 8 were waited for; matrix products, arithmetic and copies ran while one was open for 4% of the time, Pallas kernels for 3%

profile of v3, /device:TPU:1, one launch (start us, length us, event | category | flops | bytes accessed | tf_op | source)
XLA Modules:
  0.0 200.4 jit_solution(18031500080741774042)
XLA Ops:
  0.6 8.8 %collective-permute-start = (bf16[2,64,1280]{2,1,0:T(8,128)(2,1)}, bf16[2,64,1280]{2,1,0:T(8,128)(2,1)S(1)}, u32[]{:S(2)}, u32[]{:S(2)}) collective-permute-start(bf16[2,64,1280]{2,1,0:T(8,128)(2,1)} %tok_a.3), channel_id=1, source_target_pairs={{0,128},{128,0},{1,129},{129,1},{2,130},{130,2},{3,131},{131,3},{4... | collective-permute-start | bytes 983048 | tf_op jit(solution)/shard_map/ppermute | solution.py:211
  9.4 1.9 collective-permute-start.1
  11.4 0.0 collective-permute-done.tok_b
  11.4 0.0 copy-start.3
  11.4 1.8 collective-permute-done.1.grad_b
  13.2 1.1 copy-done.1
  14.3 1.0 copy-done.2
  15.2 0.9 copy-done.7
  16.1 1.7 shard_map.84
  17.9 0.7 copy-done.6
  18.5 9.5 %all-to-all-start = ((bf16[16,16,1408]{2,1,0:T(8,128)(2,1)}), bf16[16,16,1408]{2,1,0:T(8,128)(2,1)S(1)}, u32[]{:S(2)}, u32[]{:S(2)}) async-start(bf16[16,16,1408]{2,1,0:T(8,128)(2,1)} %get-tuple-element.18), calls=%async_computation | async-start | bytes 1441792 | tf_op jit(solution)/shard_map/all_to_all | solution.py:215
  28.1 2.3 %collective-permute-start.2 = (bf16[320,1280]{1,0:T(8,128)(2,1)}, bf16[320,1280]{1,0:T(8,128)(2,1)S(1)}, u32[]{:S(2)}, u32[]{:S(2)}) collective-permute-start(bf16[320,1280]{1,0:T(8,128)(2,1)} %bitcast.2.up_own), channel_id=1, source_target_pairs={{0,128},{128,0},{1,129},{129,1},{2,130},{130,2},{3,131},{131,3},{4... | collective-permute-start | bytes 2457608 | tf_op jit(solution)/shard_map/ppermute | solution.py:211
  30.4 2.0 collective-permute-start.3
  32.4 0.1 collective-permute-done.2.refs_2_.up_other
  32.6 2.3 %collective-permute-done.3.refs_3_.down_other = bf16[320,1280]{1,0:T(8,128)(2,1)S(1)} collective-permute-done((bf16[320,1280]{1,0:T(8,128)(2,1)}, bf16[320,1280]{1,0:T(8,128)(2,1)S(1)}, u32[]{:S(2)}, u32[]{:S(2)}) %collective-permute-start.3) | collective-permute-done | bytes 819232 | tf_op jit(solution)/shard_map/ppermute | solution.py:211
  34.9 25.1 %all-to-all-done.refs_1_ = bf16[16,16,1408]{2,1,0:T(8,128)(2,1)S(1)} async-done(((bf16[16,16,1408]{2,1,0:T(8,128)(2,1)}), bf16[16,16,1408]{2,1,0:T(8,128)(2,1)S(1)}, u32[]{:S(2)}, u32[]{:S(2)}) %all-to-all-start) | async-done | bytes 720928 | tf_op jit(solution)/shard_map/all_to_all | solution.py:215
  60.0 0.5 shard_map.85
  60.6 16.2 %all_to_all.35.rows = bf16[16,2,8,1280]{3,2,1,0:T(8,128)(2,1)S(1)} all-to-all(bf16[16,2,8,1280]{3,2,1,0:T(8,128)(2,1)S(1)} %bitcast.12), channel_id=1, replica_groups=mesh['zh'=2,'core'=2,'y'=4,'zl'=8,'xh'=2,'xl'=2] {'y','xh','xl'}, dimensions={0} | all-to-all | bytes 1310720 | tf_op jit(solution)/shard_map/all_to_all | solution.py:215
  76.8 3.0 %shard_map.86 = (bf16[16,2,8,1280]{3,2,1,0:T(8,128)(2,1)S(1)}, bf16[2,320,128]{2,1,0:T(8,128)(2,1)S(1)}, bf16[2,320,128]{2,1,0:T(8,128)(2,1)S(1)}) custom-call(s32[1]{0:T(128)} %bitcast.where_am_i.refs_0_, bf16[16,2,8,1280]{3,2,1,0:T(8,128)(2,1)S(1)} %all_to_all.35.rows, bf16[320,1280]{1,0:T(8,128)(2,1)} %bitcast.2.up_own, ...), custom_call_target="tpu_custom_call" | custom-call | bytes 4915204 | tf_op jit(solution)/shard_map/pallas_call | solution.py:32
  79.9 12.5 %all_to_all.36 = bf16[16,2,8,1280]{3,2,1,0:T(8,128)(2,1)S(1)} all-to-all(bf16[16,2,8,1280]{3,2,1,0:T(8,128)(2,1)S(1)} %get-tuple-element.20), channel_id=1, replica_groups=mesh['zh'=2,'core'=2,'y'=4,'zl'=8,'xh'=2,'xl'=2] {'y','xh','xl'}, dimensions={0} | all-to-all | bytes 1310720 | tf_op jit(solution)/shard_map/all_to_all | solution.py:215
  92.3 1.2 shard_map.87
  93.6 16.9 %all-to-all-start.3 = ((bf16[16,16,1408]{2,1,0:T(8,128)(2,1)}), bf16[16,16,1408]{2,1,0:T(8,128)(2,1)S(1)}, u32[]{:S(2)}, u32[]{:S(2)}) async-start(bf16[16,16,1408]{2,1,0:T(8,128)(2,1)} %shard_map.87), calls=%async_computation.3 | async-start | bytes 1441792 | tf_op jit(solution)/shard_map/all_to_all | solution.py:215
  110.5 2.2 %shard_map.89 = (bf16[2,320,1280]{2,1,0:T(8,128)(2,1)S(1)}, bf16[2,320,1280]{2,1,0:T(8,128)(2,1)}) custom-call(s32[1]{0:T(128)} %bitcast.where_am_i.refs_0_, bf16[2,320,128]{2,1,0:T(8,128)(2,1)S(1)} %get-tuple-element.26.pre_grads, bf16[2,320,128]{2,1,0:T(8,128)(2,1)S(1)} %get-tuple-element.27.hiddens, bf16[16,2,8,1280]{3,2,1,0:T(8,128)(2,1)S(1)} %all_to_all.35.rows), custom_call_target="tpu_custom_call" | custom-call | bytes 4259844 | tf_op jit(solution)/shard_map/pallas_call | solution.py:32
  112.7 1.2 copy-done
  113.9 4.6 %collective-permute-start.5 = (bf16[2,320,1280]{2,1,0:T(8,128)(2,1)}, bf16[2,320,1280]{2,1,0:T(8,128)(2,1)}, u32[]{:S(2)}, u32[]{:S(2)}) collective-permute-start(bf16[2,320,1280]{2,1,0:T(8,128)(2,1)} %get-tuple-element.29), channel_id=1, source_target_pairs={{0,128},{128,0},{1,129},{129,1},{2,130},{130,2},{3,131},{131,3},{4... | collective-permute-start | bytes 4915208 | tf_op jit(solution)/shard_map/ppermute | solution.py:211
  118.5 22.5 %all-to-all-done.3.got_hbm = bf16[16,16,1408]{2,1,0:T(8,128)(2,1)S(1)} async-done(((bf16[16,16,1408]{2,1,0:T(8,128)(2,1)}), bf16[16,16,1408]{2,1,0:T(8,128)(2,1)S(1)}, u32[]{:S(2)}, u32[]{:S(2)}) %all-to-all-start.3) | async-done | bytes 720928 | tf_op jit(solution)/shard_map/all_to_all | solution.py:215
  141.0 0.9 copy-done.8
  141.9 3.2 %shard_map.88 = (bf16[64,1280]{1,0:T(8,128)(2,1)}, bf16[64,1280]{1,0:T(8,128)(2,1)}, bf16[64,1280]{1,0:T(8,128)(2,1)}) custom-call(s32[1]{0:T(128)} %bitcast.where_am_i.refs_0_, bf16[64,1280]{1,0:T(8,128)(2,1)} %copy-done.6, bf16[2,64,1280]{2,1,0:T(8,128)(2,1)} %tok_a.3, bf16[2,64,1280]{2,1,0:T(8,128)(2,1)} %copy-done.3, bf16[2,64,1280]{2,1,0:T(8,128)(2,1)} %grad_a.3, ...), custom_call_target="tpu_custom_call" | custom-call | tf_op jit(solution)/shard_map/pallas_call | solution.py:246
  145.1 1.6 reshape.26
  146.8 9.9 %all-to-all-start.4 = ((bf16[32,2,1280]{2,1,0:T(2,128)(2,1)}), bf16[32,2,1280]{2,1,0:T(2,128)(2,1)S(1)}, u32[]{:S(2)}, u32[]{:S(2)}) async-start(bf16[32,2,1280]{2,1,0:T(2,128)(2,1)} %reshape.26), calls=%async_computation.4 | async-start | bytes 327680 | tf_op jit(solution)/shard_map/all_to_all | solution.py:215
  156.7 0.0 collective-permute-done.5
  156.7 0.0 copy-start.10
  156.7 2.3 %add_convert_fusion = bf16[2,320,1280]{2,1,0:T(8,128)(2,1)S(1)} fusion(bf16[2,320,1280]{2,1,0:T(8,128)(2,1)} %collective-permute-done.5, bf16[2,320,1280]{2,1,0:T(8,128)(2,1)} %copy-done), kind=kLoop, calls=%fused_computation | loop fusion | flops 3276800 | bytes 4915200 | tf_op jit(solution)/shard_map/convert_element_type | solution.py:243
  159.1 2.2 %collective-permute-start.4 = (bf16[64,1280]{1,0:T(8,128)(2,1)S(1)}, bf16[64,1280]{1,0:T(8,128)(2,1)S(1)}, u32[]{:S(2)}, u32[]{:S(2)}) collective-permute-start(bf16[64,1280]{1,0:T(8,128)(2,1)S(1)} %copy-done.10), channel_id=1, source_target_pairs={{0,128},{128,0},{1,129},{129,1},{2,130},{130,2},{3,131},{131,3},{4... | collective-permute-start | bytes 491528 | tf_op jit(solution)/shard_map/ppermute | solution.py:211
  161.3 3.3 %all-to-all-done.4 = bf16[32,2,1280]{2,1,0:T(2,128)(2,1)S(1)} async-done(((bf16[32,2,1280]{2,1,0:T(2,128)(2,1)}), bf16[32,2,1280]{2,1,0:T(2,128)(2,1)S(1)}, u32[]{:S(2)}, u32[]{:S(2)}) %all-to-all-start.4) | async-done | bytes 163872 | tf_op jit(solution)/shard_map/all_to_all | solution.py:215
  164.5 0.2 reduce_sum.24
  164.7 0.7 broadcast_in_dim.6
  165.4 7.6 %all-to-all-start.5 = ((bf16[16,2,1280]{2,1,0:T(2,128)(2,1)}), bf16[16,2,1280]{2,1,0:T(2,128)(2,1)S(1)}, u32[]{:S(2)}, u32[]{:S(2)}) async-start(bf16[16,2,1280]{2,1,0:T(2,128)(2,1)} %broadcast_in_dim.6), calls=%async_computation.5 | async-start | bytes 163840 | tf_op jit(solution)/shard_map/all_to_all | solution.py:215
  173.0 0.0 copy-start.9
  173.0 1.3 fusion
  174.3 10.5 %all-to-all-done.5 = bf16[16,2,1280]{2,1,0:T(2,128)(2,1)S(1)} async-done(((bf16[16,2,1280]{2,1,0:T(2,128)(2,1)}), bf16[16,2,1280]{2,1,0:T(2,128)(2,1)S(1)}, u32[]{:S(2)}, u32[]{:S(2)}) %all-to-all-start.5) | async-done | bytes 81952 | tf_op jit(solution)/shard_map/all_to_all | solution.py:215
  184.8 0.1 reduce_sum.25
  184.9 0.8 broadcast_in_dim.7
  185.6 6.2 %all-to-all-start.6 = ((bf16[32,2,1280]{2,1,0:T(2,128)(2,1)}), bf16[32,2,1280]{2,1,0:T(2,128)(2,1)S(1)}, u32[]{:S(2)}, u32[]{:S(2)}) async-start(bf16[32,2,1280]{2,1,0:T(2,128)(2,1)} %broadcast_in_dim.7), calls=%async_computation.6 | async-start | bytes 327680 | tf_op jit(solution)/shard_map/all_to_all | solution.py:215
  191.8 0.0 collective-permute-done.4
  191.8 0.8 maximum_select_fusion
  192.6 7.0 %all-to-all-done.6 = bf16[32,2,1280]{2,1,0:T(2,128)(2,1)S(1)} async-done(((bf16[32,2,1280]{2,1,0:T(2,128)(2,1)}), bf16[32,2,1280]{2,1,0:T(2,128)(2,1)S(1)}, u32[]{:S(2)}, u32[]{:S(2)}) %all-to-all-start.6) | async-done | bytes 163872 | tf_op jit(solution)/shard_map/all_to_all | solution.py:215
  199.6 0.8 reshape.27
  (13 shorter events, 0.0 us)
Async XLA Ops:
  0.6 10.7 %collective-permute-start = (bf16[2,64,1280]{2,1,0:T(8,128)(2,1)}, bf16[2,64,1280]{2,1,0:T(8,128)(2,1)S(1)}, u32[]{:S(2)}, u32[]{:S(2)}) collective-permute-start(bf16[2,64,1280]{2,1,0:T(8,128)(2,1)} %tok_a.3), channel_id=1, source_target_pairs={{0,128},{128,0},{1,129},{129,1},{2,130},{130,2},{3,131},{131,3},{4... | collective-permute-start | bytes 983048 | tf_op jit(solution)/shard_map/ppermute | solution.py:211
  9.4 3.7 %collective-permute-start.1 = (bf16[2,64,1280]{2,1,0:T(8,128)(2,1)}, bf16[2,64,1280]{2,1,0:T(8,128)(2,1)S(1)}, u32[]{:S(2)}, u32[]{:S(2)}) collective-permute-start(bf16[2,64,1280]{2,1,0:T(8,128)(2,1)} %grad_a.3), channel_id=1, source_target_pairs={{0,128},{128,0},{1,129},{129,1},{2,130},{130,2},{3,131},{131,3},{4... | collective-permute-start | bytes 983048 | tf_op jit(solution)/shard_map/ppermute | solution.py:211
  11.4 49.2 %copy-start.3 = (bf16[2,64,1280]{2,1,0:T(8,128)(2,1)}, bf16[2,64,1280]{2,1,0:T(8,128)(2,1)S(1)}, u32[]{:S(2)}) copy-start(bf16[2,64,1280]{2,1,0:T(8,128)(2,1)S(1)} %collective-permute-done.tok_b) | copy-start | bytes 983044
  13.2 47.4 %copy-start.4 = (bf16[2,64,1280]{2,1,0:T(8,128)(2,1)}, bf16[2,64,1280]{2,1,0:T(8,128)(2,1)S(1)}, u32[]{:S(2)}) copy-start(bf16[2,64,1280]{2,1,0:T(8,128)(2,1)S(1)} %collective-permute-done.1.grad_b) | copy-start | bytes 983044
  13.2 1.1 copy-start.1
  14.3 1.0 copy-start.2
  15.2 0.9 copy-start.7
  17.9 0.7 copy-start.6
  18.5 41.5 %all-to-all-start = ((bf16[16,16,1408]{2,1,0:T(8,128)(2,1)}), bf16[16,16,1408]{2,1,0:T(8,128)(2,1)S(1)}, u32[]{:S(2)}, u32[]{:S(2)}) async-start(bf16[16,16,1408]{2,1,0:T(8,128)(2,1)} %get-tuple-element.18), calls=%async_computation | async-start | bytes 1441792 | tf_op jit(solution)/shard_map/all_to_all | solution.py:215
  28.1 4.5 %collective-permute-start.2 = (bf16[320,1280]{1,0:T(8,128)(2,1)}, bf16[320,1280]{1,0:T(8,128)(2,1)S(1)}, u32[]{:S(2)}, u32[]{:S(2)}) collective-permute-start(bf16[320,1280]{1,0:T(8,128)(2,1)} %bitcast.2.up_own), channel_id=1, source_target_pairs={{0,128},{128,0},{1,129},{129,1},{2,130},{130,2},{3,131},{131,3},{4... | collective-permute-start | bytes 2457608 | tf_op jit(solution)/shard_map/ppermute | solution.py:211
  30.4 4.4 %collective-permute-start.3 = (bf16[320,1280]{1,0:T(8,128)(2,1)}, bf16[320,1280]{1,0:T(8,128)(2,1)S(1)}, u32[]{:S(2)}, u32[]{:S(2)}) collective-permute-start(bf16[320,1280]{1,0:T(8,128)(2,1)} %bitcast.10), channel_id=1, source_target_pairs={{0,128},{128,0},{1,129},{129,1},{2,130},{130,2},{3,131},{131,3},{4... | collective-permute-start | bytes 2457608 | tf_op jit(solution)/shard_map/ppermute | solution.py:211
  60.0 16.8 %copy-start.5 = (bf16[1,320,1280]{2,1,0:T(8,128)(2,1)S(1)}, bf16[1,320,1280]{2,1,0:T(8,128)(2,1)}, u32[]{:S(2)}) copy-start(bf16[1,320,1280]{2,1,0:T(8,128)(2,1)} %param.8) | copy-start | bytes 2457604
  93.6 47.4 %all-to-all-start.3 = ((bf16[16,16,1408]{2,1,0:T(8,128)(2,1)}), bf16[16,16,1408]{2,1,0:T(8,128)(2,1)S(1)}, u32[]{:S(2)}, u32[]{:S(2)}) async-start(bf16[16,16,1408]{2,1,0:T(8,128)(2,1)} %shard_map.87), calls=%async_computation.3 | async-start | bytes 1441792 | tf_op jit(solution)/shard_map/all_to_all | solution.py:215
  112.7 1.2 copy-start
  113.9 42.9 %collective-permute-start.5 = (bf16[2,320,1280]{2,1,0:T(8,128)(2,1)}, bf16[2,320,1280]{2,1,0:T(8,128)(2,1)}, u32[]{:S(2)}, u32[]{:S(2)}) collective-permute-start(bf16[2,320,1280]{2,1,0:T(8,128)(2,1)} %get-tuple-element.29), channel_id=1, source_target_pairs={{0,128},{128,0},{1,129},{129,1},{2,130},{130,2},{3,131},{131,3},{4... | collective-permute-start | bytes 4915208 | tf_op jit(solution)/shard_map/ppermute | solution.py:211
  141.0 0.9 copy-start.8
  146.8 17.8 %all-to-all-start.4 = ((bf16[32,2,1280]{2,1,0:T(2,128)(2,1)}), bf16[32,2,1280]{2,1,0:T(2,128)(2,1)S(1)}, u32[]{:S(2)}, u32[]{:S(2)}) async-start(bf16[32,2,1280]{2,1,0:T(2,128)(2,1)} %reshape.26), calls=%async_computation.4 | async-start | bytes 327680 | tf_op jit(solution)/shard_map/all_to_all | solution.py:215
  156.7 2.4 %copy-start.10 = (bf16[64,1280]{1,0:T(8,128)(2,1)S(1)}, bf16[64,1280]{1,0:T(8,128)(2,1)}, u32[]{:S(2)}) copy-start(bf16[64,1280]{1,0:T(8,128)(2,1)} %get-tuple-element.24) | copy-start | bytes 491524
  159.1 32.7 %collective-permute-start.4 = (bf16[64,1280]{1,0:T(8,128)(2,1)S(1)}, bf16[64,1280]{1,0:T(8,128)(2,1)S(1)}, u32[]{:S(2)}, u32[]{:S(2)}) collective-permute-start(bf16[64,1280]{1,0:T(8,128)(2,1)S(1)} %copy-done.10), channel_id=1, source_target_pairs={{0,128},{128,0},{1,129},{129,1},{2,130},{130,2},{3,131},{131,3},{4... | collective-permute-start | bytes 491528 | tf_op jit(solution)/shard_map/ppermute | solution.py:211
  165.4 19.4 %all-to-all-start.5 = ((bf16[16,2,1280]{2,1,0:T(2,128)(2,1)}), bf16[16,2,1280]{2,1,0:T(2,128)(2,1)S(1)}, u32[]{:S(2)}, u32[]{:S(2)}) async-start(bf16[16,2,1280]{2,1,0:T(2,128)(2,1)} %broadcast_in_dim.6), calls=%async_computation.5 | async-start | bytes 163840 | tf_op jit(solution)/shard_map/all_to_all | solution.py:215
  173.0 18.8 %copy-start.9 = (bf16[64,1280]{1,0:T(8,128)(2,1)S(1)}, bf16[64,1280]{1,0:T(8,128)(2,1)}, u32[]{:S(2)}) copy-start(bf16[64,1280]{1,0:T(8,128)(2,1)} %get-tuple-element.23) | copy-start | bytes 491524
  185.6 14.0 %all-to-all-start.6 = ((bf16[32,2,1280]{2,1,0:T(2,128)(2,1)}), bf16[32,2,1280]{2,1,0:T(2,128)(2,1)S(1)}, u32[]{:S(2)}, u32[]{:S(2)}) async-start(bf16[32,2,1280]{2,1,0:T(2,128)(2,1)} %broadcast_in_dim.7), calls=%async_computation.6 | async-start | bytes 327680 | tf_op jit(solution)/shard_map/all_to_all | solution.py:215

commit v4 on v3

--- a/solution.py
+++ b/solution.py
@@ -20,7 +20,6 @@
 SMEM = pl.BlockSpec(memory_space=pltpu.SMEM)
 VMEM = pl.BlockSpec(memory_space=pltpu.VMEM)
 ANY = pl.BlockSpec(memory_space=pl.ANY)
-HBM = pl.BlockSpec(memory_space=pltpu.HBM)
 
 
 def call(kernel, outs, *operands, after=()):
@@ -34,7 +33,7 @@
         out_shape=outs,
         in_specs=[SMEM] + [VMEM] * (len(operands) - 1) + [ANY] * len(after),
         out_specs=[VMEM] * len(outs),
-        compiler_params=pltpu.CompilerParams(vmem_limit_bytes=20 * 1024 * 1024),
+        compiler_params=pltpu.CompilerParams(vmem_limit_bytes=14 * 1024 * 1024),
         cost_estimate=pl.CostEstimate(flops=0, bytes_accessed=bytes_accessed, transcendentals=0),
     )(*operands, *after)
 
@@ -84,11 +83,10 @@
     return halves[0][:, :D] * shares[0] + halves[1][:, :D] * shares[1], top, total
 
 
-def slots_kernel(where_am_i, router_rows, tok_a, tok_b, grad_a, grad_b, out, router_t):
+def slots_kernel(where_am_i, router_t, tok_own, tok_b, grad_own, grad_b, out):
     core = where_am_i[0]
-    router_t[...] = jnp.dot(slot_order(), router_rows[...], preferred_element_type=f32).astype(bf16)
-    tok = jnp.concatenate([tok_a[core], tok_b[core]], axis=0)
-    grad = jnp.concatenate([grad_a[core], grad_b[core]], axis=0)
+    tok = jnp.concatenate([tok_own[...], tok_b[core]], axis=0)
+    grad = jnp.concatenate([grad_own[...], grad_b[core]], axis=0)
     logits = lax.dot_general(router_t[...], tok, NT, preferred_element_type=f32)
     top = jnp.max(logits, axis=1, keepdims=True)
     raised = jnp.exp(logits - top)
@@ -148,7 +146,10 @@
         out[1] = jnp.dot(hiddens[j], slot_grad, preferred_element_type=f32).astype(bf16)
 
 
-def return_kernel(where_am_i, got, kept, stats, out):
+def return_kernel(where_am_i, got, kept, stats, tok_own, tok_b, grad_own, grad_b, out, tok, grad):
+    core = where_am_i[0]
+    tok[:64], tok[64:] = tok_own[...], tok_b[core]
+    grad[:64], grad[64:] = grad_own[...], grad_b[core]
     row = lax.broadcasted_iota(jnp.int32, (LANES, 2 * LANES), 0)
     col = lax.broadcasted_iota(jnp.int32, (LANES, 2 * LANES), 1)
     source = (row & 7) * 32 + (row & 8) + (row >> 4)
@@ -164,25 +165,7 @@
             out[zh * ZL + zl, :, D:] = extra[at]
 
 
-def tokens_kernel(
-    where_am_i, router_hbm, tok_a, tok_b, grad_a, grad_b, got_hbm, own_grad, sent_grad, router_grad,
-    router_t, tok, grad, got, arrived,
-):
-    core = where_am_i[0]
-    own, other = pl.ds(0, 64), pl.ds(64, 64)
-    moves = (
-        (router_hbm, router_t),
-        (tok_a.at[core], tok.at[own]),
-        (tok_b.at[core], tok.at[other]),
-        (got_hbm, got),
-        (grad_a.at[core], grad.at[own]),
-        (grad_b.at[core], grad.at[other]),
-    )
-    copies = [pltpu.make_async_copy(source, target, arrived.at[k]) for k, (source, target) in enumerate(moves)]
-    for copy in copies:
-        copy.start()
-    for copy in copies:
-        copy.wait()
+def tokens_kernel(where_am_i, router_t, tok, grad, got, router_grad, left, right):
     halves = [got[h * ZL : (h + 1) * ZL].astype(f32) for h in range(2)]
     both = halves[0] + halves[1]
     slot_in_grad = both[:, :8, :D].reshape(SLOTS, D).astype(bf16)
@@ -199,12 +182,24 @@
     disp_part = dispatch * (dgrad - weighted)
     logit_grad = (comb_part + disp_part).astype(bf16)
     by_expert = jnp.dot(slot_order(transpose=True), logit_grad, preferred_element_type=f32).astype(bf16)
-    router_grad[...] = jnp.dot(by_expert, tok[...], preferred_element_type=f32).astype(bf16)
-    left = jnp.concatenate([dispatch.astype(bf16), logit_grad], axis=0)
-    right = jnp.concatenate([slot_in_grad, router_t[...]], axis=0)
-    all_grad = lax.dot_general(left, right, TN, preferred_element_type=f32).astype(bf16)
+    rows = jnp.dot(by_expert, tok[...], preferred_element_type=f32).astype(bf16)
+    for k in range(SLOTS // 2):
+        router_grad[k] = rows[2 * k : 2 * k + 2]
+    left[:SLOTS], left[SLOTS:] = dispatch.astype(bf16), logit_grad
+    right[...] = slot_in_grad
+
+
+def tokens_grad_kernel(where_am_i, left, right, router_t, own_grad, sent_grad):
+    both = jnp.concatenate([right[...], router_t[...]], axis=0)
+    all_grad = lax.dot_general(left[...], both, TN, preferred_element_type=f32).astype(bf16)
     own_grad[...] = all_grad[:64]
     sent_grad[...] = all_grad[64:]
+
+
+def spread_kernel(where_am_i, got, out):
+    summed = jnp.sum(got[...].astype(f32), axis=0).astype(bf16)
+    for k in range(out.shape[0]):
+        out[k] = summed
 
 
 def swap(value):
@@ -218,10 +213,12 @@
 def on_device(tokens, router, up_proj, down_proj, out_grad):
     here = lax.axis_index("core").astype(jnp.int32).reshape(1)
     tok_b, grad_b = swap(tokens), swap(out_grad)
-    slots, router_t = call(
-        slots_kernel,
-        [shaped((16, 16, WIDE), bf16), shaped((SLOTS, D), bf16)],
-        here, router.T, tokens, tok_b, out_grad, grad_b,
+    on_first = here[0] == 0
+    tok_own = jnp.where(on_first, tokens[0], tokens[1])
+    grad_own = jnp.where(on_first, out_grad[0], out_grad[1])
+    router_t = router.T.reshape(Y, ZL, XH, D).transpose(1, 0, 2, 3).reshape(SLOTS, D)
+    (slots,) = call(
+        slots_kernel, [shaped((16, 16, WIDE), bf16)], here, router_t, tok_own, tok_b, grad_own, grad_b
     )
     got = exchange(slots, COLUMN)
     up_other, down_other = swap(up_proj[0]), swap(down_proj[0])
@@ -240,30 +237,30 @@
     keep, send = call(
         weights_kernel, [shaped((2, 320, D), bf16), shaped((2, 320, D), bf16)], here, pre_grads, hiddens, rows
     )
-    summed = (keep.astype(f32) + swap(send).astype(f32)).astype(bf16)
-    (by_owner,) = call(return_kernel, [shaped((16, 16, WIDE), bf16)], here, back, kept, stats)
+    got_send = swap(send)
+    up_grad, down_grad = ((keep[k : k + 1].astype(f32) + got_send[k : k + 1].astype(f32)).astype(bf16) for k in range(2))
+    by_owner, tok, grad = call(
+        return_kernel,
+        [shaped((16, 16, WIDE), bf16), shaped((LANES, D), bf16), shaped((LANES, D), bf16)],
+        here, back, kept, stats, tok_own, tok_b, grad_own, grad_b,
+    )
     got = exchange(by_owner, COLUMN)
-    own_grad, sent_grad, router_part = pl.pallas_call(
+    router_part, left, right = call(
         tokens_kernel,
-        out_shape=[shaped((64, D), bf16), shaped((64, D), bf16), shaped((SLOTS, D), bf16)],
-        in_specs=[SMEM] + [HBM] * 6,
-        out_specs=[VMEM] * 3,
-        scratch_shapes=[
-            pltpu.VMEM((SLOTS, D), bf16),
-            pltpu.VMEM((LANES, D), bf16),
-            pltpu.VMEM((LANES, D), bf16),
-            pltpu.VMEM((16, 16, WIDE), bf16),
-            pltpu.SemaphoreType.DMA((6,)),
-        ],
-        compiler_params=pltpu.CompilerParams(vmem_limit_bytes=63 * 1024 * 1024),
-    )(here, router_t, tokens, tok_b, out_grad, grad_b, got)
+        [shaped((32, 2, D), bf16), shaped((LANES, LANES), bf16), shaped((SLOTS, D), bf16)],
+        here, router_t, tok, grad, got, after=(up_grad, down_grad),
+    )
+    own_grad, sent_grad = call(
+        tokens_grad_kernel, [shaped((64, D), bf16), shaped((64, D), bf16)], here, left, right, router_t
+    )
     got_grad = swap(sent_grad)
-    own_first = here[0] == 0
-    tokens_grad = jnp.where(own_first, jnp.stack([own_grad, got_grad]), jnp.stack([got_grad, own_grad]))
-    part = exchange(router_part.reshape(32, 2, D), PLANE_CORES).astype(f32).sum(axis=0).astype(bf16)
-    whole = exchange(jnp.broadcast_to(part, (16, 2, D)), COLUMN).astype(f32).sum(axis=0).astype(bf16)
-    full = exchange(jnp.broadcast_to(whole, (32, 2, D)), PLANE_CORES).reshape(SLOTS, D)
-    return tokens_grad, full.T.astype(f32), summed[:1], summed[1:]
+    (part,) = call(
+        spread_kernel, [shaped((16, 2, D), bf16)], here, exchange(router_part, PLANE_CORES), after=(sent_grad,)
+    )
+    (whole,) = call(spread_kernel, [shaped((32, 2, D), bf16)], here, exchange(part, COLUMN))
+    full = exchange(whole, PLANE_CORES).reshape(SLOTS, D)
+    tokens_grad = jnp.where(on_first, jnp.stack([own_grad, got_grad]), jnp.stack([got_grad, own_grad]))
+    return tokens_grad, full.T.astype(f32), up_grad, down_grad
 
 
 def solution(mesh):

time: 201 us -> 194 us (0.965)
  local copies, waits for them, and re-layouts: 10.8 us -> 3.55 us
    unnamed x22, local copies, waits for them, and re-layouts: 5.69 us -> 1.62 us
    pallas_call x1 -> x0, Pallas kernels: 3.24 us -> none  [on_device(): pl.pallas_call(tokens_kernel, out_shape=[shaped((64, D), bf16), shaped((6...]
    pallas_call x5 -> x9, Pallas kernels: 8.73 us -> 10.9 us  [call(): pl.pallas_call(body, out_shape=outs, in_specs=[SMEM] + [VMEM] * (len(oper...]
  transfers between devices with their start and end apart: 11 -> 11, of which waited for: 8 -> 8; matrix products, arithmetic and copies ran while one was open for 4% -> 2% of each run, Pallas kernels for 3% -> 1%
where the time goes in v4:
time: 194 us; the launch traced here: 193 us
  waiting for transfers between devices  74.2 us (38%)
  starting transfers between devices  72.7 us (37%)
  blocking collectives  28.8 us (15%)
  Pallas kernels  10.9 us (6%)
  local copies, waits for them, and re-layouts  3.55 us (2%)
  other arithmetic  2.37 us (1%)
    all_to_all x5, waiting for transfers between devices, exchange(): return lax.all_to_all(value, axes, split_axis=0, concat_axis=0, tiled=True)  68.6 us
    all_to_all x5, starting transfers between devices, exchange(): return lax.all_to_all(value, axes, split_axis=0, concat_axis=0, tiled=True)  50 us
    all_to_all x2, blocking collectives, exchange(): return lax.all_to_all(value, axes, split_axis=0, concat_axis=0, tiled=True)  28.8 us
    ppermute x6, starting transfers between devices, swap(): return lax.ppermute(value, 'core', [(0, 1), (1, 0)])  22.7 us
    pallas_call x9, Pallas kernels, call(): pl.pallas_call(body, out_shape=outs, in_specs=[SMEM] + [VMEM] * (len(oper...  10.9 us
    ppermute x6, waiting for transfers between devices, swap(): return lax.ppermute(value, 'core', [(0, 1), (1, 0)])  5.62 us
  transfers between devices with their start and end apart: 11, of which 8 were waited for; matrix products, arithmetic and copies ran while one was open for 2% of the time, Pallas kernels for 1%

profile of v4, /device:TPU:1, one launch (start us, length us, event | category | flops | bytes accessed | tf_op | source)
XLA Modules:
  0.0 193.3 jit_solution(4819763515040664545)
XLA Ops:
  0.6 8.8 %collective-permute-start = (bf16[2,64,1280]{2,1,0:T(8,128)(2,1)}, bf16[2,64,1280]{2,1,0:T(8,128)(2,1)S(1)}, u32[]{:S(2)}, u32[]{:S(2)}) collective-permute-start(bf16[2,64,1280]{2,1,0:T(8,128)(2,1)} %param.5), channel_id=1, source_target_pairs={{0,128},{128,0},{1,129},{129,1},{2,130},{130,2},{3,131},{131,3},{4... | collective-permute-start | bytes 983048 | tf_op jit(solution)/shard_map/ppermute | solution.py:206
  9.4 1.9 collective-permute-start.1
  11.4 1.0 reshape.31
  12.3 0.1 copy.11
  12.5 0.1 reshape.32.router_t.refs_1_
  12.5 1.2 select_bitcast_fusion
  13.7 0.0 collective-permute-done.tok_b
  13.8 0.0 copy-start.2
  13.8 0.0 collective-permute-done.1.grad_b
  13.8 0.0 copy-start.4
  13.8 1.6 shard_map.84
  15.4 9.5 %all-to-all-start = ((bf16[16,16,1408]{2,1,0:T(8,128)(2,1)}), bf16[16,16,1408]{2,1,0:T(8,128)(2,1)S(1)}, u32[]{:S(2)}, u32[]{:S(2)}) async-start(bf16[16,16,1408]{2,1,0:T(8,128)(2,1)} %shard_map.84), calls=%async_computation | async-start | bytes 1441792 | tf_op jit(solution)/shard_map/all_to_all | solution.py:210
  24.9 2.7 %collective-permute-start.2 = (bf16[320,1280]{1,0:T(8,128)(2,1)}, bf16[320,1280]{1,0:T(8,128)(2,1)S(1)}, u32[]{:S(2)}, u32[]{:S(2)}) collective-permute-start(bf16[320,1280]{1,0:T(8,128)(2,1)} %bitcast.5.up_own), channel_id=1, source_target_pairs={{0,128},{128,0},{1,129},{129,1},{2,130},{130,2},{3,131},{131,3},{4... | collective-permute-start | bytes 2457608 | tf_op jit(solution)/shard_map/ppermute | solution.py:206
  27.6 1.9 collective-permute-start.3
  29.6 0.2 collective-permute-done.2.refs_2_.up_other
  29.8 2.3 %collective-permute-done.3.refs_3_.down_other = bf16[320,1280]{1,0:T(8,128)(2,1)S(1)} collective-permute-done((bf16[320,1280]{1,0:T(8,128)(2,1)}, bf16[320,1280]{1,0:T(8,128)(2,1)S(1)}, u32[]{:S(2)}, u32[]{:S(2)}) %collective-permute-start.3) | collective-permute-done | bytes 819232 | tf_op jit(solution)/shard_map/ppermute | solution.py:206
  32.1 24.5 %all-to-all-done.refs_1_ = bf16[16,16,1408]{2,1,0:T(8,128)(2,1)S(1)} async-done(((bf16[16,16,1408]{2,1,0:T(8,128)(2,1)}), bf16[16,16,1408]{2,1,0:T(8,128)(2,1)S(1)}, u32[]{:S(2)}, u32[]{:S(2)}) %all-to-all-start) | async-done | bytes 720928 | tf_op jit(solution)/shard_map/all_to_all | solution.py:210
  56.6 0.5 shard_map.85
  57.1 16.3 %all_to_all.35.rows = bf16[16,2,8,1280]{3,2,1,0:T(8,128)(2,1)S(1)} all-to-all(bf16[16,2,8,1280]{3,2,1,0:T(8,128)(2,1)S(1)} %bitcast.19), channel_id=1, replica_groups=mesh['zh'=2,'core'=2,'y'=4,'zl'=8,'xh'=2,'xl'=2] {'y','xh','xl'}, dimensions={0} | all-to-all | bytes 1310720 | tf_op jit(solution)/shard_map/all_to_all | solution.py:210
  73.4 3.1 %shard_map.86 = (bf16[16,2,8,1280]{3,2,1,0:T(8,128)(2,1)S(1)}, bf16[2,320,128]{2,1,0:T(8,128)(2,1)S(1)}, bf16[2,320,128]{2,1,0:T(8,128)(2,1)S(1)}) custom-call(s32[1]{0:T(128)} %bitcast.where_am_i.refs_0_, bf16[16,2,8,1280]{3,2,1,0:T(8,128)(2,1)S(1)} %all_to_all.35.rows, bf16[320,1280]{1,0:T(8,128)(2,1)} %bitcast.5.up_own, ...), custom_call_target="tpu_custom_call" | custom-call | bytes 4915204 | tf_op jit(solution)/shard_map/pallas_call | solution.py:31
  76.5 0.0 copy-start.9
  76.5 0.7 copy-done.9
  77.2 12.5 %all_to_all.36 = bf16[16,2,8,1280]{3,2,1,0:T(8,128)(2,1)S(1)} all-to-all(bf16[16,2,8,1280]{3,2,1,0:T(8,128)(2,1)S(1)} %get-tuple-element.21), channel_id=1, replica_groups=mesh['zh'=2,'core'=2,'y'=4,'zl'=8,'xh'=2,'xl'=2] {'y','xh','xl'}, dimensions={0} | all-to-all | bytes 1310720 | tf_op jit(solution)/shard_map/all_to_all | solution.py:210
  89.7 1.3 shard_map.87
  91.0 17.1 %all-to-all-start.3 = ((bf16[16,16,1408]{2,1,0:T(8,128)(2,1)}), bf16[16,16,1408]{2,1,0:T(8,128)(2,1)S(1)}, u32[]{:S(2)}, u32[]{:S(2)}) async-start(bf16[16,16,1408]{2,1,0:T(8,128)(2,1)} %get-tuple-element.26), calls=%async_computation.3 | async-start | bytes 1441792 | tf_op jit(solution)/shard_map/all_to_all | solution.py:210
  108.1 0.0 copy-start.8
  108.1 0.9 copy-done.8
  109.1 1.0 shard_map.88
  110.1 4.6 %collective-permute-start.4 = (bf16[2,320,1280]{2,1,0:T(8,128)(2,1)S(1)}, bf16[2,320,1280]{2,1,0:T(8,128)(2,1)S(1)}, u32[]{:S(2)}, u32[]{:S(2)}) collective-permute-start(bf16[2,320,1280]{2,1,0:T(8,128)(2,1)S(1)} %get-tuple-element.30), channel_id=1, source_target_pairs={{0,128},{128,0},{1,129},{129,1},{2,130},{130,2},{3,131},{131,3},{4... | collective-permute-start | bytes 4915208 | tf_op jit(solution)/shard_map/ppermute | solution.py:206
  114.7 3.1 %collective-permute-done.4 = bf16[2,320,1280]{2,1,0:T(8,128)(2,1)S(1)} collective-permute-done((bf16[2,320,1280]{2,1,0:T(8,128)(2,1)S(1)}, bf16[2,320,1280]{2,1,0:T(8,128)(2,1)S(1)}, u32[]{:S(2)}, u32[]{:S(2)}) %collective-permute-start.4) | collective-permute-done | bytes 1638432 | tf_op jit(solution)/shard_map/ppermute | solution.py:206
  117.8 0.4 add_convert_fusion
  118.2 0.0 copy-start
  118.2 0.0 copy-start.1
  118.2 20.4 %all-to-all-done.3.refs_4_ = bf16[16,16,1408]{2,1,0:T(8,128)(2,1)S(1)} async-done(((bf16[16,16,1408]{2,1,0:T(8,128)(2,1)}), bf16[16,16,1408]{2,1,0:T(8,128)(2,1)S(1)}, u32[]{:S(2)}, u32[]{:S(2)}) %all-to-all-start.3) | async-done | bytes 720928 | tf_op jit(solution)/shard_map/all_to_all | solution.py:210
  138.7 1.5 shard_map.89
  140.2 9.9 %all-to-all-start.4 = ((bf16[32,2,1280]{2,1,0:T(2,128)(2,1)}), bf16[32,2,1280]{2,1,0:T(2,128)(2,1)S(1)}, u32[]{:S(2)}, u32[]{:S(2)}) async-start(bf16[32,2,1280]{2,1,0:T(2,128)(2,1)} %get-tuple-element.35), calls=%async_computation.4 | async-start | bytes 327680 | tf_op jit(solution)/shard_map/all_to_all | solution.py:210
  150.1 0.3 shard_map.90
  150.4 7.5 %all-to-all-done.4.refs_1_ = bf16[32,2,1280]{2,1,0:T(2,128)(2,1)S(1)} async-done(((bf16[32,2,1280]{2,1,0:T(2,128)(2,1)}), bf16[32,2,1280]{2,1,0:T(2,128)(2,1)S(1)}, u32[]{:S(2)}, u32[]{:S(2)}) %all-to-all-start.4) | async-done | bytes 163872 | tf_op jit(solution)/shard_map/all_to_all | solution.py:210
  157.9 0.8 shard_map.91
  158.7 7.6 %all-to-all-start.5 = ((bf16[16,2,1280]{2,1,0:T(2,128)(2,1)}), bf16[16,2,1280]{2,1,0:T(2,128)(2,1)S(1)}, u32[]{:S(2)}, u32[]{:S(2)}) async-start(bf16[16,2,1280]{2,1,0:T(2,128)(2,1)} %shard_map.91), calls=%async_computation.5 | async-start | bytes 163840 | tf_op jit(solution)/shard_map/all_to_all | solution.py:210
  166.4 2.8 %collective-permute-start.5 = (bf16[64,1280]{1,0:T(8,128)(2,1)S(1)}, bf16[64,1280]{1,0:T(8,128)(2,1)S(1)}, u32[]{:S(2)}, u32[]{:S(2)}) collective-permute-start(bf16[64,1280]{1,0:T(8,128)(2,1)S(1)} %get-tuple-element.34.refs_2_), channel_id=1, source_target_pairs={{0,128},{128,0},{1,129},{129,1},{2,130},{130,2},{3,131},{131,3},{4... | collective-permute-start | bytes 491528 | tf_op jit(solution)/shard_map/ppermute | solution.py:206
  169.1 9.0 %all-to-all-done.5.got = bf16[16,2,1280]{2,1,0:T(2,128)(2,1)S(1)} async-done(((bf16[16,2,1280]{2,1,0:T(2,128)(2,1)}), bf16[16,2,1280]{2,1,0:T(2,128)(2,1)S(1)}, u32[]{:S(2)}, u32[]{:S(2)}) %all-to-all-start.5) | async-done | bytes 81952 | tf_op jit(solution)/shard_map/all_to_all | solution.py:210
  178.2 0.8 shard_map.92
  178.9 5.8 %all-to-all-start.6 = ((bf16[32,2,1280]{2,1,0:T(2,128)(2,1)}), bf16[32,2,1280]{2,1,0:T(2,128)(2,1)S(1)}, u32[]{:S(2)}, u32[]{:S(2)}) async-start(bf16[32,2,1280]{2,1,0:T(2,128)(2,1)} %shard_map.92), calls=%async_computation.6 | async-start | bytes 327680 | tf_op jit(solution)/shard_map/all_to_all | solution.py:210
  184.8 0.0 collective-permute-done.5
  184.8 0.8 maximum_select_fusion
  185.5 7.0 %all-to-all-done.6 = bf16[32,2,1280]{2,1,0:T(2,128)(2,1)S(1)} async-done(((bf16[32,2,1280]{2,1,0:T(2,128)(2,1)}), bf16[32,2,1280]{2,1,0:T(2,128)(2,1)S(1)}, u32[]{:S(2)}, u32[]{:S(2)}) %all-to-all-start.6) | async-done | bytes 163872 | tf_op jit(solution)/shard_map/all_to_all | solution.py:210
  192.6 0.8 reshape.35
  (14 shorter events, 0.0 us)
Async XLA Ops:
  0.6 13.1 %collective-permute-start = (bf16[2,64,1280]{2,1,0:T(8,128)(2,1)}, bf16[2,64,1280]{2,1,0:T(8,128)(2,1)S(1)}, u32[]{:S(2)}, u32[]{:S(2)}) collective-permute-start(bf16[2,64,1280]{2,1,0:T(8,128)(2,1)} %param.5), channel_id=1, source_target_pairs={{0,128},{128,0},{1,129},{129,1},{2,130},{130,2},{3,131},{131,3},{4... | collective-permute-start | bytes 983048 | tf_op jit(solution)/shard_map/ppermute | solution.py:206
  9.4 4.3 %collective-permute-start.1 = (bf16[2,64,1280]{2,1,0:T(8,128)(2,1)}, bf16[2,64,1280]{2,1,0:T(8,128)(2,1)S(1)}, u32[]{:S(2)}, u32[]{:S(2)}) collective-permute-start(bf16[2,64,1280]{2,1,0:T(8,128)(2,1)} %param.9), channel_id=1, source_target_pairs={{0,128},{128,0},{1,129},{129,1},{2,130},{130,2},{3,131},{131,3},{4... | collective-permute-start | bytes 983048 | tf_op jit(solution)/shard_map/ppermute | solution.py:206
  13.8 1.6 copy-start.2
  13.8 1.6 copy-start.4
  15.4 41.2 %all-to-all-start = ((bf16[16,16,1408]{2,1,0:T(8,128)(2,1)}), bf16[16,16,1408]{2,1,0:T(8,128)(2,1)S(1)}, u32[]{:S(2)}, u32[]{:S(2)}) async-start(bf16[16,16,1408]{2,1,0:T(8,128)(2,1)} %shard_map.84), calls=%async_computation | async-start | bytes 1441792 | tf_op jit(solution)/shard_map/all_to_all | solution.py:210
  24.9 4.8 %collective-permute-start.2 = (bf16[320,1280]{1,0:T(8,128)(2,1)}, bf16[320,1280]{1,0:T(8,128)(2,1)S(1)}, u32[]{:S(2)}, u32[]{:S(2)}) collective-permute-start(bf16[320,1280]{1,0:T(8,128)(2,1)} %bitcast.5.up_own), channel_id=1, source_target_pairs={{0,128},{128,0},{1,129},{129,1},{2,130},{130,2},{3,131},{131,3},{4... | collective-permute-start | bytes 2457608 | tf_op jit(solution)/shard_map/ppermute | solution.py:206
  27.6 4.4 %collective-permute-start.3 = (bf16[320,1280]{1,0:T(8,128)(2,1)}, bf16[320,1280]{1,0:T(8,128)(2,1)S(1)}, u32[]{:S(2)}, u32[]{:S(2)}) collective-permute-start(bf16[320,1280]{1,0:T(8,128)(2,1)} %bitcast.17), channel_id=1, source_target_pairs={{0,128},{128,0},{1,129},{129,1},{2,130},{130,2},{3,131},{131,3},{4... | collective-permute-start | bytes 2457608 | tf_op jit(solution)/shard_map/ppermute | solution.py:206
  56.6 16.8 %copy-start.6 = (bf16[1,320,1280]{2,1,0:T(8,128)(2,1)S(1)}, bf16[1,320,1280]{2,1,0:T(8,128)(2,1)}, u32[]{:S(2)}) copy-start(bf16[1,320,1280]{2,1,0:T(8,128)(2,1)} %param.8) | copy-start | bytes 2457604
  73.4 16.3 %copy-start.3 = (bf16[2,64,1280]{2,1,0:T(8,128)(2,1)S(1)}, bf16[2,64,1280]{2,1,0:T(8,128)(2,1)}, u32[]{:S(2)}) copy-start(bf16[2,64,1280]{2,1,0:T(8,128)(2,1)} %copy-done.2) | copy-start | bytes 983044
  73.4 16.3 %copy-start.5 = (bf16[2,64,1280]{2,1,0:T(8,128)(2,1)S(1)}, bf16[2,64,1280]{2,1,0:T(8,128)(2,1)}, u32[]{:S(2)}) copy-start(bf16[2,64,1280]{2,1,0:T(8,128)(2,1)} %copy-done.4) | copy-start | bytes 983044
  76.5 0.7 copy-start.9
  77.2 13.8 %copy-start.7 = (bf16[2,320,128]{2,1,0:T(8,128)(2,1)}, bf16[2,320,128]{2,1,0:T(8,128)(2,1)S(1)}, u32[]{:S(2)}) copy-start(bf16[2,320,128]{2,1,0:T(8,128)(2,1)S(1)} %get-tuple-element.27.pre_grads) | copy-start | bytes 491524
  89.7 18.4 %copy-start.10 = (bf16[2,320,128]{2,1,0:T(8,128)(2,1)S(1)}, bf16[2,320,128]{2,1,0:T(8,128)(2,1)}, u32[]{:S(2)}) copy-start(bf16[2,320,128]{2,1,0:T(8,128)(2,1)} %copy-done.9) | copy-start | bytes 491524
  91.0 47.7 %all-to-all-start.3 = ((bf16[16,16,1408]{2,1,0:T(8,128)(2,1)}), bf16[16,16,1408]{2,1,0:T(8,128)(2,1)S(1)}, u32[]{:S(2)}, u32[]{:S(2)}) async-start(bf16[16,16,1408]{2,1,0:T(8,128)(2,1)} %get-tuple-element.26), calls=%async_computation.3 | async-start | bytes 1441792 | tf_op jit(solution)/shard_map/all_to_all | solution.py:210
  108.1 0.9 copy-start.8
  110.1 7.7 %collective-permute-start.4 = (bf16[2,320,1280]{2,1,0:T(8,128)(2,1)S(1)}, bf16[2,320,1280]{2,1,0:T(8,128)(2,1)S(1)}, u32[]{:S(2)}, u32[]{:S(2)}) collective-permute-start(bf16[2,320,1280]{2,1,0:T(8,128)(2,1)S(1)} %get-tuple-element.30), channel_id=1, source_target_pairs={{0,128},{128,0},{1,129},{129,1},{2,130},{130,2},{3,131},{131,3},{4... | collective-permute-start | bytes 4915208 | tf_op jit(solution)/shard_map/ppermute | solution.py:206
  118.2 22.0 %copy-start = (bf16[1,320,1280]{2,1,0:T(8,128)(2,1)}, bf16[1,320,1280]{2,1,0:T(8,128)(2,1)S(1)}, u32[]{:S(2)}) copy-start(bf16[1,320,1280]{2,1,0:T(8,128)(2,1)S(1)} %get-tuple-element.36.refs_6_) | copy-start | bytes 2457604
  118.2 22.0 %copy-start.1 = (bf16[1,320,1280]{2,1,0:T(8,128)(2,1)}, bf16[1,320,1280]{2,1,0:T(8,128)(2,1)S(1)}, u32[]{:S(2)}) copy-start(bf16[1,320,1280]{2,1,0:T(8,128)(2,1)S(1)} %get-tuple-element.37.refs_5_) | copy-start | bytes 2457604
  140.2 17.7 %all-to-all-start.4 = ((bf16[32,2,1280]{2,1,0:T(2,128)(2,1)}), bf16[32,2,1280]{2,1,0:T(2,128)(2,1)S(1)}, u32[]{:S(2)}, u32[]{:S(2)}) async-start(bf16[32,2,1280]{2,1,0:T(2,128)(2,1)} %get-tuple-element.35), calls=%async_computation.4 | async-start | bytes 327680 | tf_op jit(solution)/shard_map/all_to_all | solution.py:210
  158.7 19.4 %all-to-all-start.5 = ((bf16[16,2,1280]{2,1,0:T(2,128)(2,1)}), bf16[16,2,1280]{2,1,0:T(2,128)(2,1)S(1)}, u32[]{:S(2)}, u32[]{:S(2)}) async-start(bf16[16,2,1280]{2,1,0:T(2,128)(2,1)} %shard_map.91), calls=%async_computation.5 | async-start | bytes 163840 | tf_op jit(solution)/shard_map/all_to_all | solution.py:210
  166.4 18.4 %collective-permute-start.5 = (bf16[64,1280]{1,0:T(8,128)(2,1)S(1)}, bf16[64,1280]{1,0:T(8,128)(2,1)S(1)}, u32[]{:S(2)}, u32[]{:S(2)}) collective-permute-start(bf16[64,1280]{1,0:T(8,128)(2,1)S(1)} %get-tuple-element.34.refs_2_), channel_id=1, source_target_pairs={{0,128},{128,0},{1,129},{129,1},{2,130},{130,2},{3,131},{131,3},{4... | collective-permute-start | bytes 491528 | tf_op jit(solution)/shard_map/ppermute | solution.py:206
  178.9 13.6 %all-to-all-start.6 = ((bf16[32,2,1280]{2,1,0:T(2,128)(2,1)}), bf16[32,2,1280]{2,1,0:T(2,128)(2,1)S(1)}, u32[]{:S(2)}, u32[]{:S(2)}) async-start(bf16[32,2,1280]{2,1,0:T(2,128)(2,1)} %shard_map.92), calls=%async_computation.6 | async-start | bytes 327680 | tf_op jit(solution)/shard_map/all_to_all | solution.py:210

commit v5 on v4

--- a/solution.py
+++ b/solution.py
@@ -1,5 +1,6 @@
 import jax
 import jax.numpy as jnp
+import numpy as np
 from jax import lax
 from jax.experimental import pallas as pl
 from jax.experimental.pallas import tpu as pltpu
@@ -13,6 +14,7 @@
 PLANE = ("y", "xh", "xl")
 PLANE_CORES = ("core", "y", "xh", "xl")
 COLUMN = ("zh", "zl")
+ALL = ("zh", "core", "y", "zl", "xh", "xl")
 EVERY_GROUP = ("y", "zl", "xh", "xl")
 bf16, f32 = jnp.bfloat16, jnp.float32
 NT = (((1,), (1,)), ((), ()))
@@ -33,7 +35,7 @@
         out_shape=outs,
         in_specs=[SMEM] + [VMEM] * (len(operands) - 1) + [ANY] * len(after),
         out_specs=[VMEM] * len(outs),
-        compiler_params=pltpu.CompilerParams(vmem_limit_bytes=14 * 1024 * 1024),
+        compiler_params=pltpu.CompilerParams(vmem_limit_bytes=20 * 1024 * 1024),
         cost_estimate=pl.CostEstimate(flops=0, bytes_accessed=bytes_accessed, transcendentals=0),
     )(*operands, *after)
 
@@ -98,12 +100,14 @@
         at = slice(zl * 8, zl * 8 + 8)
         for zh in range(2):
             place = zh * ZL + zl
-            out[place, :, :D] = jnp.concatenate([part_in[at], part_grad[at]], axis=0).astype(bf16)
-            out[place, :, D:] = jnp.concatenate([stats[at], stats[at]], axis=0).astype(bf16)
-
-
-def middle_kernel(where_am_i, got, out, kept, stats_out):
-    halves = [got[h * ZL : (h + 1) * ZL].reshape(LANES, WIDE).astype(f32) for h in range(2)]
+            out[place, 0, :, :D] = part_in[at].astype(bf16)
+            out[place, 1, :, :D] = part_grad[at].astype(bf16)
+            out[place, 0, :, D:] = stats[at].astype(bf16)
+            out[place, 1, :, D:] = stats[at].astype(bf16)
+
+
+def middle(got, out, kept, stats_out):
+    halves = [got[h * ZL : (h + 1) * ZL].astype(f32).reshape(LANES, WIDE) for h in range(2)]
     weighed = (lax.broadcasted_iota(jnp.int32, (LANES, 1), 0) & 8) == 0
     summed, top, total = merged(weighed, halves)
     kept[...] = summed
@@ -112,17 +116,19 @@
     col = lax.broadcasted_iota(jnp.int32, (LANES, LANES), 1)
     source = (row & 7) * 16 + (row & 8) + (row >> 4)
     pick = jnp.where(col == source, 1.0, 0.0).astype(bf16)
-    sorted_rows = jnp.dot(pick, summed.astype(bf16), preferred_element_type=f32).astype(bf16)
+    sorted_rows = jnp.dot(pick, summed.astype(bf16), preferred_element_type=f32)
     for yx in range(Y * XH):
-        for xl in range(2):
-            out[2 * yx + xl] = sorted_rows[yx * 16 : yx * 16 + 16]
+        for array in range(2):
+            at = yx * 16 + array * 8
+            for xl in range(2):
+                out[2 * yx + xl, array, :, :D] = sorted_rows[at : at + 8].astype(bf16)
 
 
 def array_rows(ref, array):
-    return ref[:, array].astype(f32).reshape(LANES, D).astype(bf16)
-
-
-def expert_kernel(where_am_i, rows, up_own, up_other, down_own, down_other, out, pre_grads, hiddens):
+    return ref[:, array, :, :D].astype(f32).reshape(LANES, D).astype(bf16)
+
+
+def expert(rows, up_own, up_other, down_own, down_other, out, pre_grads, hiddens):
     slot_in, slot_grad = array_rows(rows, 0), array_rows(rows, 1)
     in_grad = jnp.zeros((LANES, D), f32)
     slot_out = jnp.zeros((LANES, D), f32)
@@ -135,43 +141,97 @@
         pre_grads[j] = (hid_grad * (cdf + pre_act * density)).astype(bf16)
         in_grad += lax.dot_general(pre_grads[j], w_up[...], TN, preferred_element_type=f32)
         slot_out += lax.dot_general(hiddens[j], w_down[...], TN, preferred_element_type=f32)
-    out[:, 0] = in_grad.reshape(16, 8, D).astype(bf16)
-    out[:, 1] = slot_out.reshape(16, 8, D).astype(bf16)
-
-
-def weights_kernel(where_am_i, pre_grads, hiddens, rows, keep, send):
+    out[:, 0, :, :D] = in_grad.reshape(16, 8, D).astype(bf16)
+    out[:, 1, :, :D] = slot_out.reshape(16, 8, D).astype(bf16)
+
+
+def weight_grads(pre_grads, hiddens, rows, keep, send):
     slot_in, slot_grad = array_rows(rows, 0), array_rows(rows, 1)
     for j, out in enumerate((keep, send)):
         out[0] = jnp.dot(pre_grads[j], slot_in, preferred_element_type=f32).astype(bf16)
         out[1] = jnp.dot(hiddens[j], slot_grad, preferred_element_type=f32).astype(bf16)
 
 
-def return_kernel(where_am_i, got, kept, stats, tok_own, tok_b, grad_own, grad_b, out, tok, grad):
-    core = where_am_i[0]
-    tok[:64], tok[64:] = tok_own[...], tok_b[core]
-    grad[:64], grad[64:] = grad_own[...], grad_b[core]
+def back_to_owners(got, kept, stats, out):
     row = lax.broadcasted_iota(jnp.int32, (LANES, 2 * LANES), 0)
     col = lax.broadcasted_iota(jnp.int32, (LANES, 2 * LANES), 1)
     source = (row & 7) * 32 + (row & 8) + (row >> 4)
     pick = jnp.where((col & ~16) == source, 1.0, 0.0).astype(bf16)
-    summed = jnp.dot(pick, got[...], preferred_element_type=f32).astype(bf16)
-    share = jnp.sum(kept[...] * summed.astype(f32), axis=1, keepdims=True)
+    rows = got[:, :, :, :D].astype(f32).reshape(2 * LANES, D).astype(bf16)
+    summed = jnp.dot(pick, rows, preferred_element_type=f32).astype(bf16).astype(f32)
+    share = jnp.sum(kept[...] * summed, axis=1, keepdims=True)
     top, total = stats[:, 0:1], stats[:, 1:2]
-    extra = lanes_of(pieces(share) + pieces(top) + pieces(total)).astype(bf16)
+    extra = lanes_of(pieces(share) + pieces(top) + pieces(total))
     for zl in range(ZL):
-        at = slice(zl * 16, zl * 16 + 16)
-        for zh in range(2):
-            out[zh * ZL + zl, :, :D] = summed[at]
-            out[zh * ZL + zl, :, D:] = extra[at]
-
-
-def tokens_kernel(where_am_i, router_t, tok, grad, got, router_grad, left, right):
-    halves = [got[h * ZL : (h + 1) * ZL].astype(f32) for h in range(2)]
+        for array in range(2):
+            at = slice(zl * 16 + array * 8, zl * 16 + array * 8 + 8)
+            for zh in range(2):
+                out[zh * ZL + zl, array, :, :D] = summed[at].astype(bf16)
+                out[zh * ZL + zl, array, :, D:] = extra[at].astype(bf16)
+
+
+def phase_2(where_am_i, got, slots, out, kept, stats):
+    @pl.when(where_am_i[0] == 1)
+    def _():
+        middle(got, out, kept, stats)
+
+    @pl.when(where_am_i[0] == 0)
+    def _():
+        out[...] = slots[...]
+
+
+def phase_3(where_am_i, got, up_own, up_other, down_own, down_other, out, kept, stats, pre_grads, hiddens):
+    @pl.when(where_am_i[0] == 1)
+    def _():
+        expert(got, up_own, up_other, down_own, down_other, out, pre_grads, hiddens)
+
+    @pl.when(where_am_i[0] == 0)
+    def _():
+        middle(got, out, kept, stats)
+
+
+def phase_4(where_am_i, got, kept, stats, up_own, up_other, down_own, down_other, out, pre_grads, hiddens):
+    @pl.when(where_am_i[0] == 1)
+    def _():
+        back_to_owners(got, kept, stats, out)
+
+    @pl.when(where_am_i[0] == 0)
+    def _():
+        expert(got, up_own, up_other, down_own, down_other, out, pre_grads, hiddens)
+
+
+def phase_5(where_am_i, got, kept, stats, tok_own, tok_b, grad_own, grad_b, out, tok, grad):
+    core = where_am_i[0]
+    tok[:64], tok[64:] = tok_own[...], tok_b[core]
+    grad[:64], grad[64:] = grad_own[...], grad_b[core]
+
+    @pl.when(core == 0)
+    def _():
+        back_to_owners(got, kept, stats, out)
+
+    @pl.when(core == 1)
+    def _():
+        out[...] = got[...]
+
+
+def weights_kernel(where_am_i, pre_3, hid_3, rows_3, pre_4, hid_4, rows_4, keep, send):
+    @pl.when(where_am_i[0] == 1)
+    def _():
+        weight_grads(pre_3, hid_3, rows_3, keep, send)
+
+    @pl.when(where_am_i[0] == 0)
+    def _():
+        weight_grads(pre_4, hid_4, rows_4, keep, send)
+
+
+def tokens_kernel(where_am_i, router_t, tok, grad, got_4, got_5, router_grad, left, right):
+    spans = [slice(h * ZL, (h + 1) * ZL) for h in range(2)]
+    halves = [jnp.where(where_am_i[0] == 1, got_4[span], got_5[span]).astype(f32) for span in spans]
     both = halves[0] + halves[1]
-    slot_in_grad = both[:, :8, :D].reshape(SLOTS, D).astype(bf16)
-    slot_out = both[:, 8:, :D].reshape(SLOTS, D).astype(bf16)
-    weighted = three(both[:, :8, D:].reshape(SLOTS, LANES), 0)
-    stats = halves[0][:, :8, D:].reshape(SLOTS, LANES)
+    slot_in_grad = both[:, 0, :, :D].reshape(SLOTS, D).astype(bf16)
+    slot_out = both[:, 1, :, :D].reshape(SLOTS, D).astype(bf16)
+    weighted = three(both[:, 0, :, D:].reshape(SLOTS, LANES), 0)
+    stats = halves[0][:, 0, :, D:].reshape(SLOTS, LANES)
     top, total = three(stats, 3), three(stats, 6)
     logits = lax.dot_general(router_t[...], tok[...], NT, preferred_element_type=f32)
     dispatch = jnp.exp(logits - top) / total
@@ -210,6 +270,15 @@
     return lax.all_to_all(value, axes, split_axis=0, concat_axis=0, tiled=True)
 
 
+def mixed(value, first_axes, second_axes):
+    ids = np.arange(512).reshape(2, 2, Y, ZL, XH, 2)
+    orders = {PLANE: (0, 2, 1, 3, 4), COLUMN: (1, 3, 4, 0, 2)}
+    groups = [ids[:, core].transpose(orders[axes]).reshape(16, 16) for core, axes in enumerate((first_axes, second_axes))]
+    return lax.all_to_all(
+        value, ALL, split_axis=0, concat_axis=0, tiled=True, axis_index_groups=np.concatenate(groups).tolist()
+    )
+
+
 def on_device(tokens, router, up_proj, down_proj, out_grad):
     here = lax.axis_index("core").astype(jnp.int32).reshape(1)
     tok_b, grad_b = swap(tokens), swap(out_grad)
@@ -217,38 +286,34 @@
     tok_own = jnp.where(on_first, tokens[0], tokens[1])
     grad_own = jnp.where(on_first, out_grad[0], out_grad[1])
     router_t = router.T.reshape(Y, ZL, XH, D).transpose(1, 0, 2, 3).reshape(SLOTS, D)
-    (slots,) = call(
-        slots_kernel, [shaped((16, 16, WIDE), bf16)], here, router_t, tok_own, tok_b, grad_own, grad_b
-    )
-    got = exchange(slots, COLUMN)
+    wide = shaped((16, 2, 8, WIDE), bf16)
+    acts = [shaped((2, 320, LANES), bf16)] * 2
+    held = [shaped((LANES, D), f32), shaped((LANES, LANES), f32)]
+    (slots,) = call(slots_kernel, [wide], here, router_t, tok_own, tok_b, grad_own, grad_b)
+    got_1 = mixed(slots, PLANE, COLUMN)
     up_other, down_other = swap(up_proj[0]), swap(down_proj[0])
-    by_expert, kept, stats = call(
-        middle_kernel,
-        [shaped((16, 16, D), bf16), shaped((LANES, D), f32), shaped((LANES, LANES), f32)],
-        here, got, after=(up_other, down_other),
-    )
-    rows = exchange(by_expert.reshape(16, 2, 8, D), PLANE)
-    done, pre_grads, hiddens = call(
-        expert_kernel,
-        [shaped((16, 2, 8, D), bf16), shaped((2, 320, LANES), bf16), shaped((2, 320, LANES), bf16)],
-        here, rows, up_proj[0], up_other, down_proj[0], down_other,
-    )
-    back = exchange(done, PLANE).reshape(256, D)
+    weights = (up_proj[0], up_other, down_proj[0], down_other)
+    sent_2, kept_1, stats_1 = call(phase_2, [wide, *held], here, got_1, slots, after=(up_other, down_other))
+    got_2 = mixed(sent_2, COLUMN, PLANE)
+    sent_3, kept_0, stats_0, pre_1, hid_1 = call(phase_3, [wide, *held, *acts], here, got_2, *weights)
+    got_3 = exchange(sent_3, PLANE)
+    sent_4, pre_0, hid_0 = call(phase_4, [wide, *acts], here, got_3, kept_1, stats_1, *weights)
+    got_4 = mixed(sent_4, PLANE, COLUMN)
     keep, send = call(
-        weights_kernel, [shaped((2, 320, D), bf16), shaped((2, 320, D), bf16)], here, pre_grads, hiddens, rows
+        weights_kernel, [shaped((2, 320, D), bf16), shaped((2, 320, D), bf16)],
+        here, pre_1, hid_1, got_2, pre_0, hid_0, got_3,
     )
     got_send = swap(send)
     up_grad, down_grad = ((keep[k : k + 1].astype(f32) + got_send[k : k + 1].astype(f32)).astype(bf16) for k in range(2))
-    by_owner, tok, grad = call(
-        return_kernel,
-        [shaped((16, 16, WIDE), bf16), shaped((LANES, D), bf16), shaped((LANES, D), bf16)],
-        here, back, kept, stats, tok_own, tok_b, grad_own, grad_b,
-    )
-    got = exchange(by_owner, COLUMN)
+    sent_5, tok, grad = call(
+        phase_5, [wide, shaped((LANES, D), bf16), shaped((LANES, D), bf16)],
+        here, got_4, kept_0, stats_0, tok_own, tok_b, grad_own, grad_b,
+    )
+    got_5 = mixed(sent_5, COLUMN, PLANE)
     router_part, left, right = call(
         tokens_kernel,
         [shaped((32, 2, D), bf16), shaped((LANES, LANES), bf16), shaped((SLOTS, D), bf16)],
-        here, router_t, tok, grad, got, after=(up_grad, down_grad),
+        here, router_t, tok, grad, got_4, got_5, after=(up_grad, down_grad),
     )
     own_grad, sent_grad = call(
         tokens_grad_kernel, [shaped((64, D), bf16), shaped((64, D), bf16)], here, left, right, router_t

time: 194 us -> 188 us (0.969)
  blocking collectives: 28.8 us -> 60.5 us
  waiting for transfers between devices: 74.2 us -> 46.8 us
  starting transfers between devices: 72.7 us -> 56.3 us
  local copies, waits for them, and re-layouts: 3.55 us -> 8.66 us
    all_to_all x0 -> x2, blocking collectives: none -> 47.7 us  [mixed(): lax.all_to_all(value, ALL, split_axis=0, concat_axis=0, tiled=True, axis_...]
    all_to_all x5 -> x3, waiting for transfers between devices: 68.6 us -> 23.6 us  [exchange(): return lax.all_to_all(value, axes, split_axis=0, concat_axis=0, tiled=True)]
    all_to_all x5 -> x3, starting transfers between devices: 50 us -> 22.7 us  [exchange(): return lax.all_to_all(value, axes, split_axis=0, concat_axis=0, tiled=True)]
    all_to_all x0 -> x2, waiting for transfers between devices: none -> 17.8 us  [mixed(): lax.all_to_all(value, ALL, split_axis=0, concat_axis=0, tiled=True, axis_...]
    all_to_all x2 -> x1, blocking collectives: 28.8 us -> 12.7 us  [exchange(): return lax.all_to_all(value, axes, split_axis=0, concat_axis=0, tiled=True)]
    all_to_all x0 -> x2, starting transfers between devices: none -> 13.9 us  [mixed(): lax.all_to_all(value, ALL, split_axis=0, concat_axis=0, tiled=True, axis_...]
    unnamed x22 -> x54, local copies, waits for them, and re-layouts: 1.62 us -> 6.73 us
    ppermute x6, starting transfers between devices: 22.7 us -> 19.7 us  [swap(): return lax.ppermute(value, 'core', [(0, 1), (1, 0)])]
  transfers between devices with their start and end apart: 11 -> 11, of which waited for: 8 -> 7; matrix products, arithmetic and copies ran while one was open for 2% -> 2% of each run, Pallas kernels for 1% -> 1%
where the time goes in v5:
time: 188 us; the launch traced here: 187 us
  blocking collectives  60.5 us (32%)
  starting transfers between devices  56.3 us (30%)
  waiting for transfers between devices  46.8 us (25%)
  Pallas kernels  11.5 us (6%)
  local copies, waits for them, and re-layouts  8.66 us (5%)
  other arithmetic  2.35 us (1%)
    all_to_all x2, blocking collectives, mixed(): lax.all_to_all(value, ALL, split_axis=0, concat_axis=0, tiled=True, axis_...  47.7 us
    all_to_all x3, waiting for transfers between devices, exchange(): return lax.all_to_all(value, axes, split_axis=0, concat_axis=0, tiled=True)  23.6 us
    all_to_all x3, starting transfers between devices, exchange(): return lax.all_to_all(value, axes, split_axis=0, concat_axis=0, tiled=True)  22.7 us
    ppermute x6, starting transfers between devices, swap(): return lax.ppermute(value, 'core', [(0, 1), (1, 0)])  19.7 us
    all_to_all x2, waiting for transfers between devices, mixed(): lax.all_to_all(value, ALL, split_axis=0, concat_axis=0, tiled=True, axis_...  17.8 us
    all_to_all x2, starting transfers between devices, mixed(): lax.all_to_all(value, ALL, split_axis=0, concat_axis=0, tiled=True, axis_...  13.9 us
    all_to_all x1, blocking collectives, exchange(): return lax.all_to_all(value, axes, split_axis=0, concat_axis=0, tiled=True)  12.7 us
    pallas_call x10, Pallas kernels, call(): pl.pallas_call(body, out_shape=outs, in_specs=[SMEM] + [VMEM] * (len(oper...  11.5 us
  transfers between devices with their start and end apart: 11, of which 7 were waited for; matrix products, arithmetic and copies ran while one was open for 2% of the time, Pallas kernels for 1%

profile of v5, /device:TPU:1, one launch (start us, length us, event | category | flops | bytes accessed | tf_op | source)
XLA Modules:
  0.0 187.1 jit_solution(1076980569464649796)
XLA Ops:
  0.6 8.8 %collective-permute-start = (bf16[2,64,1280]{2,1,0:T(8,128)(2,1)}, bf16[2,64,1280]{2,1,0:T(8,128)(2,1)S(1)}, u32[]{:S(2)}, u32[]{:S(2)}) collective-permute-start(bf16[2,64,1280]{2,1,0:T(8,128)(2,1)} %param.5), channel_id=1, source_target_pairs={{0,128},{128,0},{1,129},{129,1},{2,130},{130,2},{3,131},{131,3},{4... | collective-permute-start | bytes 983048 | tf_op jit(solution)/shard_map/ppermute | solution.py:266
  9.4 1.9 %collective-permute-start.1 = (bf16[2,64,1280]{2,1,0:T(8,128)(2,1)}, bf16[2,64,1280]{2,1,0:T(8,128)(2,1)S(1)}, u32[]{:S(2)}, u32[]{:S(2)}) collective-permute-start(bf16[2,64,1280]{2,1,0:T(8,128)(2,1)} %param.9), channel_id=1, source_target_pairs={{0,128},{128,0},{1,129},{129,1},{2,130},{130,2},{3,131},{131,3},{4... | collective-permute-start | bytes 983048 | tf_op jit(solution)/shard_map/ppermute | solution.py:266
  11.4 1.0 reshape.25
  12.3 0.1 copy.11
  12.5 0.1 reshape.26.router_t.refs_1_
  12.5 1.2 select_bitcast_fusion
  13.8 0.0 copy-start.12
  13.8 1.6 shard_map.84.refs_2_
  15.4 0.7 copy-done.6
  16.1 0.7 copy-done.8
  16.8 9.6 %all-to-all-start = ((bf16[16,2,8,1408]{3,2,1,0:T(8,128)(2,1)}), bf16[16,2,8,1408]{3,2,1,0:T(8,128)(2,1)}, u32[]{:S(2)}, u32[]{:S(2)}) async-start(bf16[16,2,8,1408]{3,2,1,0:T(8,128)(2,1)} %shard_map.84.refs_2_), calls=%async_computation | async-start | bytes 1441792 | tf_op jit(solution)/shard_map/all_to_all | solution.py:277
  26.4 1.9 %collective-permute-start.2 = (bf16[320,1280]{1,0:T(8,128)(2,1)S(1)}, bf16[320,1280]{1,0:T(8,128)(2,1)S(1)}, u32[]{:S(2)}, u32[]{:S(2)}) collective-permute-start(bf16[320,1280]{1,0:T(8,128)(2,1)S(1)} %bitcast.14), channel_id=1, source_target_pairs={{0,128},{128,0},{1,129},{129,1},{2,130},{130,2},{3,131},{131,3},{4... | collective-permute-start | bytes 2457608 | tf_op jit(solution)/shard_map/ppermute | solution.py:266
  28.3 2.4 %collective-permute-start.3 = (bf16[320,1280]{1,0:T(8,128)(2,1)S(1)}, bf16[320,1280]{1,0:T(8,128)(2,1)S(1)}, u32[]{:S(2)}, u32[]{:S(2)}) collective-permute-start(bf16[320,1280]{1,0:T(8,128)(2,1)S(1)} %bitcast.17), channel_id=1, source_target_pairs={{0,128},{128,0},{1,129},{129,1},{2,130},{130,2},{3,131},{131,3},{4... | collective-permute-start | bytes 2457608 | tf_op jit(solution)/shard_map/ppermute | solution.py:266
  30.7 1.9 %collective-permute-done.3.refs_4_.down_other = bf16[320,1280]{1,0:T(8,128)(2,1)S(1)} collective-permute-done((bf16[320,1280]{1,0:T(8,128)(2,1)S(1)}, bf16[320,1280]{1,0:T(8,128)(2,1)S(1)}, u32[]{:S(2)}, u32[]{:S(2)}) %collective-permute-start.3) | collective-permute-done | bytes 819232 | tf_op jit(solution)/shard_map/ppermute | solution.py:266
  32.6 15.2 %all-to-all-done.refs_1_ = bf16[16,2,8,1408]{3,2,1,0:T(8,128)(2,1)} async-done(((bf16[16,2,8,1408]{3,2,1,0:T(8,128)(2,1)}), bf16[16,2,8,1408]{3,2,1,0:T(8,128)(2,1)}, u32[]{:S(2)}, u32[]{:S(2)}) %all-to-all-start) | async-done | bytes 720928 | tf_op jit(solution)/shard_map/all_to_all | solution.py:277
  47.8 1.8 shard_map.85
  49.7 16.9 %all_to_all.40.got.rows_3 = bf16[16,2,8,1408]{3,2,1,0:T(8,128)(2,1)S(1)} all-to-all(bf16[16,2,8,1408]{3,2,1,0:T(8,128)(2,1)S(1)} %get-tuple-element.25), channel_id=1, replica_groups={{0,4,8,12,16,20,24,28,256,260,264,268,272,276,280,284},{1,5,9,13,17,21,..., dimensions={0} | all-to-all | bytes 1441792 | tf_op jit(solution)/shard_map/all_to_all | solution.py:277
  66.6 1.1 copy-done.1
  67.7 1.1 copy-done.3
  68.9 1.9 %shard_map.86 = (bf16[16,2,8,1408]{3,2,1,0:T(8,128)(2,1)S(1)}, f32[128,1280]{1,0:T(8,128)S(1)}, f32[128,128]{1,0:T(8,128)S(1)}, bf16[2,320,128]{2,1,0:T(8,128)(2,1)S(1)}, bf16[2,320,128]{2,1,0:T(8,128)(2,1)S(1)}) custom-call(s32[1]{0:T(128)} %bitcast.where_am_i.refs_0_, bf16[16,2,8,1408]{3,2,1,0:T(8,128)(2,1)S(1)} %all_to_all.40.got.rows_3, ...), custom_call_target="tpu_custom_call" | custom-call | bytes 5767172 | tf_op jit(solution)/shard_map/pallas_call | solution.py:33
  70.8 12.7 %all_to_all.41.got.rows_4 = bf16[16,2,8,1408]{3,2,1,0:T(8,128)(2,1)S(1)} all-to-all(bf16[16,2,8,1408]{3,2,1,0:T(8,128)(2,1)S(1)} %get-tuple-element.26), channel_id=1, replica_groups=mesh['zh'=2,'core'=2,'y'=4,'zl'=8,'xh'=2,'xl'=2] {'y','xh','xl'}, dimensions={0} | all-to-all | bytes 1441792 | tf_op jit(solution)/shard_map/all_to_all | solution.py:270
  83.6 0.4 shard_map.87
  84.0 0.0 copy-start.13
  84.0 30.8 %all_to_all.42.got.refs_4_ = bf16[16,2,8,1408]{3,2,1,0:T(8,128)(2,1)S(1)} all-to-all(bf16[16,2,8,1408]{3,2,1,0:T(8,128)(2,1)S(1)} %get-tuple-element.29), channel_id=1, replica_groups={{0,1,2,3,32,33,34,35,64,65,66,67,96,97,98,99},{4,5,6,7,36,37,38,39,68,6..., dimensions={0} | all-to-all | bytes 1441792 | tf_op jit(solution)/shard_map/all_to_all | solution.py:277
  114.9 1.0 shard_map.88
  115.9 0.7 copy-done.14
  116.6 0.7 copy-done.16
  117.3 4.3 %all-to-all-start.4 = ((bf16[16,2,8,1408]{3,2,1,0:T(8,128)(2,1)}), bf16[16,2,8,1408]{3,2,1,0:T(8,128)(2,1)}, u32[]{:S(2)}, u32[]{:S(2)}) async-start(bf16[16,2,8,1408]{3,2,1,0:T(8,128)(2,1)} %get-tuple-element.34), calls=%async_computation.4 | async-start | bytes 1441792 | tf_op jit(solution)/shard_map/all_to_all | solution.py:277
  121.7 0.9 copy-done.25
  122.6 1.0 shard_map.89
  123.6 1.9 %collective-permute-start.4 = (bf16[2,320,1280]{2,1,0:T(8,128)(2,1)S(1)}, bf16[2,320,1280]{2,1,0:T(8,128)(2,1)S(1)}, u32[]{:S(2)}, u32[]{:S(2)}) collective-permute-start(bf16[2,320,1280]{2,1,0:T(8,128)(2,1)S(1)} %get-tuple-element.40), channel_id=1, source_target_pairs={{0,128},{128,0},{1,129},{129,1},{2,130},{130,2},{3,131},{131,3},{4... | collective-permute-start | bytes 4915208 | tf_op jit(solution)/shard_map/ppermute | solution.py:266
  125.5 3.5 %collective-permute-done.4 = bf16[2,320,1280]{2,1,0:T(8,128)(2,1)S(1)} collective-permute-done((bf16[2,320,1280]{2,1,0:T(8,128)(2,1)S(1)}, bf16[2,320,1280]{2,1,0:T(8,128)(2,1)S(1)}, u32[]{:S(2)}, u32[]{:S(2)}) %collective-permute-start.4) | collective-permute-done | bytes 1638432 | tf_op jit(solution)/shard_map/ppermute | solution.py:266
  129.0 0.4 add_convert_fusion
  129.4 2.6 %all-to-all-done.4.refs_5_ = bf16[16,2,8,1408]{3,2,1,0:T(8,128)(2,1)} async-done(((bf16[16,2,8,1408]{3,2,1,0:T(8,128)(2,1)}), bf16[16,2,8,1408]{3,2,1,0:T(8,128)(2,1)}, u32[]{:S(2)}, u32[]{:S(2)}) %all-to-all-start.4) | async-done | bytes 720928 | tf_op jit(solution)/shard_map/all_to_all | solution.py:277
  132.0 1.9 %shard_map.90 = (bf16[32,2,1280]{2,1,0:T(2,128)(2,1)S(1)}, bf16[128,128]{1,0:T(8,128)(2,1)S(1)}, bf16[64,1280]{1,0:T(8,128)(2,1)S(1)}) custom-call(s32[1]{0:T(128)} %bitcast.where_am_i.refs_0_, bf16[64,1280]{1,0:T(8,128)(2,1)S(1)} %reshape.26.router_t.refs_1_, bf16[128,1280]{1,0:T(8,128)(2,1)S(1)} %copy-done.15, bf16[128,1280]{1,0:T(8,128)(2,1)S(1)} %copy-done.17, ...), custom_call_target="tpu_custom_call" | custom-call | bytes 2621444 | tf_op jit(solution)/shard_map/pallas_call | solution.py:33
  134.0 0.7 copy-done.26
  134.6 10.4 %all-to-all-start.5 = ((bf16[32,2,1280]{2,1,0:T(2,128)(2,1)}), bf16[32,2,1280]{2,1,0:T(2,128)(2,1)S(1)}, u32[]{:S(2)}, u32[]{:S(2)}) async-start(bf16[32,2,1280]{2,1,0:T(2,128)(2,1)} %copy-done.26), calls=%async_computation.5 | async-start | bytes 327680 | tf_op jit(solution)/shard_map/all_to_all | solution.py:270
  145.1 0.3 shard_map.91
  145.4 7.5 %all-to-all-done.5.refs_1_ = bf16[32,2,1280]{2,1,0:T(2,128)(2,1)S(1)} async-done(((bf16[32,2,1280]{2,1,0:T(2,128)(2,1)}), bf16[32,2,1280]{2,1,0:T(2,128)(2,1)S(1)}, u32[]{:S(2)}, u32[]{:S(2)}) %all-to-all-start.5) | async-done | bytes 163872 | tf_op jit(solution)/shard_map/all_to_all | solution.py:270
  152.9 0.8 shard_map.92
  153.7 6.5 %all-to-all-start.6 = ((bf16[16,2,1280]{2,1,0:T(2,128)(2,1)}), bf16[16,2,1280]{2,1,0:T(2,128)(2,1)S(1)}, u32[]{:S(2)}, u32[]{:S(2)}) async-start(bf16[16,2,1280]{2,1,0:T(2,128)(2,1)} %shard_map.92), calls=%async_computation.6 | async-start | bytes 163840 | tf_op jit(solution)/shard_map/all_to_all | solution.py:270
  160.2 2.8 %collective-permute-start.5 = (bf16[64,1280]{1,0:T(8,128)(2,1)S(1)}, bf16[64,1280]{1,0:T(8,128)(2,1)S(1)}, u32[]{:S(2)}, u32[]{:S(2)}) collective-permute-start(bf16[64,1280]{1,0:T(8,128)(2,1)S(1)} %get-tuple-element.44.refs_2_), channel_id=1, source_target_pairs={{0,128},{128,0},{1,129},{129,1},{2,130},{130,2},{3,131},{131,3},{4... | collective-permute-start | bytes 491528 | tf_op jit(solution)/shard_map/ppermute | solution.py:266
  162.9 9.0 %all-to-all-done.6.got = bf16[16,2,1280]{2,1,0:T(2,128)(2,1)S(1)} async-done(((bf16[16,2,1280]{2,1,0:T(2,128)(2,1)}), bf16[16,2,1280]{2,1,0:T(2,128)(2,1)S(1)}, u32[]{:S(2)}, u32[]{:S(2)}) %all-to-all-start.6) | async-done | bytes 81952 | tf_op jit(solution)/shard_map/all_to_all | solution.py:270
  172.0 0.8 shard_map.93
  172.7 5.8 %all-to-all-start.7 = ((bf16[32,2,1280]{2,1,0:T(2,128)(2,1)}), bf16[32,2,1280]{2,1,0:T(2,128)(2,1)S(1)}, u32[]{:S(2)}, u32[]{:S(2)}) async-start(bf16[32,2,1280]{2,1,0:T(2,128)(2,1)} %shard_map.93), calls=%async_computation.7 | async-start | bytes 327680 | tf_op jit(solution)/shard_map/all_to_all | solution.py:270
  178.6 0.8 maximum_select_fusion
  179.3 7.0 %all-to-all-done.7 = bf16[32,2,1280]{2,1,0:T(2,128)(2,1)S(1)} async-done(((bf16[32,2,1280]{2,1,0:T(2,128)(2,1)}), bf16[32,2,1280]{2,1,0:T(2,128)(2,1)S(1)}, u32[]{:S(2)}, u32[]{:S(2)}) %all-to-all-start.7) | async-done | bytes 163872 | tf_op jit(solution)/shard_map/all_to_all | solution.py:270
  186.4 0.8 reshape.27
  (48 shorter events, 0.1 us)
Async XLA Ops:
  0.6 13.1 %collective-permute-start = (bf16[2,64,1280]{2,1,0:T(8,128)(2,1)}, bf16[2,64,1280]{2,1,0:T(8,128)(2,1)S(1)}, u32[]{:S(2)}, u32[]{:S(2)}) collective-permute-start(bf16[2,64,1280]{2,1,0:T(8,128)(2,1)} %param.5), channel_id=1, source_target_pairs={{0,128},{128,0},{1,129},{129,1},{2,130},{130,2},{3,131},{131,3},{4... | collective-permute-start | bytes 983048 | tf_op jit(solution)/shard_map/ppermute | solution.py:266
  9.4 4.3 %collective-permute-start.1 = (bf16[2,64,1280]{2,1,0:T(8,128)(2,1)}, bf16[2,64,1280]{2,1,0:T(8,128)(2,1)S(1)}, u32[]{:S(2)}, u32[]{:S(2)}) collective-permute-start(bf16[2,64,1280]{2,1,0:T(8,128)(2,1)} %param.9), channel_id=1, source_target_pairs={{0,128},{128,0},{1,129},{129,1},{2,130},{130,2},{3,131},{131,3},{4... | collective-permute-start | bytes 983048 | tf_op jit(solution)/shard_map/ppermute | solution.py:266
  13.8 3.0 %copy-start.10 = (bf16[2,64,1280]{2,1,0:T(8,128)(2,1)}, bf16[2,64,1280]{2,1,0:T(8,128)(2,1)S(1)}, u32[]{:S(2)}) copy-start(bf16[2,64,1280]{2,1,0:T(8,128)(2,1)S(1)} %collective-permute-done.tok_b) | copy-start | bytes 983044
  13.8 3.0 %copy-start.12 = (bf16[2,64,1280]{2,1,0:T(8,128)(2,1)}, bf16[2,64,1280]{2,1,0:T(8,128)(2,1)S(1)}, u32[]{:S(2)}) copy-start(bf16[2,64,1280]{2,1,0:T(8,128)(2,1)S(1)} %collective-permute-done.1.grad_b) | copy-start | bytes 983044
  13.8 12.6 %copy-start = (bf16[1,320,1280]{2,1,0:T(8,128)(2,1)S(1)}, bf16[1,320,1280]{2,1,0:T(8,128)(2,1)}, u32[]{:S(2)}) copy-start(bf16[1,320,1280]{2,1,0:T(8,128)(2,1)} %param.7) | copy-start | bytes 2457604
  13.8 14.5 %copy-start.2 = (bf16[1,320,1280]{2,1,0:T(8,128)(2,1)S(1)}, bf16[1,320,1280]{2,1,0:T(8,128)(2,1)}, u32[]{:S(2)}) copy-start(bf16[1,320,1280]{2,1,0:T(8,128)(2,1)} %param.8) | copy-start | bytes 2457604
  15.4 0.7 copy-start.6
  16.1 0.7 copy-start.8
  16.8 31.1 %all-to-all-start = ((bf16[16,2,8,1408]{3,2,1,0:T(8,128)(2,1)}), bf16[16,2,8,1408]{3,2,1,0:T(8,128)(2,1)}, u32[]{:S(2)}, u32[]{:S(2)}) async-start(bf16[16,2,8,1408]{3,2,1,0:T(8,128)(2,1)} %shard_map.84.refs_2_), calls=%async_computation | async-start | bytes 1441792 | tf_op jit(solution)/shard_map/all_to_all | solution.py:277
  26.4 4.4 %collective-permute-start.2 = (bf16[320,1280]{1,0:T(8,128)(2,1)S(1)}, bf16[320,1280]{1,0:T(8,128)(2,1)S(1)}, u32[]{:S(2)}, u32[]{:S(2)}) collective-permute-start(bf16[320,1280]{1,0:T(8,128)(2,1)S(1)} %bitcast.14), channel_id=1, source_target_pairs={{0,128},{128,0},{1,129},{129,1},{2,130},{130,2},{3,131},{131,3},{4... | collective-permute-start | bytes 2457608 | tf_op jit(solution)/shard_map/ppermute | solution.py:266
  28.3 4.4 %collective-permute-start.3 = (bf16[320,1280]{1,0:T(8,128)(2,1)S(1)}, bf16[320,1280]{1,0:T(8,128)(2,1)S(1)}, u32[]{:S(2)}, u32[]{:S(2)}) collective-permute-start(bf16[320,1280]{1,0:T(8,128)(2,1)S(1)} %bitcast.17), channel_id=1, source_target_pairs={{0,128},{128,0},{1,129},{129,1},{2,130},{130,2},{3,131},{131,3},{4... | collective-permute-start | bytes 2457608 | tf_op jit(solution)/shard_map/ppermute | solution.py:266
  66.6 1.1 copy-start.1
  67.7 1.1 copy-start.3
  70.8 12.8 %copy-start.18 = (bf16[2,320,128]{2,1,0:T(8,128)(2,1)}, bf16[2,320,128]{2,1,0:T(8,128)(2,1)S(1)}, u32[]{:S(2)}) copy-start(bf16[2,320,128]{2,1,0:T(8,128)(2,1)S(1)} %get-tuple-element.35.pre_3) | copy-start | bytes 491524
  70.8 12.8 %copy-start.20 = (bf16[2,320,128]{2,1,0:T(8,128)(2,1)}, bf16[2,320,128]{2,1,0:T(8,128)(2,1)S(1)}, u32[]{:S(2)}) copy-start(bf16[2,320,128]{2,1,0:T(8,128)(2,1)S(1)} %get-tuple-element.36.hid_3) | copy-start | bytes 491524
  83.6 31.3 %copy-start.7 = (bf16[64,1280]{1,0:T(8,128)(2,1)S(1)}, bf16[64,1280]{1,0:T(8,128)(2,1)}, u32[]{:S(2)}) copy-start(bf16[64,1280]{1,0:T(8,128)(2,1)} %copy-done.6) | copy-start | bytes 491524
  83.6 31.3 %copy-start.9 = (bf16[64,1280]{1,0:T(8,128)(2,1)S(1)}, bf16[64,1280]{1,0:T(8,128)(2,1)}, u32[]{:S(2)}) copy-start(bf16[64,1280]{1,0:T(8,128)(2,1)} %copy-done.8) | copy-start | bytes 491524
  84.0 30.9 %copy-start.22 = (bf16[2,320,128]{2,1,0:T(8,128)(2,1)}, bf16[2,320,128]{2,1,0:T(8,128)(2,1)S(1)}, u32[]{:S(2)}) copy-start(bf16[2,320,128]{2,1,0:T(8,128)(2,1)S(1)} %get-tuple-element.37.pre_4) | copy-start | bytes 491524
  84.0 31.9 %copy-start.24 = (bf16[2,320,128]{2,1,0:T(8,128)(2,1)}, bf16[2,320,128]{2,1,0:T(8,128)(2,1)S(1)}, u32[]{:S(2)}) copy-start(bf16[2,320,128]{2,1,0:T(8,128)(2,1)S(1)} %get-tuple-element.38.hid_4) | copy-start | bytes 491524
  84.0 30.9 %copy-start.11 = (bf16[2,64,1280]{2,1,0:T(8,128)(2,1)S(1)}, bf16[2,64,1280]{2,1,0:T(8,128)(2,1)}, u32[]{:S(2)}) copy-start(bf16[2,64,1280]{2,1,0:T(8,128)(2,1)} %copy-done.10) | copy-start | bytes 983044
  84.0 30.9 %copy-start.13 = (bf16[2,64,1280]{2,1,0:T(8,128)(2,1)S(1)}, bf16[2,64,1280]{2,1,0:T(8,128)(2,1)}, u32[]{:S(2)}) copy-start(bf16[2,64,1280]{2,1,0:T(8,128)(2,1)} %copy-done.12) | copy-start | bytes 983044
  114.9 6.7 %copy-start.19 = (bf16[2,320,128]{2,1,0:T(8,128)(2,1)S(1)}, bf16[2,320,128]{2,1,0:T(8,128)(2,1)}, u32[]{:S(2)}) copy-start(bf16[2,320,128]{2,1,0:T(8,128)(2,1)} %copy-done.18) | copy-start | bytes 491524
  114.9 6.7 %copy-start.21 = (bf16[2,320,128]{2,1,0:T(8,128)(2,1)S(1)}, bf16[2,320,128]{2,1,0:T(8,128)(2,1)}, u32[]{:S(2)}) copy-start(bf16[2,320,128]{2,1,0:T(8,128)(2,1)} %copy-done.20) | copy-start | bytes 491524
  114.9 6.7 %copy-start.23 = (bf16[2,320,128]{2,1,0:T(8,128)(2,1)S(1)}, bf16[2,320,128]{2,1,0:T(8,128)(2,1)}, u32[]{:S(2)}) copy-start(bf16[2,320,128]{2,1,0:T(8,128)(2,1)} %copy-done.22) | copy-start | bytes 491524
  115.9 0.7 copy-start.14
  116.6 0.7 copy-start.16
  117.3 14.6 %all-to-all-start.4 = ((bf16[16,2,8,1408]{3,2,1,0:T(8,128)(2,1)}), bf16[16,2,8,1408]{3,2,1,0:T(8,128)(2,1)}, u32[]{:S(2)}, u32[]{:S(2)}) async-start(bf16[16,2,8,1408]{3,2,1,0:T(8,128)(2,1)} %get-tuple-element.34), calls=%async_computation.4 | async-start | bytes 1441792 | tf_op jit(solution)/shard_map/all_to_all | solution.py:277
  121.7 0.9 copy-start.25
  123.6 5.4 %collective-permute-start.4 = (bf16[2,320,1280]{2,1,0:T(8,128)(2,1)S(1)}, bf16[2,320,1280]{2,1,0:T(8,128)(2,1)S(1)}, u32[]{:S(2)}, u32[]{:S(2)}) collective-permute-start(bf16[2,320,1280]{2,1,0:T(8,128)(2,1)S(1)} %get-tuple-element.40), channel_id=1, source_target_pairs={{0,128},{128,0},{1,129},{129,1},{2,130},{130,2},{3,131},{131,3},{4... | collective-permute-start | bytes 4915208 | tf_op jit(solution)/shard_map/ppermute | solution.py:266
  129.0 3.0 %copy-start.15 = (bf16[128,1280]{1,0:T(8,128)(2,1)S(1)}, bf16[128,1280]{1,0:T(8,128)(2,1)}, u32[]{:S(2)}) copy-start(bf16[128,1280]{1,0:T(8,128)(2,1)} %copy-done.14) | copy-start | bytes 983044
  129.0 3.0 %copy-start.17 = (bf16[128,1280]{1,0:T(8,128)(2,1)S(1)}, bf16[128,1280]{1,0:T(8,128)(2,1)}, u32[]{:S(2)}) copy-start(bf16[128,1280]{1,0:T(8,128)(2,1)} %copy-done.16) | copy-start | bytes 983044
  129.4 4.5 %copy-start.4 = (bf16[1,320,1280]{2,1,0:T(8,128)(2,1)}, bf16[1,320,1280]{2,1,0:T(8,128)(2,1)S(1)}, u32[]{:S(2)}) copy-start(bf16[1,320,1280]{2,1,0:T(8,128)(2,1)S(1)} %get-tuple-element.46.refs_7_) | copy-start | bytes 2457604
  129.4 4.5 %copy-start.5 = (bf16[1,320,1280]{2,1,0:T(8,128)(2,1)}, bf16[1,320,1280]{2,1,0:T(8,128)(2,1)S(1)}, u32[]{:S(2)}) copy-start(bf16[1,320,1280]{2,1,0:T(8,128)(2,1)S(1)} %get-tuple-element.47.refs_6_) | copy-start | bytes 2457604
  134.0 0.7 copy-start.26
  134.6 18.3 %all-to-all-start.5 = ((bf16[32,2,1280]{2,1,0:T(2,128)(2,1)}), bf16[32,2,1280]{2,1,0:T(2,128)(2,1)S(1)}, u32[]{:S(2)}, u32[]{:S(2)}) async-start(bf16[32,2,1280]{2,1,0:T(2,128)(2,1)} %copy-done.26), calls=%async_computation.5 | async-start | bytes 327680 | tf_op jit(solution)/shard_map/all_to_all | solution.py:270
  153.7 18.3 %all-to-all-start.6 = ((bf16[16,2,1280]{2,1,0:T(2,128)(2,1)}), bf16[16,2,1280]{2,1,0:T(2,128)(2,1)S(1)}, u32[]{:S(2)}, u32[]{:S(2)}) async-start(bf16[16,2,1280]{2,1,0:T(2,128)(2,1)} %shard_map.92), calls=%async_computation.6 | async-start | bytes 163840 | tf_op jit(solution)/shard_map/all_to_all | solution.py:270
  160.2 18.4 %collective-permute-start.5 = (bf16[64,1280]{1,0:T(8,128)(2,1)S(1)}, bf16[64,1280]{1,0:T(8,128)(2,1)S(1)}, u32[]{:S(2)}, u32[]{:S(2)}) collective-permute-start(bf16[64,1280]{1,0:T(8,128)(2,1)S(1)} %get-tuple-element.44.refs_2_), channel_id=1, source_target_pairs={{0,128},{128,0},{1,129},{129,1},{2,130},{130,2},{3,131},{131,3},{4... | collective-permute-start | bytes 491528 | tf_op jit(solution)/shard_map/ppermute | solution.py:266
  172.7 13.7 %all-to-all-start.7 = ((bf16[32,2,1280]{2,1,0:T(2,128)(2,1)}), bf16[32,2,1280]{2,1,0:T(2,128)(2,1)S(1)}, u32[]{:S(2)}, u32[]{:S(2)}) async-start(bf16[32,2,1280]{2,1,0:T(2,128)(2,1)} %shard_map.93), calls=%async_computation.7 | async-start | bytes 327680 | tf_op jit(solution)/shard_map/all_to_all | solution.py:270

commit v6 on v5

--- a/solution.py
+++ b/solution.py
@@ -22,19 +22,19 @@
 SMEM = pl.BlockSpec(memory_space=pltpu.SMEM)
 VMEM = pl.BlockSpec(memory_space=pltpu.VMEM)
 ANY = pl.BlockSpec(memory_space=pl.ANY)
-
-
-def call(kernel, outs, *operands, after=()):
-    body = kernel
-    if after:
-        first, last = len(operands), len(operands) + len(after)
-        body = lambda *refs: kernel(*refs[:first], *refs[last:])
-    bytes_accessed = sum(a.size * a.dtype.itemsize for a in list(operands) + list(outs))
+HBM = pl.BlockSpec(memory_space=pltpu.HBM)
+
+
+def call(kernel, outs, *operands, after=(), stored=(), after_spec=None):
+    first, last = len(operands), len(operands) + len(after)
+    body = (lambda *refs: kernel(*refs[:first], *refs[last:])) if after else kernel
+    bytes_accessed = sum(a.size * a.dtype.itemsize for a in (*operands, *outs, *stored))
     return pl.pallas_call(
         body,
-        out_shape=outs,
-        in_specs=[SMEM] + [VMEM] * (len(operands) - 1) + [ANY] * len(after),
-        out_specs=[VMEM] * len(outs),
+        out_shape=[*outs, *stored],
+        in_specs=[SMEM] + [VMEM] * (len(operands) - 1) + [after_spec or ANY] * len(after),
+        out_specs=[VMEM] * len(outs) + [HBM] * len(stored),
+        scratch_shapes=[pltpu.VMEM(a.shape, a.dtype) for a in stored] + [pltpu.SemaphoreType.DMA(())] * len(stored),
         compiler_params=pltpu.CompilerParams(vmem_limit_bytes=20 * 1024 * 1024),
         cost_estimate=pl.CostEstimate(flops=0, bytes_accessed=bytes_accessed, transcendentals=0),
     )(*operands, *after)
@@ -200,10 +200,18 @@
         expert(got, up_own, up_other, down_own, down_other, out, pre_grads, hiddens)
 
 
-def phase_5(where_am_i, got, kept, stats, tok_own, tok_b, grad_own, grad_b, out, tok, grad):
+def phase_5(
+    where_am_i, got, kept, stats, tok_a, tok_b, grad_a, grad_b, out, tok_store, grad_store, tok, grad, *done
+):
     core = where_am_i[0]
-    tok[:64], tok[64:] = tok_own[...], tok_b[core]
-    grad[:64], grad[64:] = grad_own[...], grad_b[core]
+    tok[:64], tok[64:] = tok_a[core], tok_b[core]
+    grad[:64], grad[64:] = grad_a[core], grad_b[core]
+    copies = [
+        pltpu.make_async_copy(source, target, done[k])
+        for k, (source, target) in enumerate(((tok, tok_store), (grad, grad_store)))
+    ]
+    for copy in copies:
+        copy.start()
 
     @pl.when(core == 0)
     def _():
@@ -212,6 +220,9 @@
     @pl.when(core == 1)
     def _():
         out[...] = got[...]
+
+    for copy in copies:
+        copy.wait()
 
 
 def weights_kernel(where_am_i, pre_3, hid_3, rows_3, pre_4, hid_4, rows_4, keep, send):
@@ -293,9 +304,9 @@
     got_1 = mixed(slots, PLANE, COLUMN)
     up_other, down_other = swap(up_proj[0]), swap(down_proj[0])
     weights = (up_proj[0], up_other, down_proj[0], down_other)
-    sent_2, kept_1, stats_1 = call(phase_2, [wide, *held], here, got_1, slots, after=(up_other, down_other))
+    sent_2, kept_1, stats_1 = call(phase_2, [wide, *held], here, got_1, slots, after=weights, after_spec=VMEM)
     got_2 = mixed(sent_2, COLUMN, PLANE)
-    sent_3, kept_0, stats_0, pre_1, hid_1 = call(phase_3, [wide, *held, *acts], here, got_2, *weights)
+    sent_3, kept_0, stats_0, pre_1, hid_1 = call(phase_3, [shaped((16, 2, 8, D), bf16), *held, *acts], here, got_2, *weights)
     got_3 = exchange(sent_3, PLANE)
     sent_4, pre_0, hid_0 = call(phase_4, [wide, *acts], here, got_3, kept_1, stats_1, *weights)
     got_4 = mixed(sent_4, PLANE, COLUMN)
@@ -306,8 +317,8 @@
     got_send = swap(send)
     up_grad, down_grad = ((keep[k : k + 1].astype(f32) + got_send[k : k + 1].astype(f32)).astype(bf16) for k in range(2))
     sent_5, tok, grad = call(
-        phase_5, [wide, shaped((LANES, D), bf16), shaped((LANES, D), bf16)],
-        here, got_4, kept_0, stats_0, tok_own, tok_b, grad_own, grad_b,
+        phase_5, [wide], here, got_4, kept_0, stats_0, tokens, tok_b, out_grad, grad_b,
+        stored=[shaped((LANES, D), bf16)] * 2,
     )
     got_5 = mixed(sent_5, COLUMN, PLANE)
     router_part, left, right = call(

time: 188 us -> 185 us (0.984)
  local copies, waits for them, and re-layouts: 8.66 us -> 5.48 us
    unnamed x54, local copies, waits for them, and re-layouts: 6.73 us -> 3.55 us
where the time goes in v6:
time: 185 us; the launch traced here: 184 us
  blocking collectives  60 us (32%)
  starting transfers between devices  56.4 us (30%)
  waiting for transfers between devices  46.7 us (25%)
  Pallas kernels  11.7 us (6%)
  local copies, waits for them, and re-layouts  5.48 us (3%)
  other arithmetic  2.35 us (1%)
    all_to_all x2, blocking collectives, mixed(): lax.all_to_all(value, ALL, split_axis=0, concat_axis=0, tiled=True, axis_...  47.6 us
    all_to_all x3, waiting for transfers between devices, exchange(): return lax.all_to_all(value, axes, split_axis=0, concat_axis=0, tiled=True)  23.6 us
    all_to_all x3, starting transfers between devices, exchange(): return lax.all_to_all(value, axes, split_axis=0, concat_axis=0, tiled=True)  22.8 us
    ppermute x6, starting transfers between devices, swap(): return lax.ppermute(value, 'core', [(0, 1), (1, 0)])  19.7 us
    all_to_all x2, waiting for transfers between devices, mixed(): lax.all_to_all(value, ALL, split_axis=0, concat_axis=0, tiled=True, axis_...  17.8 us
    all_to_all x2, starting transfers between devices, mixed(): lax.all_to_all(value, ALL, split_axis=0, concat_axis=0, tiled=True, axis_...  13.9 us
    all_to_all x1, blocking collectives, exchange(): return lax.all_to_all(value, axes, split_axis=0, concat_axis=0, tiled=True)  12.4 us
    pallas_call x10, Pallas kernels, call(): pl.pallas_call(body, out_shape=[*outs, *stored], in_specs=[SMEM] + [VMEM]...  11.7 us
  transfers between devices with their start and end apart: 11, of which 7 were waited for; matrix products, arithmetic and copies ran while one was open for 2% of the time, Pallas kernels for 1%

profile of v6, /device:TPU:1, one launch (start us, length us, event | category | flops | bytes accessed | tf_op | source)
XLA Modules:
  0.0 183.8 jit_solution(5057437660185525850)
XLA Ops:
  0.6 8.8 %collective-permute-start = (bf16[2,64,1280]{2,1,0:T(8,128)(2,1)}, bf16[2,64,1280]{2,1,0:T(8,128)(2,1)S(1)}, u32[]{:S(2)}, u32[]{:S(2)}) collective-permute-start(bf16[2,64,1280]{2,1,0:T(8,128)(2,1)} %tok_a.1), channel_id=1, source_target_pairs={{0,128},{128,0},{1,129},{129,1},{2,130},{130,2},{3,131},{131,3},{4... | collective-permute-start | bytes 983048 | tf_op jit(solution)/shard_map/ppermute | solution.py:277
  9.4 1.9 %collective-permute-start.1 = (bf16[2,64,1280]{2,1,0:T(8,128)(2,1)}, bf16[2,64,1280]{2,1,0:T(8,128)(2,1)S(1)}, u32[]{:S(2)}, u32[]{:S(2)}) collective-permute-start(bf16[2,64,1280]{2,1,0:T(8,128)(2,1)} %grad_a.1), channel_id=1, source_target_pairs={{0,128},{128,0},{1,129},{129,1},{2,130},{130,2},{3,131},{131,3},{4... | collective-permute-start | bytes 983048 | tf_op jit(solution)/shard_map/ppermute | solution.py:277
  11.4 1.0 reshape.25
  12.3 0.1 copy.11
  12.5 0.1 reshape.26.router_t.refs_1_
  12.5 1.2 select_bitcast_fusion
  13.8 0.0 copy-start.12
  13.8 1.6 shard_map.84.refs_2_
  15.4 9.6 %all-to-all-start = ((bf16[16,2,8,1408]{3,2,1,0:T(8,128)(2,1)}), bf16[16,2,8,1408]{3,2,1,0:T(8,128)(2,1)}, u32[]{:S(2)}, u32[]{:S(2)}) async-start(bf16[16,2,8,1408]{3,2,1,0:T(8,128)(2,1)} %shard_map.84.refs_2_), calls=%async_computation | async-start | bytes 1441792 | tf_op jit(solution)/shard_map/all_to_all | solution.py:288
  25.0 1.9 %collective-permute-start.2 = (bf16[320,1280]{1,0:T(8,128)(2,1)S(1)}, bf16[320,1280]{1,0:T(8,128)(2,1)S(1)}, u32[]{:S(2)}, u32[]{:S(2)}) collective-permute-start(bf16[320,1280]{1,0:T(8,128)(2,1)S(1)} %bitcast.14), channel_id=1, source_target_pairs={{0,128},{128,0},{1,129},{129,1},{2,130},{130,2},{3,131},{131,3},{4... | collective-permute-start | bytes 2457608 | tf_op jit(solution)/shard_map/ppermute | solution.py:277
  27.0 2.4 %collective-permute-start.3 = (bf16[320,1280]{1,0:T(8,128)(2,1)S(1)}, bf16[320,1280]{1,0:T(8,128)(2,1)S(1)}, u32[]{:S(2)}, u32[]{:S(2)}) collective-permute-start(bf16[320,1280]{1,0:T(8,128)(2,1)S(1)} %bitcast.18), channel_id=1, source_target_pairs={{0,128},{128,0},{1,129},{129,1},{2,130},{130,2},{3,131},{131,3},{4... | collective-permute-start | bytes 2457608 | tf_op jit(solution)/shard_map/ppermute | solution.py:277
  29.4 1.9 %collective-permute-done.3.refs_6_.down_other = bf16[320,1280]{1,0:T(8,128)(2,1)S(1)} collective-permute-done((bf16[320,1280]{1,0:T(8,128)(2,1)S(1)}, bf16[320,1280]{1,0:T(8,128)(2,1)S(1)}, u32[]{:S(2)}, u32[]{:S(2)}) %collective-permute-start.3) | collective-permute-done | bytes 819232 | tf_op jit(solution)/shard_map/ppermute | solution.py:277
  31.3 15.2 %all-to-all-done.refs_1_ = bf16[16,2,8,1408]{3,2,1,0:T(8,128)(2,1)} async-done(((bf16[16,2,8,1408]{3,2,1,0:T(8,128)(2,1)}), bf16[16,2,8,1408]{3,2,1,0:T(8,128)(2,1)}, u32[]{:S(2)}, u32[]{:S(2)}) %all-to-all-start) | async-done | bytes 720928 | tf_op jit(solution)/shard_map/all_to_all | solution.py:288
  46.5 1.9 %shard_map.85 = (bf16[16,2,8,1408]{3,2,1,0:T(8,128)(2,1)S(1)}, f32[128,1280]{1,0:T(8,128)S(1)}, f32[128,128]{1,0:T(8,128)S(1)}) custom-call(s32[1]{0:T(128)} %bitcast.where_am_i.refs_0_, bf16[16,2,8,1408]{3,2,1,0:T(8,128)(2,1)} %all-to-all-done.refs_1_, bf16[16,2,8,1408]{3,2,1,0:T(8,128)(2,1)} %shard_map.84.refs_2_, bf16[320,1280]{1,0:T(8,128)(2,1)S(1)} %bitcast.15, ...), custom_call_target="tpu_custom_call" | custom-call | bytes 2883588 | tf_op jit(solution)/shard_map/pallas_call | solution.py:32
  48.4 16.9 %all_to_all.40.got.rows_3 = bf16[16,2,8,1408]{3,2,1,0:T(8,128)(2,1)S(1)} all-to-all(bf16[16,2,8,1408]{3,2,1,0:T(8,128)(2,1)S(1)} %get-tuple-element.25), channel_id=1, replica_groups={{0,4,8,12,16,20,24,28,256,260,264,268,272,276,280,284},{1,5,9,13,17,21,..., dimensions={0} | all-to-all | bytes 1441792 | tf_op jit(solution)/shard_map/all_to_all | solution.py:288
  65.3 1.9 %shard_map.86 = (bf16[16,2,8,1280]{3,2,1,0:T(8,128)(2,1)S(1)}, f32[128,1280]{1,0:T(8,128)S(1)}, f32[128,128]{1,0:T(8,128)S(1)}, bf16[2,320,128]{2,1,0:T(8,128)(2,1)S(1)}, bf16[2,320,128]{2,1,0:T(8,128)(2,1)S(1)}) custom-call(s32[1]{0:T(128)} %bitcast.where_am_i.refs_0_, bf16[16,2,8,1408]{3,2,1,0:T(8,128)(2,1)S(1)} %all_to_all.40.got.rows_3, ...), custom_call_target="tpu_custom_call" | custom-call | bytes 5701636 | tf_op jit(solution)/shard_map/pallas_call | solution.py:32
  67.2 12.4 %all_to_all.41.got.rows_4 = bf16[16,2,8,1280]{3,2,1,0:T(8,128)(2,1)S(1)} all-to-all(bf16[16,2,8,1280]{3,2,1,0:T(8,128)(2,1)S(1)} %get-tuple-element.26), channel_id=1, replica_groups=mesh['zh'=2,'core'=2,'y'=4,'zl'=8,'xh'=2,'xl'=2] {'y','xh','xl'}, dimensions={0} | all-to-all | bytes 1310720 | tf_op jit(solution)/shard_map/all_to_all | solution.py:281
  79.6 0.4 shard_map.87
  80.0 0.4 copy-done.4
  80.5 0.0 copy-start.11
  80.5 0.0 copy-start.13
  80.5 30.7 %all_to_all.42.got.refs_4_ = bf16[16,2,8,1408]{3,2,1,0:T(8,128)(2,1)S(1)} all-to-all(bf16[16,2,8,1408]{3,2,1,0:T(8,128)(2,1)S(1)} %get-tuple-element.29), channel_id=1, replica_groups={{0,1,2,3,32,33,34,35,64,65,66,67,96,97,98,99},{4,5,6,7,36,37,38,39,68,6..., dimensions={0} | all-to-all | bytes 1441792 | tf_op jit(solution)/shard_map/all_to_all | solution.py:288
  111.3 1.2 shard_map.88
  112.5 0.0 copy-start.14
  112.5 0.7 copy-done.14
  113.2 0.7 copy-done.16
  113.9 4.3 %all-to-all-start.4 = ((bf16[16,2,8,1408]{3,2,1,0:T(8,128)(2,1)}), bf16[16,2,8,1408]{3,2,1,0:T(8,128)(2,1)}, u32[]{:S(2)}, u32[]{:S(2)}) async-start(bf16[16,2,8,1408]{3,2,1,0:T(8,128)(2,1)} %get-tuple-element.34), calls=%async_computation.4 | async-start | bytes 1441792 | tf_op jit(solution)/shard_map/all_to_all | solution.py:288
  118.3 0.9 copy-done.23
  119.2 1.0 shard_map.89
  120.2 1.9 %collective-permute-start.4 = (bf16[2,320,1280]{2,1,0:T(8,128)(2,1)S(1)}, bf16[2,320,1280]{2,1,0:T(8,128)(2,1)S(1)}, u32[]{:S(2)}, u32[]{:S(2)}) collective-permute-start(bf16[2,320,1280]{2,1,0:T(8,128)(2,1)S(1)} %get-tuple-element.40), channel_id=1, source_target_pairs={{0,128},{128,0},{1,129},{129,1},{2,130},{130,2},{3,131},{131,3},{4... | collective-permute-start | bytes 4915208 | tf_op jit(solution)/shard_map/ppermute | solution.py:277
  122.1 3.5 %collective-permute-done.4 = bf16[2,320,1280]{2,1,0:T(8,128)(2,1)S(1)} collective-permute-done((bf16[2,320,1280]{2,1,0:T(8,128)(2,1)S(1)}, bf16[2,320,1280]{2,1,0:T(8,128)(2,1)S(1)}, u32[]{:S(2)}, u32[]{:S(2)}) %collective-permute-start.4) | collective-permute-done | bytes 1638432 | tf_op jit(solution)/shard_map/ppermute | solution.py:277
  125.6 0.4 add_convert_fusion
  126.0 0.0 copy-start.6
  126.0 2.5 %all-to-all-done.4.refs_5_ = bf16[16,2,8,1408]{3,2,1,0:T(8,128)(2,1)} async-done(((bf16[16,2,8,1408]{3,2,1,0:T(8,128)(2,1)}), bf16[16,2,8,1408]{3,2,1,0:T(8,128)(2,1)}, u32[]{:S(2)}, u32[]{:S(2)}) %all-to-all-start.4) | async-done | bytes 720928 | tf_op jit(solution)/shard_map/all_to_all | solution.py:288
  128.6 1.9 %shard_map.90 = (bf16[32,2,1280]{2,1,0:T(2,128)(2,1)S(1)}, bf16[128,128]{1,0:T(8,128)(2,1)S(1)}, bf16[64,1280]{1,0:T(8,128)(2,1)S(1)}) custom-call(s32[1]{0:T(128)} %bitcast.where_am_i.refs_0_, bf16[64,1280]{1,0:T(8,128)(2,1)S(1)} %reshape.26.router_t.refs_1_, bf16[128,1280]{1,0:T(8,128)(2,1)S(1)} %copy-done.15, bf16[128,1280]{1,0:T(8,128)(2,1)S(1)} %copy-done.17, ...), custom_call_target="tpu_custom_call" | custom-call | bytes 2621444 | tf_op jit(solution)/shard_map/pallas_call | solution.py:32
  130.6 0.7 copy-done.26
  131.2 10.5 %all-to-all-start.5 = ((bf16[32,2,1280]{2,1,0:T(2,128)(2,1)}), bf16[32,2,1280]{2,1,0:T(2,128)(2,1)S(1)}, u32[]{:S(2)}, u32[]{:S(2)}) async-start(bf16[32,2,1280]{2,1,0:T(2,128)(2,1)} %copy-done.26), calls=%async_computation.5 | async-start | bytes 327680 | tf_op jit(solution)/shard_map/all_to_all | solution.py:281
  141.8 0.3 shard_map.91
  142.1 7.5 %all-to-all-done.5.refs_1_ = bf16[32,2,1280]{2,1,0:T(2,128)(2,1)S(1)} async-done(((bf16[32,2,1280]{2,1,0:T(2,128)(2,1)}), bf16[32,2,1280]{2,1,0:T(2,128)(2,1)S(1)}, u32[]{:S(2)}, u32[]{:S(2)}) %all-to-all-start.5) | async-done | bytes 163872 | tf_op jit(solution)/shard_map/all_to_all | solution.py:281
  149.6 0.8 shard_map.92
  150.4 6.5 %all-to-all-start.6 = ((bf16[16,2,1280]{2,1,0:T(2,128)(2,1)}), bf16[16,2,1280]{2,1,0:T(2,128)(2,1)S(1)}, u32[]{:S(2)}, u32[]{:S(2)}) async-start(bf16[16,2,1280]{2,1,0:T(2,128)(2,1)} %shard_map.92), calls=%async_computation.6 | async-start | bytes 163840 | tf_op jit(solution)/shard_map/all_to_all | solution.py:281
  156.8 2.8 %collective-permute-start.5 = (bf16[64,1280]{1,0:T(8,128)(2,1)S(1)}, bf16[64,1280]{1,0:T(8,128)(2,1)S(1)}, u32[]{:S(2)}, u32[]{:S(2)}) collective-permute-start(bf16[64,1280]{1,0:T(8,128)(2,1)S(1)} %get-tuple-element.44.refs_2_), channel_id=1, source_target_pairs={{0,128},{128,0},{1,129},{129,1},{2,130},{130,2},{3,131},{131,3},{4... | collective-permute-start | bytes 491528 | tf_op jit(solution)/shard_map/ppermute | solution.py:277
  159.6 9.0 %all-to-all-done.6.got = bf16[16,2,1280]{2,1,0:T(2,128)(2,1)S(1)} async-done(((bf16[16,2,1280]{2,1,0:T(2,128)(2,1)}), bf16[16,2,1280]{2,1,0:T(2,128)(2,1)S(1)}, u32[]{:S(2)}, u32[]{:S(2)}) %all-to-all-start.6) | async-done | bytes 81952 | tf_op jit(solution)/shard_map/all_to_all | solution.py:281
  168.6 0.8 shard_map.93
  169.4 5.8 %all-to-all-start.7 = ((bf16[32,2,1280]{2,1,0:T(2,128)(2,1)}), bf16[32,2,1280]{2,1,0:T(2,128)(2,1)S(1)}, u32[]{:S(2)}, u32[]{:S(2)}) async-start(bf16[32,2,1280]{2,1,0:T(2,128)(2,1)} %shard_map.93), calls=%async_computation.7 | async-start | bytes 327680 | tf_op jit(solution)/shard_map/all_to_all | solution.py:281
  175.3 0.8 maximum_select_fusion
  176.0 7.0 %all-to-all-done.7 = bf16[32,2,1280]{2,1,0:T(2,128)(2,1)S(1)} async-done(((bf16[32,2,1280]{2,1,0:T(2,128)(2,1)}), bf16[32,2,1280]{2,1,0:T(2,128)(2,1)S(1)}, u32[]{:S(2)}, u32[]{:S(2)}) %all-to-all-start.7) | async-done | bytes 163872 | tf_op jit(solution)/shard_map/all_to_all | solution.py:281
  183.1 0.8 reshape.27
  (48 shorter events, 0.1 us)
Async XLA Ops:
  0.6 13.1 %collective-permute-start = (bf16[2,64,1280]{2,1,0:T(8,128)(2,1)}, bf16[2,64,1280]{2,1,0:T(8,128)(2,1)S(1)}, u32[]{:S(2)}, u32[]{:S(2)}) collective-permute-start(bf16[2,64,1280]{2,1,0:T(8,128)(2,1)} %tok_a.1), channel_id=1, source_target_pairs={{0,128},{128,0},{1,129},{129,1},{2,130},{130,2},{3,131},{131,3},{4... | collective-permute-start | bytes 983048 | tf_op jit(solution)/shard_map/ppermute | solution.py:277
  9.4 4.3 %collective-permute-start.1 = (bf16[2,64,1280]{2,1,0:T(8,128)(2,1)}, bf16[2,64,1280]{2,1,0:T(8,128)(2,1)S(1)}, u32[]{:S(2)}, u32[]{:S(2)}) collective-permute-start(bf16[2,64,1280]{2,1,0:T(8,128)(2,1)} %grad_a.1), channel_id=1, source_target_pairs={{0,128},{128,0},{1,129},{129,1},{2,130},{130,2},{3,131},{131,3},{4... | collective-permute-start | bytes 983048 | tf_op jit(solution)/shard_map/ppermute | solution.py:277
  13.8 1.7 copy-start.10
  13.8 1.6 copy-start.12
  13.8 11.2 %copy-start = (bf16[1,320,1280]{2,1,0:T(8,128)(2,1)S(1)}, bf16[1,320,1280]{2,1,0:T(8,128)(2,1)}, u32[]{:S(2)}) copy-start(bf16[1,320,1280]{2,1,0:T(8,128)(2,1)} %param.7) | copy-start | bytes 2457604
  13.8 13.2 %copy-start.1 = (bf16[1,320,1280]{2,1,0:T(8,128)(2,1)S(1)}, bf16[1,320,1280]{2,1,0:T(8,128)(2,1)}, u32[]{:S(2)}) copy-start(bf16[1,320,1280]{2,1,0:T(8,128)(2,1)} %param.8) | copy-start | bytes 2457604
  15.4 31.1 %all-to-all-start = ((bf16[16,2,8,1408]{3,2,1,0:T(8,128)(2,1)}), bf16[16,2,8,1408]{3,2,1,0:T(8,128)(2,1)}, u32[]{:S(2)}, u32[]{:S(2)}) async-start(bf16[16,2,8,1408]{3,2,1,0:T(8,128)(2,1)} %shard_map.84.refs_2_), calls=%async_computation | async-start | bytes 1441792 | tf_op jit(solution)/shard_map/all_to_all | solution.py:288
  25.0 4.4 %collective-permute-start.2 = (bf16[320,1280]{1,0:T(8,128)(2,1)S(1)}, bf16[320,1280]{1,0:T(8,128)(2,1)S(1)}, u32[]{:S(2)}, u32[]{:S(2)}) collective-permute-start(bf16[320,1280]{1,0:T(8,128)(2,1)S(1)} %bitcast.14), channel_id=1, source_target_pairs={{0,128},{128,0},{1,129},{129,1},{2,130},{130,2},{3,131},{131,3},{4... | collective-permute-start | bytes 2457608 | tf_op jit(solution)/shard_map/ppermute | solution.py:277
  27.0 4.4 %collective-permute-start.3 = (bf16[320,1280]{1,0:T(8,128)(2,1)S(1)}, bf16[320,1280]{1,0:T(8,128)(2,1)S(1)}, u32[]{:S(2)}, u32[]{:S(2)}) collective-permute-start(bf16[320,1280]{1,0:T(8,128)(2,1)S(1)} %bitcast.18), channel_id=1, source_target_pairs={{0,128},{128,0},{1,129},{129,1},{2,130},{130,2},{3,131},{131,3},{4... | collective-permute-start | bytes 2457608 | tf_op jit(solution)/shard_map/ppermute | solution.py:277
  65.3 1.9 %copy-start.2 = (bf16[16,2,8,1408]{3,2,1,0:T(8,128)(2,1)}, bf16[16,2,8,1408]{3,2,1,0:T(8,128)(2,1)S(1)}, u32[]{:S(2)}) copy-start(bf16[16,2,8,1408]{3,2,1,0:T(8,128)(2,1)S(1)} %all_to_all.40.got.rows_3) | copy-start | bytes 2162692
  67.2 12.4 %copy-start.18 = (bf16[2,320,128]{2,1,0:T(8,128)(2,1)}, bf16[2,320,128]{2,1,0:T(8,128)(2,1)S(1)}, u32[]{:S(2)}) copy-start(bf16[2,320,128]{2,1,0:T(8,128)(2,1)S(1)} %get-tuple-element.35.pre_3) | copy-start | bytes 491524
  67.2 12.8 %copy-start.20 = (bf16[2,320,128]{2,1,0:T(8,128)(2,1)}, bf16[2,320,128]{2,1,0:T(8,128)(2,1)S(1)}, u32[]{:S(2)}) copy-start(bf16[2,320,128]{2,1,0:T(8,128)(2,1)S(1)} %get-tuple-element.36.hid_3) | copy-start | bytes 491524
  79.6 0.8 copy-start.4
  80.5 30.7 %copy-start.24 = (bf16[2,320,128]{2,1,0:T(8,128)(2,1)}, bf16[2,320,128]{2,1,0:T(8,128)(2,1)S(1)}, u32[]{:S(2)}) copy-start(bf16[2,320,128]{2,1,0:T(8,128)(2,1)S(1)} %get-tuple-element.38.hid_4) | copy-start | bytes 491524
  80.5 32.0 %copy-start.22 = (bf16[2,320,128]{2,1,0:T(8,128)(2,1)}, bf16[2,320,128]{2,1,0:T(8,128)(2,1)S(1)}, u32[]{:S(2)}) copy-start(bf16[2,320,128]{2,1,0:T(8,128)(2,1)S(1)} %get-tuple-element.37.pre_4) | copy-start | bytes 491524
  80.5 30.7 %copy-start.8 = (bf16[2,64,1280]{2,1,0:T(8,128)(2,1)S(1)}, bf16[2,64,1280]{2,1,0:T(8,128)(2,1)}, u32[]{:S(2)}) copy-start(bf16[2,64,1280]{2,1,0:T(8,128)(2,1)} %grad_a.1) | copy-start | bytes 983044
  80.5 30.7 %copy-start.9 = (bf16[2,64,1280]{2,1,0:T(8,128)(2,1)S(1)}, bf16[2,64,1280]{2,1,0:T(8,128)(2,1)}, u32[]{:S(2)}) copy-start(bf16[2,64,1280]{2,1,0:T(8,128)(2,1)} %tok_a.1) | copy-start | bytes 983044
  80.5 30.7 %copy-start.11 = (bf16[2,64,1280]{2,1,0:T(8,128)(2,1)S(1)}, bf16[2,64,1280]{2,1,0:T(8,128)(2,1)}, u32[]{:S(2)}) copy-start(bf16[2,64,1280]{2,1,0:T(8,128)(2,1)} %copy-done.10) | copy-start | bytes 983044
  80.5 30.7 %copy-start.13 = (bf16[2,64,1280]{2,1,0:T(8,128)(2,1)S(1)}, bf16[2,64,1280]{2,1,0:T(8,128)(2,1)}, u32[]{:S(2)}) copy-start(bf16[2,64,1280]{2,1,0:T(8,128)(2,1)} %copy-done.12) | copy-start | bytes 983044
  111.2 7.0 %copy-start.3 = (bf16[16,2,8,1408]{3,2,1,0:T(8,128)(2,1)S(1)}, bf16[16,2,8,1408]{3,2,1,0:T(8,128)(2,1)}, u32[]{:S(2)}) copy-start(bf16[16,2,8,1408]{3,2,1,0:T(8,128)(2,1)} %copy-done.2) | copy-start | bytes 2162692
  111.2 7.0 %copy-start.5 = (bf16[16,2,8,1280]{3,2,1,0:T(8,128)(2,1)S(1)}, bf16[16,2,8,1280]{3,2,1,0:T(8,128)(2,1)}, u32[]{:S(2)}) copy-start(bf16[16,2,8,1280]{3,2,1,0:T(8,128)(2,1)} %copy-done.4) | copy-start | bytes 1966084
  111.2 7.0 %copy-start.19 = (bf16[2,320,128]{2,1,0:T(8,128)(2,1)S(1)}, bf16[2,320,128]{2,1,0:T(8,128)(2,1)}, u32[]{:S(2)}) copy-start(bf16[2,320,128]{2,1,0:T(8,128)(2,1)} %copy-done.18) | copy-start | bytes 491524
  111.3 7.0 %copy-start.21 = (bf16[2,320,128]{2,1,0:T(8,128)(2,1)S(1)}, bf16[2,320,128]{2,1,0:T(8,128)(2,1)}, u32[]{:S(2)}) copy-start(bf16[2,320,128]{2,1,0:T(8,128)(2,1)} %copy-done.20) | copy-start | bytes 491524
  111.3 7.0 %copy-start.25 = (bf16[2,320,128]{2,1,0:T(8,128)(2,1)S(1)}, bf16[2,320,128]{2,1,0:T(8,128)(2,1)}, u32[]{:S(2)}) copy-start(bf16[2,320,128]{2,1,0:T(8,128)(2,1)} %copy-done.24) | copy-start | bytes 491524
  112.5 0.7 copy-start.14
  113.2 0.7 copy-start.16
  113.9 14.6 %all-to-all-start.4 = ((bf16[16,2,8,1408]{3,2,1,0:T(8,128)(2,1)}), bf16[16,2,8,1408]{3,2,1,0:T(8,128)(2,1)}, u32[]{:S(2)}, u32[]{:S(2)}) async-start(bf16[16,2,8,1408]{3,2,1,0:T(8,128)(2,1)} %get-tuple-element.34), calls=%async_computation.4 | async-start | bytes 1441792 | tf_op jit(solution)/shard_map/all_to_all | solution.py:288
  118.3 0.9 copy-start.23
  120.2 5.4 %collective-permute-start.4 = (bf16[2,320,1280]{2,1,0:T(8,128)(2,1)S(1)}, bf16[2,320,1280]{2,1,0:T(8,128)(2,1)S(1)}, u32[]{:S(2)}, u32[]{:S(2)}) collective-permute-start(bf16[2,320,1280]{2,1,0:T(8,128)(2,1)S(1)} %get-tuple-element.40), channel_id=1, source_target_pairs={{0,128},{128,0},{1,129},{129,1},{2,130},{130,2},{3,131},{131,3},{4... | collective-permute-start | bytes 4915208 | tf_op jit(solution)/shard_map/ppermute | solution.py:277
  125.6 3.0 %copy-start.15 = (bf16[128,1280]{1,0:T(8,128)(2,1)S(1)}, bf16[128,1280]{1,0:T(8,128)(2,1)}, u32[]{:S(2)}) copy-start(bf16[128,1280]{1,0:T(8,128)(2,1)} %copy-done.14) | copy-start | bytes 983044
  125.6 3.0 %copy-start.17 = (bf16[128,1280]{1,0:T(8,128)(2,1)S(1)}, bf16[128,1280]{1,0:T(8,128)(2,1)}, u32[]{:S(2)}) copy-start(bf16[128,1280]{1,0:T(8,128)(2,1)} %copy-done.16) | copy-start | bytes 983044
  126.0 4.5 %copy-start.6 = (bf16[1,320,1280]{2,1,0:T(8,128)(2,1)}, bf16[1,320,1280]{2,1,0:T(8,128)(2,1)S(1)}, u32[]{:S(2)}) copy-start(bf16[1,320,1280]{2,1,0:T(8,128)(2,1)S(1)} %get-tuple-element.46.refs_7_) | copy-start | bytes 2457604
  126.0 4.5 %copy-start.7 = (bf16[1,320,1280]{2,1,0:T(8,128)(2,1)}, bf16[1,320,1280]{2,1,0:T(8,128)(2,1)S(1)}, u32[]{:S(2)}) copy-start(bf16[1,320,1280]{2,1,0:T(8,128)(2,1)S(1)} %get-tuple-element.47.refs_6_) | copy-start | bytes 2457604
  130.6 0.7 copy-start.26
  131.2 18.4 %all-to-all-start.5 = ((bf16[32,2,1280]{2,1,0:T(2,128)(2,1)}), bf16[32,2,1280]{2,1,0:T(2,128)(2,1)S(1)}, u32[]{:S(2)}, u32[]{:S(2)}) async-start(bf16[32,2,1280]{2,1,0:T(2,128)(2,1)} %copy-done.26), calls=%async_computation.5 | async-start | bytes 327680 | tf_op jit(solution)/shard_map/all_to_all | solution.py:281
  150.4 18.3 %all-to-all-start.6 = ((bf16[16,2,1280]{2,1,0:T(2,128)(2,1)}), bf16[16,2,1280]{2,1,0:T(2,128)(2,1)S(1)}, u32[]{:S(2)}, u32[]{:S(2)}) async-start(bf16[16,2,1280]{2,1,0:T(2,128)(2,1)} %shard_map.92), calls=%async_computation.6 | async-start | bytes 163840 | tf_op jit(solution)/shard_map/all_to_all | solution.py:281
  156.8 18.4 %collective-permute-start.5 = (bf16[64,1280]{1,0:T(8,128)(2,1)S(1)}, bf16[64,1280]{1,0:T(8,128)(2,1)S(1)}, u32[]{:S(2)}, u32[]{:S(2)}) collective-permute-start(bf16[64,1280]{1,0:T(8,128)(2,1)S(1)} %get-tuple-element.44.refs_2_), channel_id=1, source_target_pairs={{0,128},{128,0},{1,129},{129,1},{2,130},{130,2},{3,131},{131,3},{4... | collective-permute-start | bytes 491528 | tf_op jit(solution)/shard_map/ppermute | solution.py:277
  169.4 13.7 %all-to-all-start.7 = ((bf16[32,2,1280]{2,1,0:T(2,128)(2,1)}), bf16[32,2,1280]{2,1,0:T(2,128)(2,1)S(1)}, u32[]{:S(2)}, u32[]{:S(2)}) async-start(bf16[32,2,1280]{2,1,0:T(2,128)(2,1)} %shard_map.93), calls=%async_computation.7 | async-start | bytes 327680 | tf_op jit(solution)/shard_map/all_to_all | solution.py:281

commit v7 on v6

--- a/solution.py
+++ b/solution.py
@@ -331,7 +331,7 @@
     )
     got_grad = swap(sent_grad)
     (part,) = call(
-        spread_kernel, [shaped((16, 2, D), bf16)], here, exchange(router_part, PLANE_CORES), after=(sent_grad,)
+        spread_kernel, [shaped((16, 2, D), bf16)], here, exchange(router_part, PLANE_CORES)
     )
     (whole,) = call(spread_kernel, [shaped((32, 2, D), bf16)], here, exchange(part, COLUMN))
     full = exchange(whole, PLANE_CORES).reshape(SLOTS, D)

time: 185 us -> 183 us (0.989)
  blocking collectives: 60 us -> 77.8 us
  starting transfers between devices: 56.4 us -> 45.8 us
  waiting for transfers between devices: 46.7 us -> 39 us
    all_to_all x1 -> x2, blocking collectives: 12.4 us -> 30.2 us  [exchange(): return lax.all_to_all(value, axes, split_axis=0, concat_axis=0, tiled=True)]
    all_to_all x3 -> x2, starting transfers between devices: 22.8 us -> 12.3 us  [exchange(): return lax.all_to_all(value, axes, split_axis=0, concat_axis=0, tiled=True)]
    all_to_all x3 -> x2, waiting for transfers between devices: 23.6 us -> 15.8 us  [exchange(): return lax.all_to_all(value, axes, split_axis=0, concat_axis=0, tiled=True)]
  transfers between devices with their start and end apart: 11 -> 10, of which waited for: 7 -> 6; matrix products, arithmetic and copies ran while one was open for 2% -> 2% of each run, Pallas kernels for 1% -> 1%
where the time goes in v7:
time: 183 us
  blocking collectives  77.8 us (43%)
  starting transfers between devices  45.8 us (25%)
  waiting for transfers between devices  39 us (21%)
  Pallas kernels  11.7 us (6%)
  local copies, waits for them, and re-layouts  4.82 us (3%)
  other arithmetic  2.35 us (1%)
    all_to_all x2, blocking collectives, mixed(): lax.all_to_all(value, ALL, split_axis=0, concat_axis=0, tiled=True, axis_...  47.6 us
    all_to_all x2, blocking collectives, exchange(): return lax.all_to_all(value, axes, split_axis=0, concat_axis=0, tiled=True)  30.2 us
    ppermute x6, starting transfers between devices, swap(): return lax.ppermute(value, 'core', [(0, 1), (1, 0)])  19.7 us
    all_to_all x2, waiting for transfers between devices, mixed(): lax.all_to_all(value, ALL, split_axis=0, concat_axis=0, tiled=True, axis_...  17.8 us
    all_to_all x2, waiting for transfers between devices, exchange(): return lax.all_to_all(value, axes, split_axis=0, concat_axis=0, tiled=True)  15.8 us
    all_to_all x2, starting transfers between devices, mixed(): lax.all_to_all(value, ALL, split_axis=0, concat_axis=0, tiled=True, axis_...  13.9 us
    all_to_all x2, starting transfers between devices, exchange(): return lax.all_to_all(value, axes, split_axis=0, concat_axis=0, tiled=True)  12.3 us
    pallas_call x10, Pallas kernels, call(): pl.pallas_call(body, out_shape=[*outs, *stored], in_specs=[SMEM] + [VMEM]...  11.7 us
  transfers between devices with their start and end apart: 10, of which 6 were waited for; matrix products, arithmetic and copies ran while one was open for 2% of the time, Pallas kernels for 1%

profile of v7, /device:TPU:1, one launch (start us, length us, event | category | flops | bytes accessed | tf_op | source)
XLA Modules:
  0.0 182.6 jit_solution(9475112870352174089)
XLA Ops:
  0.6 8.8 %collective-permute-start = (bf16[2,64,1280]{2,1,0:T(8,128)(2,1)}, bf16[2,64,1280]{2,1,0:T(8,128)(2,1)S(1)}, u32[]{:S(2)}, u32[]{:S(2)}) collective-permute-start(bf16[2,64,1280]{2,1,0:T(8,128)(2,1)} %tok_a.1), channel_id=1, source_target_pairs={{0,128},{128,0},{1,129},{129,1},{2,130},{130,2},{3,131},{131,3},{4... | collective-permute-start | bytes 983048 | tf_op jit(solution)/shard_map/ppermute | solution.py:277
  9.4 1.9 %collective-permute-start.1 = (bf16[2,64,1280]{2,1,0:T(8,128)(2,1)}, bf16[2,64,1280]{2,1,0:T(8,128)(2,1)S(1)}, u32[]{:S(2)}, u32[]{:S(2)}) collective-permute-start(bf16[2,64,1280]{2,1,0:T(8,128)(2,1)} %grad_a.1), channel_id=1, source_target_pairs={{0,128},{128,0},{1,129},{129,1},{2,130},{130,2},{3,131},{131,3},{4... | collective-permute-start | bytes 983048 | tf_op jit(solution)/shard_map/ppermute | solution.py:277
  11.4 1.0 reshape.25
  12.3 0.1 copy.11
  12.5 0.1 reshape.26.router_t.refs_1_
  12.5 1.2 select_bitcast_fusion
  13.8 0.0 copy-start.10
  13.8 0.0 copy-start.12
  13.8 0.0 copy-start.1
  13.8 1.6 shard_map.84.refs_2_
  15.4 9.6 %all-to-all-start = ((bf16[16,2,8,1408]{3,2,1,0:T(8,128)(2,1)}), bf16[16,2,8,1408]{3,2,1,0:T(8,128)(2,1)}, u32[]{:S(2)}, u32[]{:S(2)}) async-start(bf16[16,2,8,1408]{3,2,1,0:T(8,128)(2,1)} %shard_map.84.refs_2_), calls=%async_computation | async-start | bytes 1441792 | tf_op jit(solution)/shard_map/all_to_all | solution.py:288
  25.0 1.9 %collective-permute-start.2 = (bf16[320,1280]{1,0:T(8,128)(2,1)S(1)}, bf16[320,1280]{1,0:T(8,128)(2,1)S(1)}, u32[]{:S(2)}, u32[]{:S(2)}) collective-permute-start(bf16[320,1280]{1,0:T(8,128)(2,1)S(1)} %bitcast.14), channel_id=1, source_target_pairs={{0,128},{128,0},{1,129},{129,1},{2,130},{130,2},{3,131},{131,3},{4... | collective-permute-start | bytes 2457608 | tf_op jit(solution)/shard_map/ppermute | solution.py:277
  27.0 2.4 %collective-permute-start.3 = (bf16[320,1280]{1,0:T(8,128)(2,1)S(1)}, bf16[320,1280]{1,0:T(8,128)(2,1)S(1)}, u32[]{:S(2)}, u32[]{:S(2)}) collective-permute-start(bf16[320,1280]{1,0:T(8,128)(2,1)S(1)} %bitcast.18), channel_id=1, source_target_pairs={{0,128},{128,0},{1,129},{129,1},{2,130},{130,2},{3,131},{131,3},{4... | collective-permute-start | bytes 2457608 | tf_op jit(solution)/shard_map/ppermute | solution.py:277
  29.4 1.9 %collective-permute-done.3.refs_6_.down_other = bf16[320,1280]{1,0:T(8,128)(2,1)S(1)} collective-permute-done((bf16[320,1280]{1,0:T(8,128)(2,1)S(1)}, bf16[320,1280]{1,0:T(8,128)(2,1)S(1)}, u32[]{:S(2)}, u32[]{:S(2)}) %collective-permute-start.3) | collective-permute-done | bytes 819232 | tf_op jit(solution)/shard_map/ppermute | solution.py:277
  31.3 15.2 %all-to-all-done.refs_1_ = bf16[16,2,8,1408]{3,2,1,0:T(8,128)(2,1)} async-done(((bf16[16,2,8,1408]{3,2,1,0:T(8,128)(2,1)}), bf16[16,2,8,1408]{3,2,1,0:T(8,128)(2,1)}, u32[]{:S(2)}, u32[]{:S(2)}) %all-to-all-start) | async-done | bytes 720928 | tf_op jit(solution)/shard_map/all_to_all | solution.py:288
  46.5 1.9 %shard_map.85 = (bf16[16,2,8,1408]{3,2,1,0:T(8,128)(2,1)S(1)}, f32[128,1280]{1,0:T(8,128)S(1)}, f32[128,128]{1,0:T(8,128)S(1)}) custom-call(s32[1]{0:T(128)} %bitcast.where_am_i.refs_0_, bf16[16,2,8,1408]{3,2,1,0:T(8,128)(2,1)} %all-to-all-done.refs_1_, bf16[16,2,8,1408]{3,2,1,0:T(8,128)(2,1)} %shard_map.84.refs_2_, bf16[320,1280]{1,0:T(8,128)(2,1)S(1)} %bitcast.15, ...), custom_call_target="tpu_custom_call" | custom-call | bytes 2883588 | tf_op jit(solution)/shard_map/pallas_call | solution.py:32
  48.4 16.9 %all_to_all.40.got.rows_3 = bf16[16,2,8,1408]{3,2,1,0:T(8,128)(2,1)S(1)} all-to-all(bf16[16,2,8,1408]{3,2,1,0:T(8,128)(2,1)S(1)} %get-tuple-element.25), channel_id=1, replica_groups={{0,4,8,12,16,20,24,28,256,260,264,268,272,276,280,284},{1,5,9,13,17,21,..., dimensions={0} | all-to-all | bytes 1441792 | tf_op jit(solution)/shard_map/all_to_all | solution.py:288
  65.3 1.9 %shard_map.86 = (bf16[16,2,8,1280]{3,2,1,0:T(8,128)(2,1)S(1)}, f32[128,1280]{1,0:T(8,128)S(1)}, f32[128,128]{1,0:T(8,128)S(1)}, bf16[2,320,128]{2,1,0:T(8,128)(2,1)S(1)}, bf16[2,320,128]{2,1,0:T(8,128)(2,1)S(1)}) custom-call(s32[1]{0:T(128)} %bitcast.where_am_i.refs_0_, bf16[16,2,8,1408]{3,2,1,0:T(8,128)(2,1)S(1)} %all_to_all.40.got.rows_3, ...), custom_call_target="tpu_custom_call" | custom-call | bytes 5701636 | tf_op jit(solution)/shard_map/pallas_call | solution.py:32
  67.2 12.4 %all_to_all.41.got.rows_4 = bf16[16,2,8,1280]{3,2,1,0:T(8,128)(2,1)S(1)} all-to-all(bf16[16,2,8,1280]{3,2,1,0:T(8,128)(2,1)S(1)} %get-tuple-element.26), channel_id=1, replica_groups=mesh['zh'=2,'core'=2,'y'=4,'zl'=8,'xh'=2,'xl'=2] {'y','xh','xl'}, dimensions={0} | all-to-all | bytes 1310720 | tf_op jit(solution)/shard_map/all_to_all | solution.py:281
  79.6 0.4 shard_map.87
  80.0 0.4 copy-done.4
  80.5 0.0 copy-start.11
  80.5 0.0 copy-start.13
  80.5 30.7 %all_to_all.42.got.refs_4_ = bf16[16,2,8,1408]{3,2,1,0:T(8,128)(2,1)S(1)} all-to-all(bf16[16,2,8,1408]{3,2,1,0:T(8,128)(2,1)S(1)} %get-tuple-element.29), channel_id=1, replica_groups={{0,1,2,3,32,33,34,35,64,65,66,67,96,97,98,99},{4,5,6,7,36,37,38,39,68,6..., dimensions={0} | all-to-all | bytes 1441792 | tf_op jit(solution)/shard_map/all_to_all | solution.py:288
  111.2 0.0 copy-start.5
  111.3 1.2 shard_map.88
  112.5 0.7 copy-done.14
  113.2 0.7 copy-done.16
  113.9 4.3 %all-to-all-start.4 = ((bf16[16,2,8,1408]{3,2,1,0:T(8,128)(2,1)}), bf16[16,2,8,1408]{3,2,1,0:T(8,128)(2,1)}, u32[]{:S(2)}, u32[]{:S(2)}) async-start(bf16[16,2,8,1408]{3,2,1,0:T(8,128)(2,1)} %get-tuple-element.34), calls=%async_computation.4 | async-start | bytes 1441792 | tf_op jit(solution)/shard_map/all_to_all | solution.py:288
  118.3 0.9 copy-done.23
  119.2 1.0 shard_map.89
  120.2 1.9 %collective-permute-start.4 = (bf16[2,320,1280]{2,1,0:T(8,128)(2,1)S(1)}, bf16[2,320,1280]{2,1,0:T(8,128)(2,1)S(1)}, u32[]{:S(2)}, u32[]{:S(2)}) collective-permute-start(bf16[2,320,1280]{2,1,0:T(8,128)(2,1)S(1)} %get-tuple-element.40), channel_id=1, source_target_pairs={{0,128},{128,0},{1,129},{129,1},{2,130},{130,2},{3,131},{131,3},{4... | collective-permute-start | bytes 4915208 | tf_op jit(solution)/shard_map/ppermute | solution.py:277
  122.1 3.5 %collective-permute-done.4 = bf16[2,320,1280]{2,1,0:T(8,128)(2,1)S(1)} collective-permute-done((bf16[2,320,1280]{2,1,0:T(8,128)(2,1)S(1)}, bf16[2,320,1280]{2,1,0:T(8,128)(2,1)S(1)}, u32[]{:S(2)}, u32[]{:S(2)}) %collective-permute-start.4) | collective-permute-done | bytes 1638432 | tf_op jit(solution)/shard_map/ppermute | solution.py:277
  125.6 0.4 add_convert_fusion
  126.0 0.0 copy-start.6
  126.0 2.5 %all-to-all-done.4.refs_5_ = bf16[16,2,8,1408]{3,2,1,0:T(8,128)(2,1)} async-done(((bf16[16,2,8,1408]{3,2,1,0:T(8,128)(2,1)}), bf16[16,2,8,1408]{3,2,1,0:T(8,128)(2,1)}, u32[]{:S(2)}, u32[]{:S(2)}) %all-to-all-start.4) | async-done | bytes 720928 | tf_op jit(solution)/shard_map/all_to_all | solution.py:288
  128.6 1.9 %shard_map.90 = (bf16[32,2,1280]{2,1,0:T(2,128)(2,1)S(1)}, bf16[128,128]{1,0:T(8,128)(2,1)S(1)}, bf16[64,1280]{1,0:T(8,128)(2,1)S(1)}) custom-call(s32[1]{0:T(128)} %bitcast.where_am_i.refs_0_, bf16[64,1280]{1,0:T(8,128)(2,1)S(1)} %reshape.26.router_t.refs_1_, bf16[128,1280]{1,0:T(8,128)(2,1)S(1)} %copy-done.15, bf16[128,1280]{1,0:T(8,128)(2,1)S(1)} %copy-done.17, ...), custom_call_target="tpu_custom_call" | custom-call | bytes 2621444 | tf_op jit(solution)/shard_map/pallas_call | solution.py:32
  130.5 17.8 %all_to_all.43.got = bf16[32,2,1280]{2,1,0:T(2,128)(2,1)S(1)} all-to-all(bf16[32,2,1280]{2,1,0:T(2,128)(2,1)S(1)} %get-tuple-element.45), channel_id=1, replica_groups=mesh['zh'=2,'core'=2,'y'=4,'zl'=8,'xh'=2,'xl'=2] {'core','y','xh','xl'}, dimensions={0} | all-to-all | bytes 327680 | tf_op jit(solution)/shard_map/all_to_all | solution.py:281
  148.3 0.8 shard_map.92
  149.1 6.5 %all-to-all-start.6 = ((bf16[16,2,1280]{2,1,0:T(2,128)(2,1)}), bf16[16,2,1280]{2,1,0:T(2,128)(2,1)S(1)}, u32[]{:S(2)}, u32[]{:S(2)}) async-start(bf16[16,2,1280]{2,1,0:T(2,128)(2,1)} %shard_map.92), calls=%async_computation.6 | async-start | bytes 163840 | tf_op jit(solution)/shard_map/all_to_all | solution.py:281
  155.6 0.3 shard_map.91
  155.9 2.7 %collective-permute-start.5 = (bf16[64,1280]{1,0:T(8,128)(2,1)S(1)}, bf16[64,1280]{1,0:T(8,128)(2,1)S(1)}, u32[]{:S(2)}, u32[]{:S(2)}) collective-permute-start(bf16[64,1280]{1,0:T(8,128)(2,1)S(1)} %get-tuple-element.44), channel_id=1, source_target_pairs={{0,128},{128,0},{1,129},{129,1},{2,130},{130,2},{3,131},{131,3},{4... | collective-permute-start | bytes 491528 | tf_op jit(solution)/shard_map/ppermute | solution.py:277
  158.6 8.8 %all-to-all-done.6.got = bf16[16,2,1280]{2,1,0:T(2,128)(2,1)S(1)} async-done(((bf16[16,2,1280]{2,1,0:T(2,128)(2,1)}), bf16[16,2,1280]{2,1,0:T(2,128)(2,1)S(1)}, u32[]{:S(2)}, u32[]{:S(2)}) %all-to-all-start.6) | async-done | bytes 81952 | tf_op jit(solution)/shard_map/all_to_all | solution.py:281
  167.4 0.8 shard_map.93
  168.2 5.8 %all-to-all-start.7 = ((bf16[32,2,1280]{2,1,0:T(2,128)(2,1)}), bf16[32,2,1280]{2,1,0:T(2,128)(2,1)S(1)}, u32[]{:S(2)}, u32[]{:S(2)}) async-start(bf16[32,2,1280]{2,1,0:T(2,128)(2,1)} %shard_map.93), calls=%async_computation.7 | async-start | bytes 327680 | tf_op jit(solution)/shard_map/all_to_all | solution.py:281
  174.0 0.8 maximum_select_fusion
  174.8 7.1 %all-to-all-done.7 = bf16[32,2,1280]{2,1,0:T(2,128)(2,1)S(1)} async-done(((bf16[32,2,1280]{2,1,0:T(2,128)(2,1)}), bf16[32,2,1280]{2,1,0:T(2,128)(2,1)S(1)}, u32[]{:S(2)}, u32[]{:S(2)}) %all-to-all-start.7) | async-done | bytes 163872 | tf_op jit(solution)/shard_map/all_to_all | solution.py:281
  181.8 0.8 reshape.27
  (45 shorter events, 0.1 us)
Async XLA Ops:
  0.6 13.1 %collective-permute-start = (bf16[2,64,1280]{2,1,0:T(8,128)(2,1)}, bf16[2,64,1280]{2,1,0:T(8,128)(2,1)S(1)}, u32[]{:S(2)}, u32[]{:S(2)}) collective-permute-start(bf16[2,64,1280]{2,1,0:T(8,128)(2,1)} %tok_a.1), channel_id=1, source_target_pairs={{0,128},{128,0},{1,129},{129,1},{2,130},{130,2},{3,131},{131,3},{4... | collective-permute-start | bytes 983048 | tf_op jit(solution)/shard_map/ppermute | solution.py:277
  9.4 4.3 %collective-permute-start.1 = (bf16[2,64,1280]{2,1,0:T(8,128)(2,1)}, bf16[2,64,1280]{2,1,0:T(8,128)(2,1)S(1)}, u32[]{:S(2)}, u32[]{:S(2)}) collective-permute-start(bf16[2,64,1280]{2,1,0:T(8,128)(2,1)} %grad_a.1), channel_id=1, source_target_pairs={{0,128},{128,0},{1,129},{129,1},{2,130},{130,2},{3,131},{131,3},{4... | collective-permute-start | bytes 983048 | tf_op jit(solution)/shard_map/ppermute | solution.py:277
  13.8 1.7 copy-start.10
  13.8 1.6 copy-start.12
  13.8 11.2 %copy-start = (bf16[1,320,1280]{2,1,0:T(8,128)(2,1)S(1)}, bf16[1,320,1280]{2,1,0:T(8,128)(2,1)}, u32[]{:S(2)}) copy-start(bf16[1,320,1280]{2,1,0:T(8,128)(2,1)} %param.7) | copy-start | bytes 2457604
  13.8 13.2 %copy-start.1 = (bf16[1,320,1280]{2,1,0:T(8,128)(2,1)S(1)}, bf16[1,320,1280]{2,1,0:T(8,128)(2,1)}, u32[]{:S(2)}) copy-start(bf16[1,320,1280]{2,1,0:T(8,128)(2,1)} %param.8) | copy-start | bytes 2457604
  15.4 31.1 %all-to-all-start = ((bf16[16,2,8,1408]{3,2,1,0:T(8,128)(2,1)}), bf16[16,2,8,1408]{3,2,1,0:T(8,128)(2,1)}, u32[]{:S(2)}, u32[]{:S(2)}) async-start(bf16[16,2,8,1408]{3,2,1,0:T(8,128)(2,1)} %shard_map.84.refs_2_), calls=%async_computation | async-start | bytes 1441792 | tf_op jit(solution)/shard_map/all_to_all | solution.py:288
  25.0 4.4 %collective-permute-start.2 = (bf16[320,1280]{1,0:T(8,128)(2,1)S(1)}, bf16[320,1280]{1,0:T(8,128)(2,1)S(1)}, u32[]{:S(2)}, u32[]{:S(2)}) collective-permute-start(bf16[320,1280]{1,0:T(8,128)(2,1)S(1)} %bitcast.14), channel_id=1, source_target_pairs={{0,128},{128,0},{1,129},{129,1},{2,130},{130,2},{3,131},{131,3},{4... | collective-permute-start | bytes 2457608 | tf_op jit(solution)/shard_map/ppermute | solution.py:277
  27.0 4.4 %collective-permute-start.3 = (bf16[320,1280]{1,0:T(8,128)(2,1)S(1)}, bf16[320,1280]{1,0:T(8,128)(2,1)S(1)}, u32[]{:S(2)}, u32[]{:S(2)}) collective-permute-start(bf16[320,1280]{1,0:T(8,128)(2,1)S(1)} %bitcast.18), channel_id=1, source_target_pairs={{0,128},{128,0},{1,129},{129,1},{2,130},{130,2},{3,131},{131,3},{4... | collective-permute-start | bytes 2457608 | tf_op jit(solution)/shard_map/ppermute | solution.py:277
  65.3 1.9 %copy-start.2 = (bf16[16,2,8,1408]{3,2,1,0:T(8,128)(2,1)}, bf16[16,2,8,1408]{3,2,1,0:T(8,128)(2,1)S(1)}, u32[]{:S(2)}) copy-start(bf16[16,2,8,1408]{3,2,1,0:T(8,128)(2,1)S(1)} %all_to_all.40.got.rows_3) | copy-start | bytes 2162692
  67.2 12.4 %copy-start.18 = (bf16[2,320,128]{2,1,0:T(8,128)(2,1)}, bf16[2,320,128]{2,1,0:T(8,128)(2,1)S(1)}, u32[]{:S(2)}) copy-start(bf16[2,320,128]{2,1,0:T(8,128)(2,1)S(1)} %get-tuple-element.35.pre_3) | copy-start | bytes 491524
  67.2 12.8 %copy-start.20 = (bf16[2,320,128]{2,1,0:T(8,128)(2,1)}, bf16[2,320,128]{2,1,0:T(8,128)(2,1)S(1)}, u32[]{:S(2)}) copy-start(bf16[2,320,128]{2,1,0:T(8,128)(2,1)S(1)} %get-tuple-element.36.hid_3) | copy-start | bytes 491524
  79.6 0.8 copy-start.4
  80.5 30.7 %copy-start.24 = (bf16[2,320,128]{2,1,0:T(8,128)(2,1)}, bf16[2,320,128]{2,1,0:T(8,128)(2,1)S(1)}, u32[]{:S(2)}) copy-start(bf16[2,320,128]{2,1,0:T(8,128)(2,1)S(1)} %get-tuple-element.38.hid_4) | copy-start | bytes 491524
  80.5 32.0 %copy-start.22 = (bf16[2,320,128]{2,1,0:T(8,128)(2,1)}, bf16[2,320,128]{2,1,0:T(8,128)(2,1)S(1)}, u32[]{:S(2)}) copy-start(bf16[2,320,128]{2,1,0:T(8,128)(2,1)S(1)} %get-tuple-element.37.pre_4) | copy-start | bytes 491524
  80.5 30.7 %copy-start.8 = (bf16[2,64,1280]{2,1,0:T(8,128)(2,1)S(1)}, bf16[2,64,1280]{2,1,0:T(8,128)(2,1)}, u32[]{:S(2)}) copy-start(bf16[2,64,1280]{2,1,0:T(8,128)(2,1)} %grad_a.1) | copy-start | bytes 983044
  80.5 30.7 %copy-start.9 = (bf16[2,64,1280]{2,1,0:T(8,128)(2,1)S(1)}, bf16[2,64,1280]{2,1,0:T(8,128)(2,1)}, u32[]{:S(2)}) copy-start(bf16[2,64,1280]{2,1,0:T(8,128)(2,1)} %tok_a.1) | copy-start | bytes 983044
  80.5 30.7 %copy-start.11 = (bf16[2,64,1280]{2,1,0:T(8,128)(2,1)S(1)}, bf16[2,64,1280]{2,1,0:T(8,128)(2,1)}, u32[]{:S(2)}) copy-start(bf16[2,64,1280]{2,1,0:T(8,128)(2,1)} %copy-done.10) | copy-start | bytes 983044
  80.5 30.7 %copy-start.13 = (bf16[2,64,1280]{2,1,0:T(8,128)(2,1)S(1)}, bf16[2,64,1280]{2,1,0:T(8,128)(2,1)}, u32[]{:S(2)}) copy-start(bf16[2,64,1280]{2,1,0:T(8,128)(2,1)} %copy-done.12) | copy-start | bytes 983044
  111.2 7.0 %copy-start.3 = (bf16[16,2,8,1408]{3,2,1,0:T(8,128)(2,1)S(1)}, bf16[16,2,8,1408]{3,2,1,0:T(8,128)(2,1)}, u32[]{:S(2)}) copy-start(bf16[16,2,8,1408]{3,2,1,0:T(8,128)(2,1)} %copy-done.2) | copy-start | bytes 2162692
  111.2 7.0 %copy-start.5 = (bf16[16,2,8,1280]{3,2,1,0:T(8,128)(2,1)S(1)}, bf16[16,2,8,1280]{3,2,1,0:T(8,128)(2,1)}, u32[]{:S(2)}) copy-start(bf16[16,2,8,1280]{3,2,1,0:T(8,128)(2,1)} %copy-done.4) | copy-start | bytes 1966084
  111.2 7.0 %copy-start.19 = (bf16[2,320,128]{2,1,0:T(8,128)(2,1)S(1)}, bf16[2,320,128]{2,1,0:T(8,128)(2,1)}, u32[]{:S(2)}) copy-start(bf16[2,320,128]{2,1,0:T(8,128)(2,1)} %copy-done.18) | copy-start | bytes 491524
  111.3 7.0 %copy-start.21 = (bf16[2,320,128]{2,1,0:T(8,128)(2,1)S(1)}, bf16[2,320,128]{2,1,0:T(8,128)(2,1)}, u32[]{:S(2)}) copy-start(bf16[2,320,128]{2,1,0:T(8,128)(2,1)} %copy-done.20) | copy-start | bytes 491524
  111.3 7.0 %copy-start.25 = (bf16[2,320,128]{2,1,0:T(8,128)(2,1)S(1)}, bf16[2,320,128]{2,1,0:T(8,128)(2,1)}, u32[]{:S(2)}) copy-start(bf16[2,320,128]{2,1,0:T(8,128)(2,1)} %copy-done.24) | copy-start | bytes 491524
  112.5 0.7 copy-start.14
  113.2 0.7 copy-start.16
  113.9 14.6 %all-to-all-start.4 = ((bf16[16,2,8,1408]{3,2,1,0:T(8,128)(2,1)}), bf16[16,2,8,1408]{3,2,1,0:T(8,128)(2,1)}, u32[]{:S(2)}, u32[]{:S(2)}) async-start(bf16[16,2,8,1408]{3,2,1,0:T(8,128)(2,1)} %get-tuple-element.34), calls=%async_computation.4 | async-start | bytes 1441792 | tf_op jit(solution)/shard_map/all_to_all | solution.py:288
  118.3 0.9 copy-start.23
  120.2 5.4 %collective-permute-start.4 = (bf16[2,320,1280]{2,1,0:T(8,128)(2,1)S(1)}, bf16[2,320,1280]{2,1,0:T(8,128)(2,1)S(1)}, u32[]{:S(2)}, u32[]{:S(2)}) collective-permute-start(bf16[2,320,1280]{2,1,0:T(8,128)(2,1)S(1)} %get-tuple-element.40), channel_id=1, source_target_pairs={{0,128},{128,0},{1,129},{129,1},{2,130},{130,2},{3,131},{131,3},{4... | collective-permute-start | bytes 4915208 | tf_op jit(solution)/shard_map/ppermute | solution.py:277
  125.6 3.0 %copy-start.15 = (bf16[128,1280]{1,0:T(8,128)(2,1)S(1)}, bf16[128,1280]{1,0:T(8,128)(2,1)}, u32[]{:S(2)}) copy-start(bf16[128,1280]{1,0:T(8,128)(2,1)} %copy-done.14) | copy-start | bytes 983044
  125.6 3.0 %copy-start.17 = (bf16[128,1280]{1,0:T(8,128)(2,1)S(1)}, bf16[128,1280]{1,0:T(8,128)(2,1)}, u32[]{:S(2)}) copy-start(bf16[128,1280]{1,0:T(8,128)(2,1)} %copy-done.16) | copy-start | bytes 983044
  126.0 4.5 %copy-start.6 = (bf16[1,320,1280]{2,1,0:T(8,128)(2,1)}, bf16[1,320,1280]{2,1,0:T(8,128)(2,1)S(1)}, u32[]{:S(2)}) copy-start(bf16[1,320,1280]{2,1,0:T(8,128)(2,1)S(1)} %get-tuple-element.46.refs_7_) | copy-start | bytes 2457604
  126.0 4.5 %copy-start.7 = (bf16[1,320,1280]{2,1,0:T(8,128)(2,1)}, bf16[1,320,1280]{2,1,0:T(8,128)(2,1)S(1)}, u32[]{:S(2)}) copy-start(bf16[1,320,1280]{2,1,0:T(8,128)(2,1)S(1)} %get-tuple-element.47.refs_6_) | copy-start | bytes 2457604
  149.1 18.3 %all-to-all-start.6 = ((bf16[16,2,1280]{2,1,0:T(2,128)(2,1)}), bf16[16,2,1280]{2,1,0:T(2,128)(2,1)S(1)}, u32[]{:S(2)}, u32[]{:S(2)}) async-start(bf16[16,2,1280]{2,1,0:T(2,128)(2,1)} %shard_map.92), calls=%async_computation.6 | async-start | bytes 163840 | tf_op jit(solution)/shard_map/all_to_all | solution.py:281
  155.9 18.1 %collective-permute-start.5 = (bf16[64,1280]{1,0:T(8,128)(2,1)S(1)}, bf16[64,1280]{1,0:T(8,128)(2,1)S(1)}, u32[]{:S(2)}, u32[]{:S(2)}) collective-permute-start(bf16[64,1280]{1,0:T(8,128)(2,1)S(1)} %get-tuple-element.44), channel_id=1, source_target_pairs={{0,128},{128,0},{1,129},{129,1},{2,130},{130,2},{3,131},{131,3},{4... | collective-permute-start | bytes 491528 | tf_op jit(solution)/shard_map/ppermute | solution.py:277
  168.2 13.6 %all-to-all-start.7 = ((bf16[32,2,1280]{2,1,0:T(2,128)(2,1)}), bf16[32,2,1280]{2,1,0:T(2,128)(2,1)S(1)}, u32[]{:S(2)}, u32[]{:S(2)}) async-start(bf16[32,2,1280]{2,1,0:T(2,128)(2,1)} %shard_map.93), calls=%async_computation.7 | async-start | bytes 327680 | tf_op jit(solution)/shard_map/all_to_all | solution.py:281

commit v8 on v7

--- a/solution.py
+++ b/solution.py
@@ -171,31 +171,31 @@
 
 
 def phase_2(where_am_i, got, slots, out, kept, stats):
+    @pl.when(where_am_i[0] == 0)
+    def _():
+        middle(got, out, kept, stats)
+
     @pl.when(where_am_i[0] == 1)
     def _():
+        out[...] = slots[...]
+
+
+def phase_3(where_am_i, got, up_own, up_other, down_own, down_other, out, kept, stats, pre_grads, hiddens):
+    @pl.when(where_am_i[0] == 0)
+    def _():
+        expert(got, up_own, up_other, down_own, down_other, out, pre_grads, hiddens)
+
+    @pl.when(where_am_i[0] == 1)
+    def _():
         middle(got, out, kept, stats)
 
+
+def phase_4(where_am_i, got, kept, stats, up_own, up_other, down_own, down_other, out, pre_grads, hiddens):
     @pl.when(where_am_i[0] == 0)
     def _():
-        out[...] = slots[...]
-
-
-def phase_3(where_am_i, got, up_own, up_other, down_own, down_other, out, kept, stats, pre_grads, hiddens):
+        back_to_owners(got, kept, stats, out)
+
     @pl.when(where_am_i[0] == 1)
-    def _():
-        expert(got, up_own, up_other, down_own, down_other, out, pre_grads, hiddens)
-
-    @pl.when(where_am_i[0] == 0)
-    def _():
-        middle(got, out, kept, stats)
-
-
-def phase_4(where_am_i, got, kept, stats, up_own, up_other, down_own, down_other, out, pre_grads, hiddens):
-    @pl.when(where_am_i[0] == 1)
-    def _():
-        back_to_owners(got, kept, stats, out)
-
-    @pl.when(where_am_i[0] == 0)
     def _():
         expert(got, up_own, up_other, down_own, down_other, out, pre_grads, hiddens)
 
@@ -213,11 +213,11 @@
     for copy in copies:
         copy.start()
 
+    @pl.when(core == 1)
+    def _():
+        back_to_owners(got, kept, stats, out)
+
     @pl.when(core == 0)
-    def _():
-        back_to_owners(got, kept, stats, out)
-
-    @pl.when(core == 1)
     def _():
         out[...] = got[...]
 
@@ -226,18 +226,18 @@
 
 
 def weights_kernel(where_am_i, pre_3, hid_3, rows_3, pre_4, hid_4, rows_4, keep, send):
+    @pl.when(where_am_i[0] == 0)
+    def _():
+        weight_grads(pre_3, hid_3, rows_3, keep, send)
+
     @pl.when(where_am_i[0] == 1)
-    def _():
-        weight_grads(pre_3, hid_3, rows_3, keep, send)
-
-    @pl.when(where_am_i[0] == 0)
     def _():
         weight_grads(pre_4, hid_4, rows_4, keep, send)
 
 
 def tokens_kernel(where_am_i, router_t, tok, grad, got_4, got_5, router_grad, left, right):
     spans = [slice(h * ZL, (h + 1) * ZL) for h in range(2)]
-    halves = [jnp.where(where_am_i[0] == 1, got_4[span], got_5[span]).astype(f32) for span in spans]
+    halves = [jnp.where(where_am_i[0] == 0, got_4[span], got_5[span]).astype(f32) for span in spans]
     both = halves[0] + halves[1]
     slot_in_grad = both[:, 0, :, :D].reshape(SLOTS, D).astype(bf16)
     slot_out = both[:, 1, :, :D].reshape(SLOTS, D).astype(bf16)
@@ -301,15 +301,15 @@
     acts = [shaped((2, 320, LANES), bf16)] * 2
     held = [shaped((LANES, D), f32), shaped((LANES, LANES), f32)]
     (slots,) = call(slots_kernel, [wide], here, router_t, tok_own, tok_b, grad_own, grad_b)
-    got_1 = mixed(slots, PLANE, COLUMN)
+    got_1 = mixed(slots, COLUMN, PLANE)
     up_other, down_other = swap(up_proj[0]), swap(down_proj[0])
     weights = (up_proj[0], up_other, down_proj[0], down_other)
     sent_2, kept_1, stats_1 = call(phase_2, [wide, *held], here, got_1, slots, after=weights, after_spec=VMEM)
-    got_2 = mixed(sent_2, COLUMN, PLANE)
+    got_2 = mixed(sent_2, PLANE, COLUMN)
     sent_3, kept_0, stats_0, pre_1, hid_1 = call(phase_3, [shaped((16, 2, 8, D), bf16), *held, *acts], here, got_2, *weights)
     got_3 = exchange(sent_3, PLANE)
     sent_4, pre_0, hid_0 = call(phase_4, [wide, *acts], here, got_3, kept_1, stats_1, *weights)
-    got_4 = mixed(sent_4, PLANE, COLUMN)
+    got_4 = mixed(sent_4, COLUMN, PLANE)
     keep, send = call(
         weights_kernel, [shaped((2, 320, D), bf16), shaped((2, 320, D), bf16)],
         here, pre_1, hid_1, got_2, pre_0, hid_0, got_3,
@@ -320,7 +320,7 @@
         phase_5, [wide], here, got_4, kept_0, stats_0, tokens, tok_b, out_grad, grad_b,
         stored=[shaped((LANES, D), bf16)] * 2,
     )
-    got_5 = mixed(sent_5, COLUMN, PLANE)
+    got_5 = mixed(sent_5, PLANE, COLUMN)
     router_part, left, right = call(
         tokens_kernel,
         [shaped((32, 2, D), bf16), shaped((LANES, LANES), bf16), shaped((SLOTS, D), bf16)],

time: 183 us -> 186 us (1.016)
  waiting for transfers between devices: 39 us -> 21.2 us
  starting transfers between devices: 45.8 us -> 62.4 us
  blocking collectives: 77.8 us -> 81.3 us
    ppermute x6, starting transfers between devices: 19.7 us -> 40.3 us  [swap(): return lax.ppermute(value, 'core', [(0, 1), (1, 0)])]
    all_to_all x2, waiting for transfers between devices: 17.8 us -> 0.01 us  [mixed(): lax.all_to_all(value, ALL, split_axis=0, concat_axis=0, tiled=True, axis_...]
    all_to_all x2, blocking collectives: 30.2 us -> 32.9 us  [exchange(): return lax.all_to_all(value, axes, split_axis=0, concat_axis=0, tiled=True)]
    all_to_all x2, starting transfers between devices: 13.9 us -> 11.3 us  [mixed(): lax.all_to_all(value, ALL, split_axis=0, concat_axis=0, tiled=True, axis_...]
  transfers between devices with their start and end apart: 10 -> 10, of which waited for: 6 -> 4; matrix products, arithmetic and copies ran while one was open for 2% -> 2% of each run, Pallas kernels for 1% -> 1%
where the time goes in v8:
time: 186 us; the launch traced here: 185 us
  blocking collectives  81.3 us (44%)
  starting transfers between devices  62.4 us (34%)
  waiting for transfers between devices  21.2 us (11%)
  Pallas kernels  11.7 us (6%)
  local copies, waits for them, and re-layouts  5.35 us (3%)
  other arithmetic  2.35 us (1%)
    all_to_all x2, blocking collectives, mixed(): lax.all_to_all(value, ALL, split_axis=0, concat_axis=0, tiled=True, axis_...  48.4 us
    ppermute x6, starting transfers between devices, swap(): return lax.ppermute(value, 'core', [(0, 1), (1, 0)])  40.3 us
    all_to_all x2, blocking collectives, exchange(): return lax.all_to_all(value, axes, split_axis=0, concat_axis=0, tiled=True)  32.9 us
    all_to_all x2, waiting for transfers between devices, exchange(): return lax.all_to_all(value, axes, split_axis=0, concat_axis=0, tiled=True)  15.8 us
    pallas_call x10, Pallas kernels, call(): pl.pallas_call(body, out_shape=[*outs, *stored], in_specs=[SMEM] + [VMEM]...  11.7 us
    all_to_all x2, starting transfers between devices, mixed(): lax.all_to_all(value, ALL, split_axis=0, concat_axis=0, tiled=True, axis_...  11.3 us
    all_to_all x2, starting transfers between devices, exchange(): return lax.all_to_all(value, axes, split_axis=0, concat_axis=0, tiled=True)  10.8 us
    ppermute x6, waiting for transfers between devices, swap(): return lax.ppermute(value, 'core', [(0, 1), (1, 0)])  5.41 us
  transfers between devices with their start and end apart: 10, of which 4 were waited for; matrix products, arithmetic and copies ran while one was open for 2% of the time, Pallas kernels for 1%

profile of v8, /device:TPU:1, one launch (start us, length us, event | category | flops | bytes accessed | tf_op | source)
XLA Modules:
  0.0 185.4 jit_solution(5506673009568259747)
XLA Ops:
  0.6 8.8 %collective-permute-start = (bf16[2,64,1280]{2,1,0:T(8,128)(2,1)}, bf16[2,64,1280]{2,1,0:T(8,128)(2,1)S(1)}, u32[]{:S(2)}, u32[]{:S(2)}) collective-permute-start(bf16[2,64,1280]{2,1,0:T(8,128)(2,1)} %tok_a.1), channel_id=1, source_target_pairs={{0,128},{128,0},{1,129},{129,1},{2,130},{130,2},{3,131},{131,3},{4... | collective-permute-start | bytes 983048 | tf_op jit(solution)/shard_map/ppermute | solution.py:277
  9.4 1.9 %collective-permute-start.1 = (bf16[2,64,1280]{2,1,0:T(8,128)(2,1)}, bf16[2,64,1280]{2,1,0:T(8,128)(2,1)S(1)}, u32[]{:S(2)}, u32[]{:S(2)}) collective-permute-start(bf16[2,64,1280]{2,1,0:T(8,128)(2,1)} %grad_a.1), channel_id=1, source_target_pairs={{0,128},{128,0},{1,129},{129,1},{2,130},{130,2},{3,131},{131,3},{4... | collective-permute-start | bytes 983048 | tf_op jit(solution)/shard_map/ppermute | solution.py:277
  11.4 1.0 reshape.25
  12.3 0.1 copy.11
  12.5 0.1 reshape.26.router_t.refs_1_
  12.5 1.2 select_bitcast_fusion
  13.8 0.0 copy-start.12
  13.8 0.0 copy-start.1
  13.8 1.6 shard_map.84.refs_2_
  15.4 4.3 %all-to-all-start = ((bf16[16,2,8,1408]{3,2,1,0:T(8,128)(2,1)}), bf16[16,2,8,1408]{3,2,1,0:T(8,128)(2,1)}, u32[]{:S(2)}, u32[]{:S(2)}) async-start(bf16[16,2,8,1408]{3,2,1,0:T(8,128)(2,1)} %shard_map.84.refs_2_), calls=%async_computation | async-start | bytes 1441792 | tf_op jit(solution)/shard_map/all_to_all | solution.py:288
  19.7 8.0 %collective-permute-start.2 = (bf16[320,1280]{1,0:T(8,128)(2,1)S(1)}, bf16[320,1280]{1,0:T(8,128)(2,1)S(1)}, u32[]{:S(2)}, u32[]{:S(2)}) collective-permute-start(bf16[320,1280]{1,0:T(8,128)(2,1)S(1)} %bitcast.14), channel_id=1, source_target_pairs={{0,128},{128,0},{1,129},{129,1},{2,130},{130,2},{3,131},{131,3},{4... | collective-permute-start | bytes 2457608 | tf_op jit(solution)/shard_map/ppermute | solution.py:277
  27.7 1.9 %collective-permute-start.3 = (bf16[320,1280]{1,0:T(8,128)(2,1)S(1)}, bf16[320,1280]{1,0:T(8,128)(2,1)S(1)}, u32[]{:S(2)}, u32[]{:S(2)}) collective-permute-start(bf16[320,1280]{1,0:T(8,128)(2,1)S(1)} %bitcast.18), channel_id=1, source_target_pairs={{0,128},{128,0},{1,129},{129,1},{2,130},{130,2},{3,131},{131,3},{4... | collective-permute-start | bytes 2457608 | tf_op jit(solution)/shard_map/ppermute | solution.py:277
  29.7 2.3 %collective-permute-done.3.refs_6_.down_other = bf16[320,1280]{1,0:T(8,128)(2,1)S(1)} collective-permute-done((bf16[320,1280]{1,0:T(8,128)(2,1)S(1)}, bf16[320,1280]{1,0:T(8,128)(2,1)S(1)}, u32[]{:S(2)}, u32[]{:S(2)}) %collective-permute-start.3) | collective-permute-done | bytes 819232 | tf_op jit(solution)/shard_map/ppermute | solution.py:277
  32.0 1.4 shard_map.85
  33.3 35.4 %all_to_all.40.got.rows_3 = bf16[16,2,8,1408]{3,2,1,0:T(8,128)(2,1)S(1)} all-to-all(bf16[16,2,8,1408]{3,2,1,0:T(8,128)(2,1)S(1)} %get-tuple-element.25), channel_id=1, replica_groups={{0,1,2,3,32,33,34,35,64,65,66,67,96,97,98,99},{4,5,6,7,36,37,38,39,68,6..., dimensions={0} | all-to-all | bytes 1441792 | tf_op jit(solution)/shard_map/all_to_all | solution.py:288
  68.7 0.5 shard_map.86
  69.3 0.3 copy-done.2
  69.6 17.8 %all_to_all.41.got.rows_4 = bf16[16,2,8,1280]{3,2,1,0:T(8,128)(2,1)S(1)} all-to-all(bf16[16,2,8,1280]{3,2,1,0:T(8,128)(2,1)S(1)} %get-tuple-element.26), channel_id=1, replica_groups=mesh['zh'=2,'core'=2,'y'=4,'zl'=8,'xh'=2,'xl'=2] {'y','xh','xl'}, dimensions={0} | all-to-all | bytes 1310720 | tf_op jit(solution)/shard_map/all_to_all | solution.py:281
  87.4 1.9 %shard_map.87 = (bf16[16,2,8,1408]{3,2,1,0:T(8,128)(2,1)S(1)}, bf16[2,320,128]{2,1,0:T(8,128)(2,1)S(1)}, bf16[2,320,128]{2,1,0:T(8,128)(2,1)S(1)}) custom-call(s32[1]{0:T(128)} %bitcast.where_am_i.refs_0_, bf16[16,2,8,1280]{3,2,1,0:T(8,128)(2,1)S(1)} %all_to_all.41.got.rows_4, f32[128,1280]{1,0:T(8,128)S(1)} %get-tuple-element.27.kept, ...), custom_call_target="tpu_custom_call" | custom-call | bytes 5701636 | tf_op jit(solution)/shard_map/pallas_call | solution.py:32
  89.3 0.0 copy-start.8
  89.4 0.0 copy-start.13
  89.4 13.0 %all_to_all.42.got.refs_4_ = bf16[16,2,8,1408]{3,2,1,0:T(8,128)(2,1)S(1)} all-to-all(bf16[16,2,8,1408]{3,2,1,0:T(8,128)(2,1)S(1)} %get-tuple-element.29), channel_id=1, replica_groups={{0,4,8,12,16,20,24,28,256,260,264,268,272,276,280,284},{1,5,9,13,17,21,..., dimensions={0} | all-to-all | bytes 1441792 | tf_op jit(solution)/shard_map/all_to_all | solution.py:288
  102.4 0.0 copy-start.5
  102.5 1.5 shard_map.88
  104.0 0.0 copy-start.14
  104.0 0.7 copy-done.14
  104.8 0.7 copy-done.16
  105.5 7.0 %all-to-all-start.4 = ((bf16[16,2,8,1408]{3,2,1,0:T(8,128)(2,1)}), bf16[16,2,8,1408]{3,2,1,0:T(8,128)(2,1)}, u32[]{:S(2)}, u32[]{:S(2)}) async-start(bf16[16,2,8,1408]{3,2,1,0:T(8,128)(2,1)} %get-tuple-element.34), calls=%async_computation.4 | async-start | bytes 1441792 | tf_op jit(solution)/shard_map/all_to_all | solution.py:288
  112.6 0.9 copy-done.23
  113.5 1.0 shard_map.89
  114.5 16.9 %collective-permute-start.4 = (bf16[2,320,1280]{2,1,0:T(8,128)(2,1)S(1)}, bf16[2,320,1280]{2,1,0:T(8,128)(2,1)S(1)}, u32[]{:S(2)}, u32[]{:S(2)}) collective-permute-start(bf16[2,320,1280]{2,1,0:T(8,128)(2,1)S(1)} %get-tuple-element.40), channel_id=1, source_target_pairs={{0,128},{128,0},{1,129},{129,1},{2,130},{130,2},{3,131},{131,3},{4... | collective-permute-start | bytes 4915208 | tf_op jit(solution)/shard_map/ppermute | solution.py:277
  131.4 3.1 %collective-permute-done.4 = bf16[2,320,1280]{2,1,0:T(8,128)(2,1)S(1)} collective-permute-done((bf16[2,320,1280]{2,1,0:T(8,128)(2,1)S(1)}, bf16[2,320,1280]{2,1,0:T(8,128)(2,1)S(1)}, u32[]{:S(2)}, u32[]{:S(2)}) %collective-permute-start.4) | collective-permute-done | bytes 1638432 | tf_op jit(solution)/shard_map/ppermute | solution.py:277
  134.5 0.4 add_convert_fusion
  134.9 0.0 copy-start.7
  135.0 0.5 copy-done.15
  135.5 0.1 copy-done.17
  135.6 1.9 %shard_map.90 = (bf16[32,2,1280]{2,1,0:T(2,128)(2,1)S(1)}, bf16[128,128]{1,0:T(8,128)(2,1)S(1)}, bf16[64,1280]{1,0:T(8,128)(2,1)S(1)}) custom-call(s32[1]{0:T(128)} %bitcast.where_am_i.refs_0_, bf16[64,1280]{1,0:T(8,128)(2,1)S(1)} %reshape.26.router_t.refs_1_, bf16[128,1280]{1,0:T(8,128)(2,1)S(1)} %copy-done.15, bf16[128,1280]{1,0:T(8,128)(2,1)S(1)} %copy-done.17, ...), custom_call_target="tpu_custom_call" | custom-call | bytes 2621444 | tf_op jit(solution)/shard_map/pallas_call | solution.py:32
  137.6 15.1 %all_to_all.43.got = bf16[32,2,1280]{2,1,0:T(2,128)(2,1)S(1)} all-to-all(bf16[32,2,1280]{2,1,0:T(2,128)(2,1)S(1)} %get-tuple-element.45), channel_id=1, replica_groups=mesh['zh'=2,'core'=2,'y'=4,'zl'=8,'xh'=2,'xl'=2] {'core','y','xh','xl'}, dimensions={0} | all-to-all | bytes 327680 | tf_op jit(solution)/shard_map/all_to_all | solution.py:281
  152.7 0.8 shard_map.92
  153.5 4.9 %all-to-all-start.6 = ((bf16[16,2,1280]{2,1,0:T(2,128)(2,1)}), bf16[16,2,1280]{2,1,0:T(2,128)(2,1)S(1)}, u32[]{:S(2)}, u32[]{:S(2)}) async-start(bf16[16,2,1280]{2,1,0:T(2,128)(2,1)} %shard_map.92), calls=%async_computation.6 | async-start | bytes 163840 | tf_op jit(solution)/shard_map/all_to_all | solution.py:281
  158.4 0.3 shard_map.91
  158.7 2.7 %collective-permute-start.5 = (bf16[64,1280]{1,0:T(8,128)(2,1)S(1)}, bf16[64,1280]{1,0:T(8,128)(2,1)S(1)}, u32[]{:S(2)}, u32[]{:S(2)}) collective-permute-start(bf16[64,1280]{1,0:T(8,128)(2,1)S(1)} %get-tuple-element.44), channel_id=1, source_target_pairs={{0,128},{128,0},{1,129},{129,1},{2,130},{130,2},{3,131},{131,3},{4... | collective-permute-start | bytes 491528 | tf_op jit(solution)/shard_map/ppermute | solution.py:277
  161.5 8.8 %all-to-all-done.6.got = bf16[16,2,1280]{2,1,0:T(2,128)(2,1)S(1)} async-done(((bf16[16,2,1280]{2,1,0:T(2,128)(2,1)}), bf16[16,2,1280]{2,1,0:T(2,128)(2,1)S(1)}, u32[]{:S(2)}, u32[]{:S(2)}) %all-to-all-start.6) | async-done | bytes 81952 | tf_op jit(solution)/shard_map/all_to_all | solution.py:281
  170.2 0.8 shard_map.93
  171.0 5.8 %all-to-all-start.7 = ((bf16[32,2,1280]{2,1,0:T(2,128)(2,1)}), bf16[32,2,1280]{2,1,0:T(2,128)(2,1)S(1)}, u32[]{:S(2)}, u32[]{:S(2)}) async-start(bf16[32,2,1280]{2,1,0:T(2,128)(2,1)} %shard_map.93), calls=%async_computation.7 | async-start | bytes 327680 | tf_op jit(solution)/shard_map/all_to_all | solution.py:281
  176.8 0.8 maximum_select_fusion
  177.6 7.1 %all-to-all-done.7 = bf16[32,2,1280]{2,1,0:T(2,128)(2,1)S(1)} async-done(((bf16[32,2,1280]{2,1,0:T(2,128)(2,1)}), bf16[32,2,1280]{2,1,0:T(2,128)(2,1)S(1)}, u32[]{:S(2)}, u32[]{:S(2)}) %all-to-all-start.7) | async-done | bytes 163872 | tf_op jit(solution)/shard_map/all_to_all | solution.py:281
  184.7 0.8 reshape.27
  (45 shorter events, 0.1 us)
Async XLA Ops:
  0.6 13.1 %collective-permute-start = (bf16[2,64,1280]{2,1,0:T(8,128)(2,1)}, bf16[2,64,1280]{2,1,0:T(8,128)(2,1)S(1)}, u32[]{:S(2)}, u32[]{:S(2)}) collective-permute-start(bf16[2,64,1280]{2,1,0:T(8,128)(2,1)} %tok_a.1), channel_id=1, source_target_pairs={{0,128},{128,0},{1,129},{129,1},{2,130},{130,2},{3,131},{131,3},{4... | collective-permute-start | bytes 983048 | tf_op jit(solution)/shard_map/ppermute | solution.py:277
  9.4 4.3 %collective-permute-start.1 = (bf16[2,64,1280]{2,1,0:T(8,128)(2,1)}, bf16[2,64,1280]{2,1,0:T(8,128)(2,1)S(1)}, u32[]{:S(2)}, u32[]{:S(2)}) collective-permute-start(bf16[2,64,1280]{2,1,0:T(8,128)(2,1)} %grad_a.1), channel_id=1, source_target_pairs={{0,128},{128,0},{1,129},{129,1},{2,130},{130,2},{3,131},{131,3},{4... | collective-permute-start | bytes 983048 | tf_op jit(solution)/shard_map/ppermute | solution.py:277
  13.8 1.7 copy-start.10
  13.8 1.6 copy-start.12
  13.8 5.9 %copy-start = (bf16[1,320,1280]{2,1,0:T(8,128)(2,1)S(1)}, bf16[1,320,1280]{2,1,0:T(8,128)(2,1)}, u32[]{:S(2)}) copy-start(bf16[1,320,1280]{2,1,0:T(8,128)(2,1)} %param.7) | copy-start | bytes 2457604
  13.8 13.9 %copy-start.1 = (bf16[1,320,1280]{2,1,0:T(8,128)(2,1)S(1)}, bf16[1,320,1280]{2,1,0:T(8,128)(2,1)}, u32[]{:S(2)}) copy-start(bf16[1,320,1280]{2,1,0:T(8,128)(2,1)} %param.8) | copy-start | bytes 2457604
  15.4 16.5 %all-to-all-start = ((bf16[16,2,8,1408]{3,2,1,0:T(8,128)(2,1)}), bf16[16,2,8,1408]{3,2,1,0:T(8,128)(2,1)}, u32[]{:S(2)}, u32[]{:S(2)}) async-start(bf16[16,2,8,1408]{3,2,1,0:T(8,128)(2,1)} %shard_map.84.refs_2_), calls=%async_computation | async-start | bytes 1441792 | tf_op jit(solution)/shard_map/all_to_all | solution.py:288
  19.7 9.9 %collective-permute-start.2 = (bf16[320,1280]{1,0:T(8,128)(2,1)S(1)}, bf16[320,1280]{1,0:T(8,128)(2,1)S(1)}, u32[]{:S(2)}, u32[]{:S(2)}) collective-permute-start(bf16[320,1280]{1,0:T(8,128)(2,1)S(1)} %bitcast.14), channel_id=1, source_target_pairs={{0,128},{128,0},{1,129},{129,1},{2,130},{130,2},{3,131},{131,3},{4... | collective-permute-start | bytes 2457608 | tf_op jit(solution)/shard_map/ppermute | solution.py:277
  27.7 4.2 %collective-permute-start.3 = (bf16[320,1280]{1,0:T(8,128)(2,1)S(1)}, bf16[320,1280]{1,0:T(8,128)(2,1)S(1)}, u32[]{:S(2)}, u32[]{:S(2)}) collective-permute-start(bf16[320,1280]{1,0:T(8,128)(2,1)S(1)} %bitcast.18), channel_id=1, source_target_pairs={{0,128},{128,0},{1,129},{129,1},{2,130},{130,2},{3,131},{131,3},{4... | collective-permute-start | bytes 2457608 | tf_op jit(solution)/shard_map/ppermute | solution.py:277
  68.7 0.9 copy-start.2
  69.6 17.8 %copy-start.18 = (bf16[2,320,128]{2,1,0:T(8,128)(2,1)}, bf16[2,320,128]{2,1,0:T(8,128)(2,1)S(1)}, u32[]{:S(2)}) copy-start(bf16[2,320,128]{2,1,0:T(8,128)(2,1)S(1)} %get-tuple-element.35.pre_3) | copy-start | bytes 491524
  69.6 19.7 %copy-start.20 = (bf16[2,320,128]{2,1,0:T(8,128)(2,1)}, bf16[2,320,128]{2,1,0:T(8,128)(2,1)S(1)}, u32[]{:S(2)}) copy-start(bf16[2,320,128]{2,1,0:T(8,128)(2,1)S(1)} %get-tuple-element.36.hid_3) | copy-start | bytes 491524
  87.4 1.9 %copy-start.4 = (bf16[16,2,8,1280]{3,2,1,0:T(8,128)(2,1)}, bf16[16,2,8,1280]{3,2,1,0:T(8,128)(2,1)S(1)}, u32[]{:S(2)}) copy-start(bf16[16,2,8,1280]{3,2,1,0:T(8,128)(2,1)S(1)} %all_to_all.41.got.rows_4) | copy-start | bytes 1966084
  89.3 13.1 %copy-start.24 = (bf16[2,320,128]{2,1,0:T(8,128)(2,1)}, bf16[2,320,128]{2,1,0:T(8,128)(2,1)S(1)}, u32[]{:S(2)}) copy-start(bf16[2,320,128]{2,1,0:T(8,128)(2,1)S(1)} %get-tuple-element.38.hid_4) | copy-start | bytes 491524
  89.3 14.7 %copy-start.22 = (bf16[2,320,128]{2,1,0:T(8,128)(2,1)}, bf16[2,320,128]{2,1,0:T(8,128)(2,1)S(1)}, u32[]{:S(2)}) copy-start(bf16[2,320,128]{2,1,0:T(8,128)(2,1)S(1)} %get-tuple-element.37.pre_4) | copy-start | bytes 491524
  89.3 13.1 %copy-start.8 = (bf16[2,64,1280]{2,1,0:T(8,128)(2,1)S(1)}, bf16[2,64,1280]{2,1,0:T(8,128)(2,1)}, u32[]{:S(2)}) copy-start(bf16[2,64,1280]{2,1,0:T(8,128)(2,1)} %grad_a.1) | copy-start | bytes 983044
  89.4 13.1 %copy-start.9 = (bf16[2,64,1280]{2,1,0:T(8,128)(2,1)S(1)}, bf16[2,64,1280]{2,1,0:T(8,128)(2,1)}, u32[]{:S(2)}) copy-start(bf16[2,64,1280]{2,1,0:T(8,128)(2,1)} %tok_a.1) | copy-start | bytes 983044
  89.4 13.1 %copy-start.11 = (bf16[2,64,1280]{2,1,0:T(8,128)(2,1)S(1)}, bf16[2,64,1280]{2,1,0:T(8,128)(2,1)}, u32[]{:S(2)}) copy-start(bf16[2,64,1280]{2,1,0:T(8,128)(2,1)} %copy-done.10) | copy-start | bytes 983044
  89.4 13.1 %copy-start.13 = (bf16[2,64,1280]{2,1,0:T(8,128)(2,1)S(1)}, bf16[2,64,1280]{2,1,0:T(8,128)(2,1)}, u32[]{:S(2)}) copy-start(bf16[2,64,1280]{2,1,0:T(8,128)(2,1)} %copy-done.12) | copy-start | bytes 983044
  102.4 10.1 %copy-start.3 = (bf16[16,2,8,1408]{3,2,1,0:T(8,128)(2,1)S(1)}, bf16[16,2,8,1408]{3,2,1,0:T(8,128)(2,1)}, u32[]{:S(2)}) copy-start(bf16[16,2,8,1408]{3,2,1,0:T(8,128)(2,1)} %copy-done.2) | copy-start | bytes 2162692
  102.4 10.1 %copy-start.5 = (bf16[16,2,8,1280]{3,2,1,0:T(8,128)(2,1)S(1)}, bf16[16,2,8,1280]{3,2,1,0:T(8,128)(2,1)}, u32[]{:S(2)}) copy-start(bf16[16,2,8,1280]{3,2,1,0:T(8,128)(2,1)} %copy-done.4) | copy-start | bytes 1966084
  102.5 10.1 %copy-start.19 = (bf16[2,320,128]{2,1,0:T(8,128)(2,1)S(1)}, bf16[2,320,128]{2,1,0:T(8,128)(2,1)}, u32[]{:S(2)}) copy-start(bf16[2,320,128]{2,1,0:T(8,128)(2,1)} %copy-done.18) | copy-start | bytes 491524
  102.5 10.1 %copy-start.21 = (bf16[2,320,128]{2,1,0:T(8,128)(2,1)S(1)}, bf16[2,320,128]{2,1,0:T(8,128)(2,1)}, u32[]{:S(2)}) copy-start(bf16[2,320,128]{2,1,0:T(8,128)(2,1)} %copy-done.20) | copy-start | bytes 491524
  102.5 10.1 %copy-start.25 = (bf16[2,320,128]{2,1,0:T(8,128)(2,1)S(1)}, bf16[2,320,128]{2,1,0:T(8,128)(2,1)}, u32[]{:S(2)}) copy-start(bf16[2,320,128]{2,1,0:T(8,128)(2,1)} %copy-done.24) | copy-start | bytes 491524
  104.0 0.7 copy-start.14
  104.8 0.7 copy-start.16
  105.5 29.5 %all-to-all-start.4 = ((bf16[16,2,8,1408]{3,2,1,0:T(8,128)(2,1)}), bf16[16,2,8,1408]{3,2,1,0:T(8,128)(2,1)}, u32[]{:S(2)}, u32[]{:S(2)}) async-start(bf16[16,2,8,1408]{3,2,1,0:T(8,128)(2,1)} %get-tuple-element.34), calls=%async_computation.4 | async-start | bytes 1441792 | tf_op jit(solution)/shard_map/all_to_all | solution.py:288
  112.6 0.9 copy-start.23
  114.5 20.0 %collective-permute-start.4 = (bf16[2,320,1280]{2,1,0:T(8,128)(2,1)S(1)}, bf16[2,320,1280]{2,1,0:T(8,128)(2,1)S(1)}, u32[]{:S(2)}, u32[]{:S(2)}) collective-permute-start(bf16[2,320,1280]{2,1,0:T(8,128)(2,1)S(1)} %get-tuple-element.40), channel_id=1, source_target_pairs={{0,128},{128,0},{1,129},{129,1},{2,130},{130,2},{3,131},{131,3},{4... | collective-permute-start | bytes 4915208 | tf_op jit(solution)/shard_map/ppermute | solution.py:277
  134.5 1.0 copy-start.15
  134.5 1.1 copy-start.17
  134.9 2.6 %copy-start.6 = (bf16[1,320,1280]{2,1,0:T(8,128)(2,1)}, bf16[1,320,1280]{2,1,0:T(8,128)(2,1)S(1)}, u32[]{:S(2)}) copy-start(bf16[1,320,1280]{2,1,0:T(8,128)(2,1)S(1)} %get-tuple-element.46.refs_7_) | copy-start | bytes 2457604
  134.9 2.6 %copy-start.7 = (bf16[1,320,1280]{2,1,0:T(8,128)(2,1)}, bf16[1,320,1280]{2,1,0:T(8,128)(2,1)S(1)}, u32[]{:S(2)}) copy-start(bf16[1,320,1280]{2,1,0:T(8,128)(2,1)S(1)} %get-tuple-element.47.refs_6_) | copy-start | bytes 2457604
  153.5 16.7 %all-to-all-start.6 = ((bf16[16,2,1280]{2,1,0:T(2,128)(2,1)}), bf16[16,2,1280]{2,1,0:T(2,128)(2,1)S(1)}, u32[]{:S(2)}, u32[]{:S(2)}) async-start(bf16[16,2,1280]{2,1,0:T(2,128)(2,1)} %shard_map.92), calls=%async_computation.6 | async-start | bytes 163840 | tf_op jit(solution)/shard_map/all_to_all | solution.py:281
  158.7 18.1 %collective-permute-start.5 = (bf16[64,1280]{1,0:T(8,128)(2,1)S(1)}, bf16[64,1280]{1,0:T(8,128)(2,1)S(1)}, u32[]{:S(2)}, u32[]{:S(2)}) collective-permute-start(bf16[64,1280]{1,0:T(8,128)(2,1)S(1)} %get-tuple-element.44), channel_id=1, source_target_pairs={{0,128},{128,0},{1,129},{129,1},{2,130},{130,2},{3,131},{131,3},{4... | collective-permute-start | bytes 491528 | tf_op jit(solution)/shard_map/ppermute | solution.py:277
  171.0 13.6 %all-to-all-start.7 = ((bf16[32,2,1280]{2,1,0:T(2,128)(2,1)}), bf16[32,2,1280]{2,1,0:T(2,128)(2,1)S(1)}, u32[]{:S(2)}, u32[]{:S(2)}) async-start(bf16[32,2,1280]{2,1,0:T(2,128)(2,1)} %shard_map.93), calls=%async_computation.7 | async-start | bytes 327680 | tf_op jit(solution)/shard_map/all_to_all | solution.py:281
